TPU v7x, 256 devices: a whole 4x4x8 slice. The times are simulated.
256 devices in a mesh: gx: 16 (over z, x_lo), gy: 16 (over x_hi, y, core).
Axes of the slice: x: 4 (x_hi: 2, x_lo: 2; x = x_hi * 2 + x_lo), y: 4, z: 8, core: 2. Of those that a mesh axis runs over, the one named last changes fastest.
Arguments:
- populations: float32 [27, 8, 128, 4096], P(None, None, 'gx', 'gy'), may hold values from 0 to 1, as said below
- bottom_in: float32 [9, 128, 4096], P(None, 'gx', 'gy'), may hold values from 0.01 to 0.06
- top_in: float32 [9, 128, 4096], P(None, 'gx', 'gy'), may hold values from 0.01 to 0.06
- turbine_mask: int32 [8, 128, 4096], P(None, 'gx', 'gy'), may hold values from 0 to 1, as said below
- rotor_index: int32 [8, 128, 4096], P(None, 'gx', 'gy'), may hold values from 0 to 63, as said below
Outputs:
- final_populations: float32 [27, 8, 128, 4096], P(None, None, 'gx', 'gy')
Inputs may be any that keep to these rules, and one draw needn't show every extreme that they name: `populations`: every population is positive, near a jet-shaped equilibrium. Cells with turbine_mask 1 form actuator disks: the cells of one disk lie in two streamwise-neighbouring cells and within 2 cells of the disk's hub, spanwise and vertically. All cells of one disk carry one rotor_index and different disks carry different ones; some rotors have no cell with turbine_mask 1. Where turbine_mask is 0, rotor_index is arbitrary.
All inputs are finite; a program needn't handle non-finite values.
Results may differ from a plain program's by a relative error of at most 0.0001.
Values sent between devices are 32-bit elements; how exact they have to be, the bound alone decides.
No kernel may reach another device: no remote copies, remote signals or barrier semaphores. Data moves between devices by JAX's collectives and lax.ppermute only.
A program may use at most 64 MiB of HBM per device.

v0:
```python
import functools

import jax
import jax.numpy as jnp
from jax import lax
from jax.experimental import pallas as pl
from jax.experimental.pallas import tpu as pltpu
from jax.sharding import PartitionSpec as P

ROTORS = 64
SOUND = 1.0 / 3.0
TAU_BASE = 0.52
SMAG_GAIN = 5.0
CORIOLIS = 0.05
GEO_U = 0.08
THRUST_GAIN = 4.0
EMPTY = 127
LEVELS = 8
VMEM_LIMIT = 48 * 1024 * 1024

RHO, VX, VY, VZ, DXX, DYY, DZZ, DXY, DXZ, DYZ = range(10)
X_FIELDS = (RHO, VX, VY, VZ, DXX, DXY, DXZ)
Y_FIELDS = (RHO, VX, VY, VZ, DYY, DXY, DYZ)


def iota(axis):
    return lax.broadcasted_iota(jnp.int32, (8, 128), axis)


def roll(block, shift, axis):
    size = block.shape[axis]
    return pltpu.roll(block, shift % size, axis) if shift % size else block


def low_moments(f):
    along_z = {}
    for a in range(3):
        for b in range(3):
            low, mid, high = f(a, b, 0), f(a, b, 1), f(a, b, 2)
            ends = low + high
            along_z[a, b] = (ends + mid, high - low, ends)
    slabs = []
    for a in range(3):
        (l0, l1, l2), (m0, m1, m2), (h0, h1, h2) = (along_z[a, b] for b in range(3))
        ends = l0 + h0
        slabs.append((ends + m0, h0 - l0, ends, l1 + m1 + h1, h1 - l1, l2 + m2 + h2))
    low, mid, high = slabs
    ends = low[0] + high[0]
    return {
        "0": ends + mid[0],
        "x": high[0] - low[0],
        "xx": ends,
        "y": low[1] + mid[1] + high[1],
        "xy": high[1] - low[1],
        "yy": low[2] + mid[2] + high[2],
        "z": low[3] + mid[3] + high[3],
        "xz": high[3] - low[3],
        "yz": low[4] + mid[4] + high[4],
        "zz": low[5] + mid[5] + high[5],
    }


def relax(m):
    rho = m["0"]
    inverse = 1.0 / rho
    ux, uy, uz = m["x"] * inverse, m["y"] * inverse, m["z"] * inverse
    third = rho * SOUND
    qxx = m["xx"] - (m["x"] * ux + third)
    qyy = m["yy"] - (m["y"] * uy + third)
    qzz = m["zz"] - (m["z"] * uz + third)
    qxy = m["xy"] - m["x"] * uy
    qxz = m["xz"] - m["x"] * uz
    qyz = m["yz"] - m["y"] * uz
    strain = qxx * qxx + qyy * qyy + qzz * qzz + 2.0 * (qxy * qxy + qxz * qxz + qyz * qyz)
    keep = 1.0 - 1.0 / (TAU_BASE + SMAG_GAIN * jnp.sqrt(strain))
    vx = ux + CORIOLIS * uy
    vy = uy - CORIOLIS * (ux - GEO_U)
    fields = [rho, vx, vy, uz] + [keep * q for q in (qxx, qyy, qzz, qxy, qxz, qyz)]
    return ux, fields


def shapes(speed):
    square = speed * speed + SOUND
    return (0.5 * (square - speed), 1.0 - square, 0.5 * (square + speed))


def spread(values):
    lanes = iota(1)
    stride = 1
    while len(values) > 1:
        first = (lanes & stride) == 0
        values = [
            jnp.where(first, a, b) + roll(jnp.where(first, b, a), stride, 1)
            for a, b in zip(values[0::2], values[1::2])
        ]
        stride *= 2
    total = values[0]
    while stride < 128:
        total = total + roll(total, stride, 1)
        stride *= 2
    for shift in (4, 2, 1):
        total = total + roll(total, shift, 0)
    return total


def rotor_sums(labels, speeds, with_counts):
    sums, counts = [], []
    for rotor in range(ROTORS):
        total = jnp.zeros((8, 128), jnp.float32)
        count = jnp.zeros((8, 128), jnp.float32)
        for label, speed in zip(labels, speeds):
            hit = label == rotor
            total = total + jnp.where(hit, speed, 0.0)
            if with_counts:
                count = count + jnp.where(hit, 1.0, 0.0)
        sums.append(total)
        counts.append(count)
    if with_counts:
        return spread(sums + counts)
    return jnp.where(iota(1) < ROTORS, spread(sums), 0.0)


def collide(f, label, state, to_right, to_left, edges, with_labels):
    lanes = iota(1)
    rows = iota(0)
    labels, speeds = [], []
    right_edge = jnp.zeros((8, 128), jnp.float32)
    left_edge = jnp.zeros((8, 128), jnp.float32)
    for z in range(LEVELS):
        halves = []
        for j in range(2):
            ux, fields = relax(low_moments(functools.partial(f, z, j)))
            for index, value in enumerate(fields):
                state[index, j, 8 * z : 8 * z + 8, :] = value
            mark = label(z, j)
            labels.append(mark)
            speeds.append(ux)
            halves.append([fields[index] for index in Y_FIELDS] + [mark.astype(jnp.float32)])
        for index in range(8):
            both = jnp.where(lanes == 0, halves[0][index], halves[1][index])
            place = 16 * index + 2 * z
            moved = roll(both, place + 1, 1)
            right_edge = jnp.where(lanes == place, moved, right_edge)
            left_edge = jnp.where(lanes == place + 1, moved, left_edge)
    edges[0] = right_edge
    edges[1] = left_edge
    for target, row in ((to_right, 7), (to_left, 0)):
        slot = 0
        for index in X_FIELDS:
            for j in range(2):
                target[slot] = state[index, j, pl.ds(row, 8, stride=8), :]
                slot += 1
    sums = rotor_sums(labels, speeds, with_labels)
    for target, row in ((to_right, 7), (to_left, 0)):
        last = target.shape[0] - 1
        upper = jnp.broadcast_to(right_edge[row : row + 1], (8, 128))
        lower = jnp.broadcast_to(left_edge[row : row + 1], (8, 128))
        target[last] = jnp.where(rows == 0, upper, jnp.where(rows == 1, lower, sums))
    edges[2] = sums


def first_kernel(f_ref, mask_ref, rotor_ref, state, labels, to_right, to_left, edges):
    def f(z, j, a, b, c):
        return f_ref[9 * a + 3 * b + c, z, :, 128 * j : 128 * j + 128]

    def label(z, j):
        here = (z, slice(None), slice(128 * j, 128 * j + 128))
        mark = jnp.where(mask_ref[here] != 0, rotor_ref[here], EMPTY)
        labels[j, 8 * z : 8 * z + 8, :] = mark
        return mark

    collide(f, label, state, to_right, to_left, edges, True)
    for target, row in ((to_right, 7), (to_left, 0)):
        for j in range(2):
            target[2 * len(X_FIELDS) + j] = labels[j, pl.ds(row, 8, stride=8), :].astype(jnp.float32)


def relay_kernel(edges, left, right, to_up, to_down):
    rows = iota(0)
    last = left.shape[0] - 1
    a, b = left[last], right[last]
    sums = edges[2] + a[2:3] + b[2:3]
    to_up[0] = edges[0]
    to_up[1] = jnp.where(rows == 0, a[0:1], jnp.where(rows == 7, b[0:1], sums))
    to_down[0] = edges[1]
    to_down[1] = jnp.where(rows == 0, a[1:2], jnp.where(rows == 7, b[1:2], sums))


def look_up(table, label):
    return jnp.take_along_axis(table, label, axis=1, mode="promise_in_bounds")


def stream(table, state, labels, left, right, left_marks, right_marks, below, above, bottom, top, out, ghost):
    lanes = iota(1)
    rows = iota(0)
    for side, (source, marks) in enumerate(((left, left_marks), (right, right_marks))):
        a = 2 - 2 * side
        sign = 1.0 - 2.0 * side
        for j in range(2):
            rho, vx, vy, vz, dxx, dxy, dxz = (source[2 * n + j] for n in range(7))
            vx = vx - look_up(table, marks(j))
            part = rho * shapes(vx)[a]
            along_y, along_z = shapes(vy), shapes(vz)
            for b in range(3):
                column = part * along_y[b]
                for c in range(3):
                    value = column * along_z[c]
                    if b == 1 and c == 1:
                        value = value + 0.5 * dxx
                    elif c == 1:
                        value = value + (0.25 * sign * (b - 1)) * dxy
                    elif b == 1:
                        value = value + (0.25 * sign * (c - 1)) * dxz
                    ghost[side, 3 * b + c, j] = value

    even = (lanes & 1) == 0
    sign = jnp.where(even, 0.25, -0.25)

    def column_slots(block, wanted):
        rho, vx, vy, vz, dyy, dxy, dyz, mark = (roll(block, -16 * n, 1) for n in range(8))
        vx = vx - look_up(table, jnp.clip(mark, 0.0, float(EMPTY)).astype(jnp.int32))
        along_x, along_y, along_z = shapes(vx), shapes(vy), shapes(vz)
        part = rho * jnp.where(even, along_y[2], along_y[0])
        slots = {}
        for a in wanted:
            piece = part * along_x[a]
            for c in range(3):
                value = piece * along_z[c]
                if a == 1 and c == 1:
                    value = value + 0.5 * dyy
                elif c == 1:
                    value = value + ((a - 1) * sign) * dxy
                elif a == 1:
                    value = value + ((c - 1) * sign) * dyz
                slots[a, c] = value
        return slots

    def merged(n):
        return jnp.where(even, below[n], roll(above[n], -2, 1))

    columns = column_slots(merged(0), (0, 1, 2))
    corners = column_slots(merged(1), (0, 2))
    for c in range(3):
        columns[2, c] = jnp.where(rows == 0, corners[2, c], roll(columns[2, c], 1, 0))
        columns[0, c] = jnp.where(rows == 7, corners[0, c], roll(columns[0, c], -1, 0))

    for z in range(LEVELS):
        tiles = []
        for j in range(2):
            fields = [state[index, j, 8 * z : 8 * z + 8, :] for index in range(10)]
            thrust = look_up(table, labels[j, 8 * z : 8 * z + 8, :])
            parts = [fields[RHO] * h for h in shapes(fields[VX] - thrust)]
            tiles.append((fields, parts, shapes(fields[VY]), shapes(fields[VZ])))
        for c in range(3):
            level = z + c - 1
            if level < 0 or level >= LEVELS:
                continue
            for a in range(3):
                inflow = roll(columns[a, c], -2 * z, 1)
                for b in range(3):
                    values = []
                    for j, (d, parts, along_y, along_z) in enumerate(tiles):
                        value = parts[a] * along_y[b] * along_z[c]
                        ones = (a == 1) + (b == 1) + (c == 1)
                        if ones == 3:
                            value = value - (d[DXX] + d[DYY] + d[DZZ])
                        elif ones == 2:
                            value = value + 0.5 * (d[DXX] if a != 1 else d[DYY] if b != 1 else d[DZZ])
                        elif ones == 1 and c == 1:
                            value = value + (0.25 * (a - 1) * (b - 1)) * d[DXY]
                        elif ones == 1 and b == 1:
                            value = value + (0.25 * (a - 1) * (c - 1)) * d[DXZ]
                        elif ones == 1:
                            value = value + (0.25 * (b - 1) * (c - 1)) * d[DYZ]
                        if a == 2:
                            value = jnp.where(rows == 0, ghost[0, 3 * b + c, j, z : z + 1, :], roll(value, 1, 0))
                        elif a == 0:
                            value = jnp.where(rows == 7, ghost[1, 3 * b + c, j, z : z + 1, :], roll(value, -1, 0))
                        values.append(value)
                    first, second = values
                    if b == 2:
                        first, second = roll(first, 1, 1), roll(second, 1, 1)
                        second = jnp.where(lanes == 0, first, second)
                        first = jnp.where(lanes == 0, inflow, first)
                    elif b == 0:
                        first, second = roll(first, -1, 1), roll(second, -1, 1)
                        first = jnp.where(lanes == 127, second, first)
                        second = jnp.where(lanes == 127, inflow, second)
                    out[9 * a + 3 * b + c, level, :, 0:128] = first
                    out[9 * a + 3 * b + c, level, :, 128:256] = second
    for a in range(3):
        for b in range(3):
            out[9 * a + 3 * b + 2, 0] = bottom[3 * a + b]
            out[9 * a + 3 * b, LEVELS - 1] = top[3 * a + b]


def disk_table(sums, counts):
    disk = sums / jnp.maximum(counts, 1.0)
    return jnp.where(iota(1) < ROTORS, THRUST_GAIN * disk * jnp.abs(disk), 0.0)


def all_sums(edges, left, right, below, above):
    last = left.shape[0] - 1
    return edges[2] + left[last][2:3] + right[last][2:3] + below[1][2:3] + above[1][2:3]


def marks_of(message):
    return lambda j: message[2 * len(X_FIELDS) + j].astype(jnp.int32)


def middle_kernel(
    state, labels, edges, left, right, below, above, bottom, top,
    new_state, to_right, to_left, new_edges, counts, f_ref, ghost,
):
    totals = all_sums(edges, left, right, below, above)
    seen = roll(totals, 64, 1)
    counts[...] = seen
    table = disk_table(totals, seen)
    stream(table, state, labels, left, right, marks_of(left), marks_of(right), below, above, bottom, top, f_ref, ghost)

    def f(z, j, a, b, c):
        return f_ref[9 * a + 3 * b + c, z, :, 128 * j : 128 * j + 128]

    def label(z, j):
        return labels[j, 8 * z : 8 * z + 8, :]

    collide(f, label, new_state, to_right, to_left, new_edges, False)


def last_kernel(
    state, labels, edges, left, right, old_left, old_right, below, above, bottom, top, counts, out, ghost
):
    totals = all_sums(edges, left, right, below, above)
    table = disk_table(totals, counts[...])
    stream(table, state, labels, left, right, marks_of(old_left), marks_of(old_right), below, above, bottom, top, out, ghost)


def call(kernel, inputs, outputs, scratch=()):
    whole = pl.BlockSpec(memory_space=pltpu.VMEM)
    return pl.pallas_call(
        kernel,
        out_shape=[jax.ShapeDtypeStruct(shape, dtype) for shape, dtype in outputs],
        in_specs=[whole] * len(inputs),
        out_specs=[whole] * len(outputs),
        scratch_shapes=[pltpu.VMEM(shape, jnp.float32) for shape in scratch],
        compiler_params=pltpu.CompilerParams(vmem_limit_bytes=VMEM_LIMIT),
    )(*inputs)


def both_ways(upward, downward, axis):
    count = lax.axis_size(axis)
    return (
        lax.ppermute(upward, axis, [(i, (i + 1) % count) for i in range(count)]),
        lax.ppermute(downward, axis, [((i + 1) % count, i) for i in range(count)]),
    )


def body(populations, bottom_in, top_in, turbine_mask, rotor_index):
    f32 = jnp.float32
    state_shape = ((10, 2, 64, 128), f32)
    edge_shape = ((3, 8, 128), f32)
    y_shape = ((2, 8, 128), f32)
    ghost = (2, 9, 2, 8, 128)
    n = 2 * len(X_FIELDS)
    x_first, x_later = ((n + 3, 8, 128), f32), ((n + 1, 8, 128), f32)

    state, labels, to_right, to_left, edges = call(
        first_kernel,
        (populations, turbine_mask, rotor_index),
        (state_shape, ((2, 64, 128), jnp.int32), x_first, x_first, edge_shape),
    )
    left, right = both_ways(to_right, to_left, "gx")
    to_up, to_down = call(relay_kernel, (edges, left, right), (y_shape, y_shape))
    below, above = both_ways(to_up, to_down, "gy")

    state, to_right, to_left, edges, counts = call(
        middle_kernel,
        (state, labels, edges, left, right, below, above, bottom_in, top_in),
        (state_shape, x_later, x_later, edge_shape, ((8, 128), f32)),
        (populations.shape, ghost),
    )
    old_left, old_right = left, right
    left, right = both_ways(to_right, to_left, "gx")
    to_up, to_down = call(relay_kernel, (edges, left, right), (y_shape, y_shape))
    below, above = both_ways(to_up, to_down, "gy")

    (out,) = call(
        last_kernel,
        (state, labels, edges, left, right, old_left, old_right, below, above, bottom_in, top_in, counts),
        ((populations.shape, f32),),
        (ghost,),
    )
    return out


def solution(mesh):
    placed = (
        P(None, None, "gx", "gy"),
        P(None, "gx", "gy"),
        P(None, "gx", "gy"),
        P(None, "gx", "gy"),
        P(None, "gx", "gy"),
    )
    return jax.shard_map(
        body, mesh=mesh, in_specs=placed, out_specs=P(None, None, "gx", "gy"), check_vma=False
    )
```

profile of v0, /device:TPU:123, one launch (start us, length us, event | category | flops | bytes accessed | tf_op | source)
XLA Modules:
  0.0 40.6 jit_solution(14939745725345365931)
XLA Ops:
  0.0 0.0 copy-start
  0.0 1.5 %copy-done = f32[27,8,8,256]{3,2,1,0:T(8,128)S(1)} copy-done((f32[27,8,8,256]{3,2,1,0:T(8,128)S(1)}, f32[27,8,8,256]{3,2,1,0:T(8,128)}, u32[]{:S(2)}) %copy-start) | copy-done | bytes 1769496
  1.5 0.0 copy-start.3
  1.5 0.8 %copy-done.3 = s32[8,8,256]{2,1,0:T(8,128)S(1)} copy-done((s32[8,8,256]{2,1,0:T(8,128)S(1)}, s32[8,8,256]{2,1,0:T(8,128)}, u32[]{:S(2)}) %copy-start.3) | copy-done | bytes 65560
  2.3 0.0 copy-start.4
  2.3 0.8 %copy-done.4 = s32[8,8,256]{2,1,0:T(8,128)S(1)} copy-done((s32[8,8,256]{2,1,0:T(8,128)S(1)}, s32[8,8,256]{2,1,0:T(8,128)}, u32[]{:S(2)}) %copy-start.4) | copy-done | bytes 65560
  3.2 0.0 copy-start.1
  3.2 0.0 copy-start.2
  3.2 1.5 %shard_map.55 = (f32[10,2,64,128]{3,2,1,0:T(8,128)S(1)}, s32[2,64,128]{2,1,0:T(8,128)S(1)}, f32[17,8,128]{2,1,0:T(8,128)S(1)}, f32[17,8,128]{2,1,0:T(8,128)S(1)}, f32[3,8,128]{2,1,0:T(8,128)S(1)}) custom-call(f32[27,8,8,256]{3,2,1,0:T(8,128)S(1)} %copy-done, s32[8,8,256]{2,1,0:T(8,128)S(1)} %copy-done.3, s32[8,8,256]{2,1,0:T(8,128)S(1)} %copy-done.4), custom_call_target="tpu_custom_call" | custom-call | tf_op jit(solution)/shard_map/pallas_call | solution.py:340
  4.7 2.9 %collective-permute-start = (f32[17,8,128]{2,1,0:T(8,128)S(1)}, f32[17,8,128]{2,1,0:T(8,128)S(1)}, u32[]{:S(2)}, u32[]{:S(2)}) collective-permute-start(f32[17,8,128]{2,1,0:T(8,128)S(1)} %get-tuple-element.22), channel_id=1, source_target_pairs={{0,16},{16,32},{32,48},{48,64},{64,80},{80,96},{96,112},{112,128},... | collective-permute-start | bytes 208904 | tf_op jit(solution)/shard_map/ppermute | solution.py:353
  7.5 0.0 collective-permute-start.1
  7.5 1.4 %collective-permute-done.left.old_left = f32[17,8,128]{2,1,0:T(8,128)S(1)} collective-permute-done((f32[17,8,128]{2,1,0:T(8,128)S(1)}, f32[17,8,128]{2,1,0:T(8,128)S(1)}, u32[]{:S(2)}, u32[]{:S(2)}) %collective-permute-start) | collective-permute-done | bytes 69664 | tf_op jit(solution)/shard_map/ppermute | solution.py:353
  8.9 3.9 %collective-permute-done.1.right.old_right = f32[17,8,128]{2,1,0:T(8,128)S(1)} collective-permute-done((f32[17,8,128]{2,1,0:T(8,128)S(1)}, f32[17,8,128]{2,1,0:T(8,128)S(1)}, u32[]{:S(2)}, u32[]{:S(2)}) %collective-permute-start.1) | collective-permute-done | bytes 69664 | tf_op jit(solution)/shard_map/ppermute | solution.py:354
  12.8 3.8 %collective-permute-start.2 = (f32[2,8,128]{2,1,0:T(8,128)S(1)}, f32[2,8,128]{2,1,0:T(8,128)S(1)}, u32[]{:S(2)}, u32[]{:S(2)}) collective-permute-start(f32[2,8,128]{2,1,0:T(8,128)S(1)} %get-tuple-element.24), channel_id=1, source_target_pairs={{0,1},{1,2},{2,3},{3,4},{4,5},{5,6},{6,7},{7,8},{8,9},{9,10},{10,1... | collective-permute-start | bytes 24584 | tf_op jit(solution)/shard_map/ppermute | solution.py:353
  16.6 0.0 collective-permute-start.3
  16.6 0.8 %collective-permute-done.2.below = f32[2,8,128]{2,1,0:T(8,128)S(1)} collective-permute-done((f32[2,8,128]{2,1,0:T(8,128)S(1)}, f32[2,8,128]{2,1,0:T(8,128)S(1)}, u32[]{:S(2)}, u32[]{:S(2)}) %collective-permute-start.2) | collective-permute-done | bytes 8224 | tf_op jit(solution)/shard_map/ppermute | solution.py:353
  17.4 5.9 %collective-permute-done.3.above = f32[2,8,128]{2,1,0:T(8,128)S(1)} collective-permute-done((f32[2,8,128]{2,1,0:T(8,128)S(1)}, f32[2,8,128]{2,1,0:T(8,128)S(1)}, u32[]{:S(2)}, u32[]{:S(2)}) %collective-permute-start.3) | collective-permute-done | bytes 8224 | tf_op jit(solution)/shard_map/ppermute | solution.py:354
  23.3 0.0 copy-done.1
  23.3 0.0 copy-done.2
  23.3 1.6 %shard_map.57 = (f32[10,2,64,128]{3,2,1,0:T(8,128)S(1)}, f32[15,8,128]{2,1,0:T(8,128)S(1)}, f32[15,8,128]{2,1,0:T(8,128)S(1)}, f32[3,8,128]{2,1,0:T(8,128)S(1)}, f32[8,128]{1,0:T(8,128)S(1)}) custom-call(f32[10,2,64,128]{3,2,1,0:T(8,128)S(1)} %get-tuple-element.19.state, s32[2,64,128]{2,1,0:T(8,128)S(1)} %get-tuple-element.20.labels, ...), custom_call_target="tpu_custom_call" | custom-call | tf_op jit(solution)/shard_map/pallas_call | solution.py:340
  25.0 0.8 %collective-permute-start.4 = (f32[15,8,128]{2,1,0:T(8,128)S(1)}, f32[15,8,128]{2,1,0:T(8,128)S(1)}, u32[]{:S(2)}, u32[]{:S(2)}) collective-permute-start(f32[15,8,128]{2,1,0:T(8,128)S(1)} %get-tuple-element.28), channel_id=1, source_target_pairs={{0,16},{16,32},{32,48},{48,64},{64,80},{80,96},{96,112},{112,128},... | collective-permute-start | bytes 184328 | tf_op jit(solution)/shard_map/ppermute | solution.py:353
  25.7 0.8 %collective-permute-start.5 = (f32[15,8,128]{2,1,0:T(8,128)S(1)}, f32[15,8,128]{2,1,0:T(8,128)S(1)}, u32[]{:S(2)}, u32[]{:S(2)}) collective-permute-start(f32[15,8,128]{2,1,0:T(8,128)S(1)} %get-tuple-element.29), channel_id=1, source_target_pairs={{16,0},{32,16},{48,32},{64,48},{80,64},{96,80},{112,96},{128,112},... | collective-permute-start | bytes 184328 | tf_op jit(solution)/shard_map/ppermute | solution.py:354
  26.5 1.6 %collective-permute-done.4.left = f32[15,8,128]{2,1,0:T(8,128)S(1)} collective-permute-done((f32[15,8,128]{2,1,0:T(8,128)S(1)}, f32[15,8,128]{2,1,0:T(8,128)S(1)}, u32[]{:S(2)}, u32[]{:S(2)}) %collective-permute-start.4) | collective-permute-done | bytes 61472 | tf_op jit(solution)/shard_map/ppermute | solution.py:353
  28.1 2.8 %collective-permute-done.5.right = f32[15,8,128]{2,1,0:T(8,128)S(1)} collective-permute-done((f32[15,8,128]{2,1,0:T(8,128)S(1)}, f32[15,8,128]{2,1,0:T(8,128)S(1)}, u32[]{:S(2)}, u32[]{:S(2)}) %collective-permute-start.5) | collective-permute-done | bytes 61472 | tf_op jit(solution)/shard_map/ppermute | solution.py:354
  30.9 0.9 %collective-permute-start.6 = (f32[2,8,128]{2,1,0:T(8,128)S(1)}, f32[2,8,128]{2,1,0:T(8,128)S(1)}, u32[]{:S(2)}, u32[]{:S(2)}) collective-permute-start(f32[2,8,128]{2,1,0:T(8,128)S(1)} %get-tuple-element.30), channel_id=1, source_target_pairs={{0,1},{1,2},{2,3},{3,4},{4,5},{5,6},{6,7},{7,8},{8,9},{9,10},{10,1... | collective-permute-start | bytes 24584 | tf_op jit(solution)/shard_map/ppermute | solution.py:353
  31.8 0.0 collective-permute-start.7
  31.8 0.8 %collective-permute-done.6.below = f32[2,8,128]{2,1,0:T(8,128)S(1)} collective-permute-done((f32[2,8,128]{2,1,0:T(8,128)S(1)}, f32[2,8,128]{2,1,0:T(8,128)S(1)}, u32[]{:S(2)}, u32[]{:S(2)}) %collective-permute-start.6) | collective-permute-done | bytes 8224 | tf_op jit(solution)/shard_map/ppermute | solution.py:353
  32.6 5.9 %collective-permute-done.7.above = f32[2,8,128]{2,1,0:T(8,128)S(1)} collective-permute-done((f32[2,8,128]{2,1,0:T(8,128)S(1)}, f32[2,8,128]{2,1,0:T(8,128)S(1)}, u32[]{:S(2)}, u32[]{:S(2)}) %collective-permute-start.7) | collective-permute-done | bytes 8224 | tf_op jit(solution)/shard_map/ppermute | solution.py:354
  38.5 2.1 %shard_map.59 = f32[27,8,8,256]{3,2,1,0:T(8,128)} custom-call(f32[10,2,64,128]{3,2,1,0:T(8,128)S(1)} %get-tuple-element.26.state, s32[2,64,128]{2,1,0:T(8,128)S(1)} %get-tuple-element.20.labels, f32[3,8,128]{2,1,0:T(8,128)S(1)} %get-tuple-element.27.edges, f32[15,8,128]{2,1,0:T(8,128)S(1)} %collective-permute-done.4.left, ...), custom_call_target="tpu_custom_call" | custom-call | tf_op jit(solution)/shard_map/pallas_call | solution.py:340
  (2 shorter events, 0.0 us)
Async XLA Ops:
  0.0 1.5 %copy-start = (f32[27,8,8,256]{3,2,1,0:T(8,128)S(1)}, f32[27,8,8,256]{3,2,1,0:T(8,128)}, u32[]{:S(2)}) copy-start(f32[27,8,8,256]{3,2,1,0:T(8,128)} %f_ref.1) | copy-start | bytes 5308420
  1.5 0.8 %copy-start.3 = (s32[8,8,256]{2,1,0:T(8,128)S(1)}, s32[8,8,256]{2,1,0:T(8,128)}, u32[]{:S(2)}) copy-start(s32[8,8,256]{2,1,0:T(8,128)} %mask_ref.1) | copy-start | bytes 196612
  2.3 0.8 %copy-start.4 = (s32[8,8,256]{2,1,0:T(8,128)S(1)}, s32[8,8,256]{2,1,0:T(8,128)}, u32[]{:S(2)}) copy-start(s32[8,8,256]{2,1,0:T(8,128)} %rotor_ref.1) | copy-start | bytes 196612
  3.2 20.1 %copy-start.1 = (f32[9,8,256]{2,1,0:T(8,128)S(1)}, f32[9,8,256]{2,1,0:T(8,128)}, u32[]{:S(2)}) copy-start(f32[9,8,256]{2,1,0:T(8,128)} %bottom.3) | copy-start | bytes 221188
  3.2 20.1 %copy-start.2 = (f32[9,8,256]{2,1,0:T(8,128)S(1)}, f32[9,8,256]{2,1,0:T(8,128)}, u32[]{:S(2)}) copy-start(f32[9,8,256]{2,1,0:T(8,128)} %top.3) | copy-start | bytes 221188
  4.7 4.2 %collective-permute-start = (f32[17,8,128]{2,1,0:T(8,128)S(1)}, f32[17,8,128]{2,1,0:T(8,128)S(1)}, u32[]{:S(2)}, u32[]{:S(2)}) collective-permute-start(f32[17,8,128]{2,1,0:T(8,128)S(1)} %get-tuple-element.22), channel_id=1, source_target_pairs={{0,16},{16,32},{32,48},{48,64},{64,80},{80,96},{96,112},{112,128},... | collective-permute-start | bytes 208904 | tf_op jit(solution)/shard_map/ppermute | solution.py:353
  7.5 5.3 %collective-permute-start.1 = (f32[17,8,128]{2,1,0:T(8,128)S(1)}, f32[17,8,128]{2,1,0:T(8,128)S(1)}, u32[]{:S(2)}, u32[]{:S(2)}) collective-permute-start(f32[17,8,128]{2,1,0:T(8,128)S(1)} %get-tuple-element.23), channel_id=1, source_target_pairs={{16,0},{32,16},{48,32},{64,48},{80,64},{96,80},{112,96},{128,112},... | collective-permute-start | bytes 208904 | tf_op jit(solution)/shard_map/ppermute | solution.py:354
  12.8 4.6 %collective-permute-start.2 = (f32[2,8,128]{2,1,0:T(8,128)S(1)}, f32[2,8,128]{2,1,0:T(8,128)S(1)}, u32[]{:S(2)}, u32[]{:S(2)}) collective-permute-start(f32[2,8,128]{2,1,0:T(8,128)S(1)} %get-tuple-element.24), channel_id=1, source_target_pairs={{0,1},{1,2},{2,3},{3,4},{4,5},{5,6},{6,7},{7,8},{8,9},{9,10},{10,1... | collective-permute-start | bytes 24584 | tf_op jit(solution)/shard_map/ppermute | solution.py:353
  16.6 6.7 %collective-permute-start.3 = (f32[2,8,128]{2,1,0:T(8,128)S(1)}, f32[2,8,128]{2,1,0:T(8,128)S(1)}, u32[]{:S(2)}, u32[]{:S(2)}) collective-permute-start(f32[2,8,128]{2,1,0:T(8,128)S(1)} %get-tuple-element.25), channel_id=1, source_target_pairs={{1,0},{2,1},{3,2},{4,3},{5,4},{6,5},{7,6},{8,7},{9,8},{10,9},{11,1... | collective-permute-start | bytes 24584 | tf_op jit(solution)/shard_map/ppermute | solution.py:354
  25.0 3.1 %collective-permute-start.4 = (f32[15,8,128]{2,1,0:T(8,128)S(1)}, f32[15,8,128]{2,1,0:T(8,128)S(1)}, u32[]{:S(2)}, u32[]{:S(2)}) collective-permute-start(f32[15,8,128]{2,1,0:T(8,128)S(1)} %get-tuple-element.28), channel_id=1, source_target_pairs={{0,16},{16,32},{32,48},{48,64},{64,80},{80,96},{96,112},{112,128},... | collective-permute-start | bytes 184328 | tf_op jit(solution)/shard_map/ppermute | solution.py:353
  25.7 5.2 %collective-permute-start.5 = (f32[15,8,128]{2,1,0:T(8,128)S(1)}, f32[15,8,128]{2,1,0:T(8,128)S(1)}, u32[]{:S(2)}, u32[]{:S(2)}) collective-permute-start(f32[15,8,128]{2,1,0:T(8,128)S(1)} %get-tuple-element.29), channel_id=1, source_target_pairs={{16,0},{32,16},{48,32},{64,48},{80,64},{96,80},{112,96},{128,112},... | collective-permute-start | bytes 184328 | tf_op jit(solution)/shard_map/ppermute | solution.py:354
  30.9 1.7 %collective-permute-start.6 = (f32[2,8,128]{2,1,0:T(8,128)S(1)}, f32[2,8,128]{2,1,0:T(8,128)S(1)}, u32[]{:S(2)}, u32[]{:S(2)}) collective-permute-start(f32[2,8,128]{2,1,0:T(8,128)S(1)} %get-tuple-element.30), channel_id=1, source_target_pairs={{0,1},{1,2},{2,3},{3,4},{4,5},{5,6},{6,7},{7,8},{8,9},{9,10},{10,1... | collective-permute-start | bytes 24584 | tf_op jit(solution)/shard_map/ppermute | solution.py:353
  31.8 6.7 %collective-permute-start.7 = (f32[2,8,128]{2,1,0:T(8,128)S(1)}, f32[2,8,128]{2,1,0:T(8,128)S(1)}, u32[]{:S(2)}, u32[]{:S(2)}) collective-permute-start(f32[2,8,128]{2,1,0:T(8,128)S(1)} %get-tuple-element.31), channel_id=1, source_target_pairs={{1,0},{2,1},{3,2},{4,3},{5,4},{6,5},{7,6},{8,7},{9,8},{10,9},{11,1... | collective-permute-start | bytes 24584 | tf_op jit(solution)/shard_map/ppermute | solution.py:354
where the time goes:
time: 40.8 us; the launch traced here: 40.6 us
  waiting for transfers between devices  23 us (56%)
  starting transfers between devices  9.07 us (22%)
  Pallas kernels  5.29 us (13%)
  local copies, waits for them, and re-layouts  3.16 us (8%)
    ppermute x4, waiting for transfers between devices, both_ways(): lax.ppermute(downward, axis, [((i + 1) % count, i) for i in range(count)])  18.5 us
    ppermute x4, starting transfers between devices, both_ways(): lax.ppermute(upward, axis, [(i, (i + 1) % count) for i in range(count)])  8.28 us
    pallas_call x5, Pallas kernels, call(): pl.pallas_call(kernel, out_shape=[jax.ShapeDtypeStruct(shape, dtype) for...  5.29 us
    ppermute x4, waiting for transfers between devices, both_ways(): lax.ppermute(upward, axis, [(i, (i + 1) % count) for i in range(count)])  4.55 us
    unnamed x10, local copies, waits for them, and re-layouts  3.16 us
  transfers between devices with their start and end apart: 8, of which 8 were waited for; matrix products, arithmetic and copies ran while one was open for 0% of the time, Pallas kernels for 0%

commit v1 on v0

v1 whole, which is shorter than its diff:
```python
import functools

import jax
import jax.numpy as jnp
from jax import lax
from jax.experimental import pallas as pl
from jax.experimental.pallas import tpu as pltpu
from jax.sharding import PartitionSpec as P

ROTORS = 64
SOUND = 1.0 / 3.0
TAU_BASE = 0.52
SMAG_GAIN = 5.0
CORIOLIS = 0.05
GEO_U = 0.08
THRUST_GAIN = 4.0
EMPTY = 127
LEVELS = 8
VMEM_LIMIT = 48 * 1024 * 1024

RHO, VX, VY, VZ, DXX, DYY, DZZ, DXY, DXZ, DYZ = range(10)
X_FIELDS = (RHO, VX, VY, VZ, DXX, DXY, DXZ)
Y_FIELDS = (RHO, VX, VY, VZ, DYY, DXY, DYZ)


def iota(axis):
    return lax.broadcasted_iota(jnp.int32, (8, 128), axis)


def roll(block, shift, axis):
    size = block.shape[axis]
    return pltpu.roll(block, shift % size, axis) if shift % size else block


def low_moments(f):
    along_z = {}
    for a in range(3):
        for b in range(3):
            low, mid, high = f(a, b, 0), f(a, b, 1), f(a, b, 2)
            ends = low + high
            along_z[a, b] = (ends + mid, high - low, ends)
    slabs = []
    for a in range(3):
        (l0, l1, l2), (m0, m1, m2), (h0, h1, h2) = (along_z[a, b] for b in range(3))
        ends = l0 + h0
        slabs.append((ends + m0, h0 - l0, ends, l1 + m1 + h1, h1 - l1, l2 + m2 + h2))
    low, mid, high = slabs
    ends = low[0] + high[0]
    return {
        "0": ends + mid[0],
        "x": high[0] - low[0],
        "xx": ends,
        "y": low[1] + mid[1] + high[1],
        "xy": high[1] - low[1],
        "yy": low[2] + mid[2] + high[2],
        "z": low[3] + mid[3] + high[3],
        "xz": high[3] - low[3],
        "yz": low[4] + mid[4] + high[4],
        "zz": low[5] + mid[5] + high[5],
    }


def relax(m):
    rho = m["0"]
    inverse = 1.0 / rho
    ux, uy, uz = m["x"] * inverse, m["y"] * inverse, m["z"] * inverse
    third = rho * SOUND
    qxx = m["xx"] - (m["x"] * ux + third)
    qyy = m["yy"] - (m["y"] * uy + third)
    qzz = m["zz"] - (m["z"] * uz + third)
    qxy = m["xy"] - m["x"] * uy
    qxz = m["xz"] - m["x"] * uz
    qyz = m["yz"] - m["y"] * uz
    strain = qxx * qxx + qyy * qyy + qzz * qzz + 2.0 * (qxy * qxy + qxz * qxz + qyz * qyz)
    keep = 1.0 - 1.0 / (TAU_BASE + SMAG_GAIN * jnp.sqrt(strain))
    vx = ux + CORIOLIS * uy
    vy = uy - CORIOLIS * (ux - GEO_U)
    fields = [rho, vx, vy, uz] + [keep * q for q in (qxx, qyy, qzz, qxy, qxz, qyz)]
    return ux, fields


def shapes(speed):
    square = speed * speed + SOUND
    return (0.5 * (square - speed), 1.0 - square, 0.5 * (square + speed))


def spread(values):
    lanes = iota(1)
    stride = 1
    while len(values) > 1:
        first = (lanes & stride) == 0
        values = [
            jnp.where(first, a, b) + roll(jnp.where(first, b, a), stride, 1)
            for a, b in zip(values[0::2], values[1::2])
        ]
        stride *= 2
    total = values[0]
    while stride < 128:
        total = total + roll(total, stride, 1)
        stride *= 2
    for shift in (4, 2, 1):
        total = total + roll(total, shift, 0)
    return total


def rotor_sums(labels, speeds, with_counts):
    sums, counts = [], []
    for rotor in range(ROTORS):
        total = jnp.zeros((8, 128), jnp.float32)
        count = jnp.zeros((8, 128), jnp.float32)
        for label, speed in zip(labels, speeds):
            hit = label == rotor
            total = total + jnp.where(hit, speed, 0.0)
            if with_counts:
                count = count + jnp.where(hit, 1.0, 0.0)
        sums.append(total)
        counts.append(count)
    if with_counts:
        return spread(sums + counts)
    return jnp.where(iota(1) < ROTORS, spread(sums), 0.0)


def collide(f, label, state, marks=(), speeds=(), first=False):
    marks, speeds = list(marks), list(speeds)
    for z in range(LEVELS):
        for j in range(2):
            ux, fields = relax(low_moments(functools.partial(f, z, j)))
            for index, value in enumerate(fields):
                state[index, j, 8 * z : 8 * z + 8, :] = value
            marks.append(label(z, j))
            speeds.append(ux)
    return rotor_sums(marks, speeds, first)


def first_kernel(f_ref, mask_ref, rotor_ref, bottom, top, state, labels, edges, to_up, to_down):
    lanes = iota(1)

    def f(z, j, a, b, c):
        return f_ref[9 * a + 3 * b + c, z, :, 128 * j : 128 * j + 128]

    def label(z, j):
        here = (z, slice(None), slice(128 * j, 128 * j + 128))
        mark = jnp.where(mask_ref[here] != 0, rotor_ref[here], EMPTY)
        labels[j, 8 * z : 8 * z + 8, :] = mark
        return mark

    sums = collide(f, label, state, first=True)

    def edge(read):
        block = jnp.zeros((8, 128), jnp.float32)
        for z in range(LEVELS):
            both = jnp.where(lanes < 64, read(z, 0), read(z, 1))
            block = jnp.where(lanes // 16 == z, roll(both, 16 * z + 8, 1), block)
        return block

    blocks = [edge(lambda z, j, n=n: state[n, j, 8 * z : 8 * z + 8, :]) for n in range(10)]
    blocks.append(edge(lambda z, j: labels[j, 8 * z : 8 * z + 8, :].astype(jnp.float32)))
    for n, block in enumerate(blocks):
        edges[n] = block
    edges[11] = sums
    low = (lanes & 8) == 0
    for n in range(6):
        one = blocks[2 * n]
        other = blocks[2 * n + 1] if n < 5 else one
        to_up[n] = jnp.where(low, one, roll(other, 8, 1))
        to_down[n] = jnp.where(low, roll(other, -8, 1), one)
    to_up[6] = sums
    to_down[6] = sums
    for place, source in ((7, bottom), (8, top)):
        upward = jnp.zeros((8, 128), jnp.float32)
        downward = upward
        for n in range(9):
            both = jnp.where(lanes < 64, source[n, :, 0:128], source[n, :, 128:256])
            moved = roll(both, 8 * n + 8, 1)
            upward = jnp.where(lanes // 8 == n, moved, upward)
            downward = jnp.where(lanes // 8 == n + 1, moved, downward)
        to_up[place] = upward
        to_down[place] = downward


def rows_of(blocks, row):
    rows = iota(0)
    out = jnp.broadcast_to(blocks[0][row : row + 1], (8, 128))
    for n in range(1, len(blocks)):
        out = jnp.where(rows == n, jnp.broadcast_to(blocks[n][row : row + 1], (8, 128)), out)
    return out


def edge_rows(state, target, row):
    slot = 0
    for index in X_FIELDS:
        for j in range(2):
            target[slot] = state[index, j, pl.ds(row, 8, stride=8), :]
            slot += 1
    return slot


def relay_kernel(state, labels, edges, below, above, domains, to_right, to_left, column_sums):
    low = (iota(1) & 8) == 0
    sums = edges[11] + below[6] + above[6]
    column_sums[...] = sums
    for n in range(11):
        under, over = below[n // 2], above[n // 2]
        if n % 2:
            under, over = roll(under, -8, 1), roll(over, 8, 1)
        domains[0, n] = jnp.where(low, under, edges[n])
        domains[1, n] = jnp.where(low, edges[n], over)
    for target, row in ((to_right, 7), (to_left, 0)):
        slot = edge_rows(state, target, row)
        for j in range(2):
            target[slot + j] = labels[j, pl.ds(row, 8, stride=8), :].astype(jnp.float32)
        for side in range(2):
            target[slot + 2 + side] = rows_of([domains[side, n] for n in X_FIELDS + (10,)], row)
        target[slot + 4] = sums


def look_up(table, label):
    return jnp.take_along_axis(table, label, axis=1, mode="promise_in_bounds")


def index_of(mark):
    return jnp.clip(mark, 0.0, float(EMPTY)).astype(jnp.int32)


def slot_value(d, parts, along_y, along_z, a, b, c):
    value = parts[a] * along_y[b] * along_z[c]
    ones = (a == 1) + (b == 1) + (c == 1)
    if ones == 3:
        return value - (d[DXX] + d[DYY] + d[DZZ])
    if ones == 2:
        return value + 0.5 * (d[DXX] if a != 1 else d[DYY] if b != 1 else d[DZZ])
    if ones == 1 and c == 1:
        return value + (0.25 * (a - 1) * (b - 1)) * d[DXY]
    if ones == 1 and b == 1:
        return value + (0.25 * (a - 1) * (c - 1)) * d[DXZ]
    if ones == 1:
        return value + (0.25 * (b - 1) * (c - 1)) * d[DYZ]
    return value


def entering(table, fields, mark, a):
    rho, vx, vy, vz, dxx, dxy, dxz = fields
    part = rho * shapes(vx - look_up(table, mark))[a]
    d = {DXX: dxx, DXY: dxy, DXZ: dxz}
    along_y, along_z = shapes(vy), shapes(vz)
    return {(b, c): slot_value(d, {a: part}, along_y, along_z, a, b, c) for b in range(3) for c in range(3)}


def shift_rows(value, a, before, after):
    if a == 2:
        return jnp.where(iota(0) == 0, before, roll(value, 1, 0))
    if a == 0:
        return jnp.where(iota(0) == 7, after, roll(value, -1, 0))
    return value


def row_blocks(block, count):
    return [jnp.broadcast_to(block[n : n + 1], (8, 128)) for n in range(count)]


def step_domain(table, side, domains, left, right, below, above):
    lanes = iota(1)
    d = [domains[side, n] for n in range(10)]
    thrust = look_up(table, index_of(domains[side, 10]))
    parts = [d[RHO] * h for h in shapes(d[VX] - thrust)]
    along_y, along_z = shapes(d[VY]), shapes(d[VZ])
    n = 2 * len(X_FIELDS) + 2 + side
    beside = {}
    for a, message in ((2, left), (0, right)):
        fields = row_blocks(message[n], 8)
        beside[a] = entering(table, fields[:7], index_of(fields[7]), a)
    into, new = {}, {}
    for a in range(3):
        for b in range(3):
            for c in range(3):
                value = slot_value(d, parts, along_y, along_z, a, b, c)
                value = shift_rows(value, a, beside[2][b, c], beside[0][b, c])
                value = roll(value, b - 1, 1)
                if b == 2 - 2 * side:
                    into[a, c] = value
                slot = 3 * a + b
                message = above if side else below
                if c == 2:
                    value = jnp.where(lanes < 16, roll(message[7], -8 * slot, 1), roll(value, 16, 1))
                elif c == 0:
                    value = jnp.where(lanes >= 112, roll(message[8], 112 - 8 * slot, 1), roll(value, -16, 1))
                new[a, b, c] = value
    return into, new


def last_columns(table, strip, left, right):
    even = (iota(1) & 1) == 0
    sign = jnp.where(even, 0.25, -0.25)

    def slots_of(fields, wanted):
        rho, vx, vy, vz, dyy, dxy, dyz, mark = fields
        along_x, along_y, along_z = shapes(vx - look_up(table, index_of(mark))), shapes(vy), shapes(vz)
        part = rho * jnp.where(even, along_y[2], along_y[0])
        slots = {}
        for a in wanted:
            piece = part * along_x[a]
            for c in range(3):
                value = piece * along_z[c]
                if a == 1 and c == 1:
                    value = value + 0.5 * dyy
                elif c == 1:
                    value = value + ((a - 1) * sign) * dxy
                elif a == 1:
                    value = value + ((c - 1) * sign) * dyz
                slots[a, c] = value
        return slots

    n = 2 * len(X_FIELDS)
    columns = slots_of([strip[k] for k in range(8)], (0, 1, 2))
    before = slots_of(row_blocks(left[n], 8), (2,))
    after = slots_of(row_blocks(right[n], 8), (0,))
    for c in range(3):
        columns[2, c] = shift_rows(columns[2, c], 2, before[2, c], None)
        columns[0, c] = shift_rows(columns[0, c], 0, None, after[0, c])
    return columns


def stream(table, state, labels, columns, left, right, left_marks, right_marks, bottom, top, out, ghost):
    lanes = iota(1)
    for side, (source, marks) in enumerate(((left, left_marks), (right, right_marks))):
        a = 2 - 2 * side
        for j in range(2):
            fields = [source[2 * n + j] for n in range(len(X_FIELDS))]
            for (b, c), value in entering(table, fields, marks(j), a).items():
                ghost[side, 3 * b + c, j] = value

    for z in range(LEVELS):
        tiles = []
        for j in range(2):
            fields = [state[index, j, 8 * z : 8 * z + 8, :] for index in range(10)]
            thrust = look_up(table, labels[j, 8 * z : 8 * z + 8, :])
            parts = [fields[RHO] * h for h in shapes(fields[VX] - thrust)]
            tiles.append((fields, parts, shapes(fields[VY]), shapes(fields[VZ])))
        for c in range(3):
            level = z + c - 1
            if level < 0 or level >= LEVELS:
                continue
            for a in range(3):
                inflow = roll(columns[a, c], -16 * z - 8, 1)
                for b in range(3):
                    first, second = (
                        shift_rows(
                            slot_value(*tile, a, b, c),
                            a,
                            ghost[0, 3 * b + c, j, z : z + 1, :],
                            ghost[1, 3 * b + c, j, z : z + 1, :],
                        )
                        for j, tile in enumerate(tiles)
                    )
                    if b == 2:
                        first, second = roll(first, 1, 1), roll(second, 1, 1)
                        second = jnp.where(lanes == 0, first, second)
                        first = jnp.where(lanes == 0, inflow, first)
                    elif b == 0:
                        first, second = roll(first, -1, 1), roll(second, -1, 1)
                        first = jnp.where(lanes == 127, second, first)
                        second = jnp.where(lanes == 127, inflow, second)
                    out[9 * a + 3 * b + c, level, :, 0:128] = first
                    out[9 * a + 3 * b + c, level, :, 128:256] = second
    for a in range(3):
        for b in range(3):
            out[9 * a + 3 * b + 2, 0] = bottom[3 * a + b]
            out[9 * a + 3 * b, LEVELS - 1] = top[3 * a + b]


def disk_table(sums, counts):
    disk = sums / jnp.maximum(counts, 1.0)
    return jnp.where(iota(1) < ROTORS, THRUST_GAIN * disk * jnp.abs(disk), 0.0)


def marks_of(message):
    return lambda j: message[2 * len(X_FIELDS) + j].astype(jnp.int32)


def middle_kernel(
    state, labels, domains, column_sums, left, right, below, above, bottom, top,
    new_state, to_right, to_left, strip, counts, sums_out, f_ref, ghost,
):
    lanes = iota(1)
    even = (lanes & 1) == 0
    last = 2 * len(X_FIELDS) + 4
    totals = column_sums[...] + left[last] + right[last]
    seen = roll(totals, 64, 1)
    counts[...] = seen
    table = disk_table(totals, seen)

    marks, speeds, kept, columns = [], [], [], [{}, {}]
    for side in range(2):
        columns[side], new = step_domain(table, side, domains, left, right, below, above)
        ux, fields = relax(low_moments(lambda a, b, c: new[a, b, c]))
        column = lanes & 15
        near = jnp.logical_and(column >= 8, column < 13) if side else jnp.logical_and(column >= 3, column < 8)
        mark = domains[side, 10]
        marks.append(jnp.where(near, index_of(mark), EMPTY))
        speeds.append(ux)
        kept.append([fields[n] for n in Y_FIELDS] + [mark])
    strips = [jnp.where(even, roll(one, 1, 1), roll(other, -1, 1)) for one, other in zip(*kept)]
    for n, block in enumerate(strips):
        strip[n] = block
    merged = {key: jnp.where(even, columns[0][key], columns[1][key]) for key in columns[0]}
    stream(table, state, labels, merged, left, right, marks_of(left), marks_of(right), bottom, top, f_ref, ghost)

    def f(z, j, a, b, c):
        return f_ref[9 * a + 3 * b + c, z, :, 128 * j : 128 * j + 128]

    def label(z, j):
        return labels[j, 8 * z : 8 * z + 8, :]

    sums = collide(f, label, new_state, marks, speeds)
    sums_out[...] = sums
    for target, row in ((to_right, 7), (to_left, 0)):
        slot = edge_rows(new_state, target, row)
        target[slot] = rows_of(strips, row)
        target[slot + 1] = sums


def last_kernel(
    state, labels, strip, sums, counts, left, right, old_left, old_right, bottom, top, out, ghost
):
    last = 2 * len(X_FIELDS) + 1
    totals = sums[...] + left[last] + right[last]
    table = disk_table(totals, counts[...])
    columns = last_columns(table, strip, left, right)
    stream(table, state, labels, columns, left, right, marks_of(old_left), marks_of(old_right), bottom, top, out, ghost)


def call(kernel, inputs, outputs, scratch=()):
    whole = pl.BlockSpec(memory_space=pltpu.VMEM)
    return pl.pallas_call(
        kernel,
        out_shape=[jax.ShapeDtypeStruct(shape, dtype) for shape, dtype in outputs],
        in_specs=[whole] * len(inputs),
        out_specs=[whole] * len(outputs),
        scratch_shapes=[pltpu.VMEM(shape, jnp.float32) for shape in scratch],
        compiler_params=pltpu.CompilerParams(vmem_limit_bytes=VMEM_LIMIT),
    )(*inputs)


def both_ways(upward, downward, axis):
    count = lax.axis_size(axis)
    return (
        lax.ppermute(upward, axis, [(i, (i + 1) % count) for i in range(count)]),
        lax.ppermute(downward, axis, [((i + 1) % count, i) for i in range(count)]),
    )


def body(populations, bottom_in, top_in, turbine_mask, rotor_index):
    f32 = jnp.float32
    state_shape = ((10, 2, 64, 128), f32)
    one = ((8, 128), f32)
    ghost = (2, 9, 2, 8, 128)
    n = 2 * len(X_FIELDS)

    def blocks(*count):
        return (count + (8, 128), f32)

    state, labels, edges, to_up, to_down = call(
        first_kernel,
        (populations, turbine_mask, rotor_index, bottom_in, top_in),
        (state_shape, ((2, 64, 128), jnp.int32), blocks(12), blocks(9), blocks(9)),
    )
    below, above = both_ways(to_up, to_down, "gy")
    domains, to_right, to_left, column_sums = call(
        relay_kernel,
        (state, labels, edges, below, above),
        (blocks(2, 11), blocks(n + 5), blocks(n + 5), one),
    )
    old_left, old_right = both_ways(to_right, to_left, "gx")
    state, to_right, to_left, strip, counts, sums = call(
        middle_kernel,
        (state, labels, domains, column_sums, old_left, old_right, below, above, bottom_in, top_in),
        (state_shape, blocks(n + 2), blocks(n + 2), blocks(8), one, one),
        (populations.shape, ghost),
    )
    left, right = both_ways(to_right, to_left, "gx")
    (out,) = call(
        last_kernel,
        (state, labels, strip, sums, counts, left, right, old_left, old_right, bottom_in, top_in),
        ((populations.shape, f32),),
        (ghost,),
    )
    return out


def solution(mesh):
    placed = (
        P(None, None, "gx", "gy"),
        P(None, "gx", "gy"),
        P(None, "gx", "gy"),
        P(None, "gx", "gy"),
        P(None, "gx", "gy"),
    )
    return jax.shard_map(
        body, mesh=mesh, in_specs=placed, out_specs=P(None, None, "gx", "gy"), check_vma=False
    )
```

time: 40.8 us -> 34.6 us (0.85)
  waiting for transfers between devices: 23 us -> 16.2 us
  local copies, waits for them, and re-layouts: 3.16 us -> 4.93 us
  starting transfers between devices: 9.07 us -> 7.41 us
  Pallas kernels: 5.29 us -> 5.77 us
    ppermute x4 -> x3, waiting for transfers between devices: 18.5 us -> 12 us  [both_ways(): lax.ppermute(downward, axis, [((i + 1) % count, i) for i in range(count)])]
    ppermute x4 -> x3, starting transfers between devices: 8.28 us -> 5.95 us  [both_ways(): lax.ppermute(upward, axis, [(i, (i + 1) % count) for i in range(count)])]
    unnamed x10 -> x14, local copies, waits for them, and re-layouts: 3.16 us -> 4.93 us
    ppermute x4 -> x3, starting transfers between devices: 0.79 us -> 1.46 us  [both_ways(): lax.ppermute(downward, axis, [((i + 1) % count, i) for i in range(count)])]
    pallas_call x5 -> x4, Pallas kernels: 5.29 us -> 5.77 us  [call(): pl.pallas_call(kernel, out_shape=[jax.ShapeDtypeStruct(shape, dtype) for...]
    ppermute x4 -> x3, waiting for transfers between devices: 4.55 us -> 4.15 us  [both_ways(): lax.ppermute(upward, axis, [(i, (i + 1) % count) for i in range(count)])]
  transfers between devices with their start and end apart: 8 -> 6, of which waited for: 8 -> 6; matrix products, arithmetic and copies ran while one was open for 0% -> 0% of each run, Pallas kernels for 0% -> 0%
where the time goes in v1:
time: 34.6 us; the launch traced here: 34.3 us
  waiting for transfers between devices  16.2 us (47%)
  starting transfers between devices  7.41 us (21%)
  Pallas kernels  5.77 us (17%)
  local copies, waits for them, and re-layouts  4.93 us (14%)
    ppermute x3, waiting for transfers between devices, both_ways(): lax.ppermute(downward, axis, [((i + 1) % count, i) for i in range(count)])  12 us
    ppermute x3, starting transfers between devices, both_ways(): lax.ppermute(upward, axis, [(i, (i + 1) % count) for i in range(count)])  5.95 us
    pallas_call x4, Pallas kernels, call(): pl.pallas_call(kernel, out_shape=[jax.ShapeDtypeStruct(shape, dtype) for...  5.77 us
    unnamed x14, local copies, waits for them, and re-layouts  4.93 us
    ppermute x3, waiting for transfers between devices, both_ways(): lax.ppermute(upward, axis, [(i, (i + 1) % count) for i in range(count)])  4.15 us
    ppermute x3, starting transfers between devices, both_ways(): lax.ppermute(downward, axis, [((i + 1) % count, i) for i in range(count)])  1.46 us
  transfers between devices with their start and end apart: 6, of which 6 were waited for; matrix products, arithmetic and copies ran while one was open for 0% of the time, Pallas kernels for 0%

profile of v1, /device:TPU:123, one launch (start us, length us, event | category | flops | bytes accessed | tf_op | source)
XLA Modules:
  0.0 34.3 jit_solution(9519902571689020669)
XLA Ops:
  0.0 0.0 copy-start
  0.0 1.5 %copy-done = f32[27,8,8,256]{3,2,1,0:T(8,128)S(1)} copy-done((f32[27,8,8,256]{3,2,1,0:T(8,128)S(1)}, f32[27,8,8,256]{3,2,1,0:T(8,128)}, u32[]{:S(2)}) %copy-start) | copy-done | bytes 1769496
  1.5 0.0 copy-start.1
  1.5 0.9 %copy-done.1 = f32[9,8,256]{2,1,0:T(8,128)S(1)} copy-done((f32[9,8,256]{2,1,0:T(8,128)S(1)}, f32[9,8,256]{2,1,0:T(8,128)}, u32[]{:S(2)}) %copy-start.1) | copy-done | bytes 73752
  2.4 0.0 copy-start.3
  2.4 0.9 %copy-done.3 = f32[9,8,256]{2,1,0:T(8,128)S(1)} copy-done((f32[9,8,256]{2,1,0:T(8,128)S(1)}, f32[9,8,256]{2,1,0:T(8,128)}, u32[]{:S(2)}) %copy-start.3) | copy-done | bytes 73752
  3.2 0.0 copy-start.5
  3.2 0.8 %copy-done.5 = s32[8,8,256]{2,1,0:T(8,128)S(1)} copy-done((s32[8,8,256]{2,1,0:T(8,128)S(1)}, s32[8,8,256]{2,1,0:T(8,128)}, u32[]{:S(2)}) %copy-start.5) | copy-done | bytes 65560
  4.1 0.0 copy-start.6
  4.1 0.8 %copy-done.6 = s32[8,8,256]{2,1,0:T(8,128)S(1)} copy-done((s32[8,8,256]{2,1,0:T(8,128)S(1)}, s32[8,8,256]{2,1,0:T(8,128)}, u32[]{:S(2)}) %copy-start.6) | copy-done | bytes 65560
  4.9 0.0 copy-start.2
  4.9 0.0 copy-start.4
  4.9 1.6 %shard_map.55 = (f32[10,2,64,128]{3,2,1,0:T(8,128)S(1)}, s32[2,64,128]{2,1,0:T(8,128)S(1)}, f32[12,8,128]{2,1,0:T(8,128)S(1)}, f32[9,8,128]{2,1,0:T(8,128)S(1)}, f32[9,8,128]{2,1,0:T(8,128)S(1)}) custom-call(f32[27,8,8,256]{3,2,1,0:T(8,128)S(1)} %copy-done, s32[8,8,256]{2,1,0:T(8,128)S(1)} %copy-done.5, s32[8,8,256]{2,1,0:T(8,128)S(1)} %copy-done.6, ...), custom_call_target="tpu_custom_call" | custom-call | tf_op jit(solution)/shard_map/pallas_call | solution.py:434
  6.5 2.1 %collective-permute-start = (f32[9,8,128]{2,1,0:T(8,128)S(1)}, f32[9,8,128]{2,1,0:T(8,128)S(1)}, u32[]{:S(2)}, u32[]{:S(2)}) collective-permute-start(f32[9,8,128]{2,1,0:T(8,128)S(1)} %get-tuple-element.23), channel_id=1, source_target_pairs={{0,1},{1,2},{2,3},{3,4},{4,5},{5,6},{6,7},{7,8},{8,9},{9,10},{10,1... | collective-permute-start | bytes 110600 | tf_op jit(solution)/shard_map/ppermute | solution.py:447
  8.6 0.0 collective-permute-start.1
  8.6 1.1 %collective-permute-done.below = f32[9,8,128]{2,1,0:T(8,128)S(1)} collective-permute-done((f32[9,8,128]{2,1,0:T(8,128)S(1)}, f32[9,8,128]{2,1,0:T(8,128)S(1)}, u32[]{:S(2)}, u32[]{:S(2)}) %collective-permute-start) | collective-permute-done | bytes 36896 | tf_op jit(solution)/shard_map/ppermute | solution.py:447
  9.7 5.9 %collective-permute-done.1.above = f32[9,8,128]{2,1,0:T(8,128)S(1)} collective-permute-done((f32[9,8,128]{2,1,0:T(8,128)S(1)}, f32[9,8,128]{2,1,0:T(8,128)S(1)}, u32[]{:S(2)}, u32[]{:S(2)}) %collective-permute-start.1) | collective-permute-done | bytes 36896 | tf_op jit(solution)/shard_map/ppermute | solution.py:448
  15.6 0.1 shard_map.56
  15.7 3.8 %collective-permute-start.2 = (f32[19,8,128]{2,1,0:T(8,128)S(1)}, f32[19,8,128]{2,1,0:T(8,128)S(1)}, u32[]{:S(2)}, u32[]{:S(2)}) collective-permute-start(f32[19,8,128]{2,1,0:T(8,128)S(1)} %get-tuple-element.27), channel_id=1, source_target_pairs={{0,16},{16,32},{32,48},{48,64},{64,80},{80,96},{96,112},{112,128},... | collective-permute-start | bytes 233480 | tf_op jit(solution)/shard_map/ppermute | solution.py:447
  19.5 0.0 collective-permute-start.3
  19.5 1.4 %collective-permute-done.2.left.old_left = f32[19,8,128]{2,1,0:T(8,128)S(1)} collective-permute-done((f32[19,8,128]{2,1,0:T(8,128)S(1)}, f32[19,8,128]{2,1,0:T(8,128)S(1)}, u32[]{:S(2)}, u32[]{:S(2)}) %collective-permute-start.2) | collective-permute-done | bytes 77856 | tf_op jit(solution)/shard_map/ppermute | solution.py:447
  21.0 3.9 %collective-permute-done.3.right.old_right = f32[19,8,128]{2,1,0:T(8,128)S(1)} collective-permute-done((f32[19,8,128]{2,1,0:T(8,128)S(1)}, f32[19,8,128]{2,1,0:T(8,128)S(1)}, u32[]{:S(2)}, u32[]{:S(2)}) %collective-permute-start.3) | collective-permute-done | bytes 77856 | tf_op jit(solution)/shard_map/ppermute | solution.py:448
  24.9 0.0 copy-done.2
  24.9 0.0 copy-done.4
  24.9 1.9 %shard_map.57 = (f32[10,2,64,128]{3,2,1,0:T(8,128)S(1)}, f32[16,8,128]{2,1,0:T(8,128)S(1)}, f32[16,8,128]{2,1,0:T(8,128)S(1)}, f32[8,8,128]{2,1,0:T(8,128)S(1)},...) custom-call(f32[10,2,64,128]{3,2,1,0:T(8,128)S(1)} %get-tuple-element.20.state, s32[2,64,128]{2,1,0:T(8,128)S(1)} %get-tuple-element.21.labels, ...), custom_call_target="tpu_custom_call" | custom-call | tf_op jit(solution)/shard_map/pallas_call | solution.py:434
  26.8 0.0 collective-permute-start.4
  26.8 1.5 %collective-permute-start.5 = (f32[16,8,128]{2,1,0:T(8,128)S(1)}, f32[16,8,128]{2,1,0:T(8,128)S(1)}, u32[]{:S(2)}, u32[]{:S(2)}) collective-permute-start(f32[16,8,128]{2,1,0:T(8,128)S(1)} %get-tuple-element.34), channel_id=1, source_target_pairs={{16,0},{32,16},{48,32},{64,48},{80,64},{96,80},{112,96},{128,112},... | collective-permute-start | bytes 196616 | tf_op jit(solution)/shard_map/ppermute | solution.py:448
  28.3 1.6 %collective-permute-done.4.left = f32[16,8,128]{2,1,0:T(8,128)S(1)} collective-permute-done((f32[16,8,128]{2,1,0:T(8,128)S(1)}, f32[16,8,128]{2,1,0:T(8,128)S(1)}, u32[]{:S(2)}, u32[]{:S(2)}) %collective-permute-start.4) | collective-permute-done | bytes 65568 | tf_op jit(solution)/shard_map/ppermute | solution.py:447
  29.9 2.2 %collective-permute-done.5.right = f32[16,8,128]{2,1,0:T(8,128)S(1)} collective-permute-done((f32[16,8,128]{2,1,0:T(8,128)S(1)}, f32[16,8,128]{2,1,0:T(8,128)S(1)}, u32[]{:S(2)}, u32[]{:S(2)}) %collective-permute-start.5) | collective-permute-done | bytes 65568 | tf_op jit(solution)/shard_map/ppermute | solution.py:448
  32.1 2.2 %shard_map.58 = f32[27,8,8,256]{3,2,1,0:T(8,128)} custom-call(f32[10,2,64,128]{3,2,1,0:T(8,128)S(1)} %get-tuple-element.29.state, s32[2,64,128]{2,1,0:T(8,128)S(1)} %get-tuple-element.21.labels, f32[8,8,128]{2,1,0:T(8,128)S(1)} %get-tuple-element.30.strip, f32[8,128]{1,0:T(8,128)S(1)} %get-tuple-element.31.sums, f32[8,128]{1,0:T(8,128)S(1)} %get-tuple-element.32.counts, ...), custom_call_target="tpu_custom_call" | custom-call | tf_op jit(solution)/shard_map/pallas_call | solution.py:434
Async XLA Ops:
  0.0 1.5 %copy-start = (f32[27,8,8,256]{3,2,1,0:T(8,128)S(1)}, f32[27,8,8,256]{3,2,1,0:T(8,128)}, u32[]{:S(2)}) copy-start(f32[27,8,8,256]{3,2,1,0:T(8,128)} %f_ref.1) | copy-start | bytes 5308420
  1.5 0.9 %copy-start.1 = (f32[9,8,256]{2,1,0:T(8,128)S(1)}, f32[9,8,256]{2,1,0:T(8,128)}, u32[]{:S(2)}) copy-start(f32[9,8,256]{2,1,0:T(8,128)} %bottom.5) | copy-start | bytes 221188
  2.4 0.9 %copy-start.3 = (f32[9,8,256]{2,1,0:T(8,128)S(1)}, f32[9,8,256]{2,1,0:T(8,128)}, u32[]{:S(2)}) copy-start(f32[9,8,256]{2,1,0:T(8,128)} %top.5) | copy-start | bytes 221188
  3.2 0.8 %copy-start.5 = (s32[8,8,256]{2,1,0:T(8,128)S(1)}, s32[8,8,256]{2,1,0:T(8,128)}, u32[]{:S(2)}) copy-start(s32[8,8,256]{2,1,0:T(8,128)} %mask_ref.1) | copy-start | bytes 196612
  4.1 0.8 %copy-start.6 = (s32[8,8,256]{2,1,0:T(8,128)S(1)}, s32[8,8,256]{2,1,0:T(8,128)}, u32[]{:S(2)}) copy-start(s32[8,8,256]{2,1,0:T(8,128)} %rotor_ref.1) | copy-start | bytes 196612
  4.9 19.9 %copy-start.2 = (f32[9,8,256]{2,1,0:T(8,128)S(1)}, f32[9,8,256]{2,1,0:T(8,128)}, u32[]{:S(2)}) copy-start(f32[9,8,256]{2,1,0:T(8,128)} %bottom.5) | copy-start | bytes 221188
  4.9 19.9 %copy-start.4 = (f32[9,8,256]{2,1,0:T(8,128)S(1)}, f32[9,8,256]{2,1,0:T(8,128)}, u32[]{:S(2)}) copy-start(f32[9,8,256]{2,1,0:T(8,128)} %top.5) | copy-start | bytes 221188
  6.5 3.2 %collective-permute-start = (f32[9,8,128]{2,1,0:T(8,128)S(1)}, f32[9,8,128]{2,1,0:T(8,128)S(1)}, u32[]{:S(2)}, u32[]{:S(2)}) collective-permute-start(f32[9,8,128]{2,1,0:T(8,128)S(1)} %get-tuple-element.23), channel_id=1, source_target_pairs={{0,1},{1,2},{2,3},{3,4},{4,5},{5,6},{6,7},{7,8},{8,9},{9,10},{10,1... | collective-permute-start | bytes 110600 | tf_op jit(solution)/shard_map/ppermute | solution.py:447
  8.6 7.0 %collective-permute-start.1 = (f32[9,8,128]{2,1,0:T(8,128)S(1)}, f32[9,8,128]{2,1,0:T(8,128)S(1)}, u32[]{:S(2)}, u32[]{:S(2)}) collective-permute-start(f32[9,8,128]{2,1,0:T(8,128)S(1)} %get-tuple-element.24), channel_id=1, source_target_pairs={{1,0},{2,1},{3,2},{4,3},{5,4},{6,5},{7,6},{8,7},{9,8},{10,9},{11,1... | collective-permute-start | bytes 110600 | tf_op jit(solution)/shard_map/ppermute | solution.py:448
  15.7 5.2 %collective-permute-start.2 = (f32[19,8,128]{2,1,0:T(8,128)S(1)}, f32[19,8,128]{2,1,0:T(8,128)S(1)}, u32[]{:S(2)}, u32[]{:S(2)}) collective-permute-start(f32[19,8,128]{2,1,0:T(8,128)S(1)} %get-tuple-element.27), channel_id=1, source_target_pairs={{0,16},{16,32},{32,48},{48,64},{64,80},{80,96},{96,112},{112,128},... | collective-permute-start | bytes 233480 | tf_op jit(solution)/shard_map/ppermute | solution.py:447
  19.5 5.4 %collective-permute-start.3 = (f32[19,8,128]{2,1,0:T(8,128)S(1)}, f32[19,8,128]{2,1,0:T(8,128)S(1)}, u32[]{:S(2)}, u32[]{:S(2)}) collective-permute-start(f32[19,8,128]{2,1,0:T(8,128)S(1)} %get-tuple-element.28), channel_id=1, source_target_pairs={{16,0},{32,16},{48,32},{64,48},{80,64},{96,80},{112,96},{128,112},... | collective-permute-start | bytes 233480 | tf_op jit(solution)/shard_map/ppermute | solution.py:448
  26.8 3.1 %collective-permute-start.4 = (f32[16,8,128]{2,1,0:T(8,128)S(1)}, f32[16,8,128]{2,1,0:T(8,128)S(1)}, u32[]{:S(2)}, u32[]{:S(2)}) collective-permute-start(f32[16,8,128]{2,1,0:T(8,128)S(1)} %get-tuple-element.33), channel_id=1, source_target_pairs={{0,16},{16,32},{32,48},{48,64},{64,80},{80,96},{96,112},{112,128},... | collective-permute-start | bytes 196616 | tf_op jit(solution)/shard_map/ppermute | solution.py:447
  26.8 5.3 %collective-permute-start.5 = (f32[16,8,128]{2,1,0:T(8,128)S(1)}, f32[16,8,128]{2,1,0:T(8,128)S(1)}, u32[]{:S(2)}, u32[]{:S(2)}) collective-permute-start(f32[16,8,128]{2,1,0:T(8,128)S(1)} %get-tuple-element.34), channel_id=1, source_target_pairs={{16,0},{32,16},{48,32},{64,48},{80,64},{96,80},{112,96},{128,112},... | collective-permute-start | bytes 196616 | tf_op jit(solution)/shard_map/ppermute | solution.py:448

commit v2 on v1

--- a/solution.py
+++ b/solution.py
@@ -132,10 +132,27 @@
     return rotor_sums(marks, speeds, first)
 
 
-def first_kernel(f_ref, mask_ref, rotor_ref, bottom, top, state, labels, edges, to_up, to_down):
+def first_kernel(
+    f_hbm, mask_hbm, rotor_hbm, bottom_hbm, top_hbm, state, labels, edges, to_even, to_odd,
+    f_ref, mask_ref, rotor_ref, bottom, top, arrived,
+):
     lanes = iota(1)
+    levels = [pltpu.make_async_copy(f_hbm.at[:, z], f_ref.at[:, z], arrived.at[z]) for z in range(LEVELS)]
+    others = [
+        pltpu.make_async_copy(source, target, arrived.at[LEVELS + n])
+        for n, (source, target) in enumerate(
+            ((mask_hbm, mask_ref), (rotor_hbm, rotor_ref), (bottom_hbm, bottom), (top_hbm, top))
+        )
+    ]
+    for copy in [levels[0]] + others[:2] + levels[1:] + others[2:]:
+        copy.start()
+    others[0].wait()
+    others[1].wait()
+    waiting = list(levels)
 
     def f(z, j, a, b, c):
+        if len(waiting) == LEVELS - z:
+            waiting.pop(0).wait()
         return f_ref[9 * a + 3 * b + c, z, :, 128 * j : 128 * j + 128]
 
     def label(z, j):
@@ -158,14 +175,20 @@
     for n, block in enumerate(blocks):
         edges[n] = block
     edges[11] = sums
+    upward_first = lax.rem(lax.axis_index("gy"), 2) == 0
     low = (lanes & 8) == 0
+
+    def send(n, upward, downward):
+        to_even[n] = jnp.where(upward_first, upward, downward)
+        to_odd[n] = jnp.where(upward_first, downward, upward)
+
     for n in range(6):
         one = blocks[2 * n]
         other = blocks[2 * n + 1] if n < 5 else one
-        to_up[n] = jnp.where(low, one, roll(other, 8, 1))
-        to_down[n] = jnp.where(low, roll(other, -8, 1), one)
-    to_up[6] = sums
-    to_down[6] = sums
+        send(n, jnp.where(low, one, roll(other, 8, 1)), jnp.where(low, roll(other, -8, 1), one))
+    send(6, sums, sums)
+    others[2].wait()
+    others[3].wait()
     for place, source in ((7, bottom), (8, top)):
         upward = jnp.zeros((8, 128), jnp.float32)
         downward = upward
@@ -174,8 +197,7 @@
             moved = roll(both, 8 * n + 8, 1)
             upward = jnp.where(lanes // 8 == n, moved, upward)
             downward = jnp.where(lanes // 8 == n + 1, moved, downward)
-        to_up[place] = upward
-        to_down[place] = downward
+        send(place, upward, downward)
 
 
 def rows_of(blocks, row):
@@ -195,7 +217,13 @@
     return slot
 
 
-def relay_kernel(state, labels, edges, below, above, domains, to_right, to_left, column_sums):
+def relay_kernel(state, labels, edges, even, odd, domains, to_right, to_left, column_sums, beside):
+    upward_first = lax.rem(lax.axis_index("gy"), 2) == 0
+    below = [jnp.where(upward_first, odd[n], even[n]) for n in range(9)]
+    above = [jnp.where(upward_first, even[n], odd[n]) for n in range(9)]
+    for side, message in enumerate((below, above)):
+        for n in range(2):
+            beside[side, n] = message[7 + n]
     low = (iota(1) & 8) == 0
     sums = edges[11] + below[6] + above[6]
     column_sums[...] = sums
@@ -258,32 +286,31 @@
     return [jnp.broadcast_to(block[n : n + 1], (8, 128)) for n in range(count)]
 
 
-def step_domain(table, side, domains, left, right, below, above):
+def step_domain(table, side, domains, left, right, beside):
     lanes = iota(1)
     d = [domains[side, n] for n in range(10)]
     thrust = look_up(table, index_of(domains[side, 10]))
     parts = [d[RHO] * h for h in shapes(d[VX] - thrust)]
     along_y, along_z = shapes(d[VY]), shapes(d[VZ])
     n = 2 * len(X_FIELDS) + 2 + side
-    beside = {}
+    outer = {}
     for a, message in ((2, left), (0, right)):
         fields = row_blocks(message[n], 8)
-        beside[a] = entering(table, fields[:7], index_of(fields[7]), a)
+        outer[a] = entering(table, fields[:7], index_of(fields[7]), a)
     into, new = {}, {}
     for a in range(3):
         for b in range(3):
             for c in range(3):
                 value = slot_value(d, parts, along_y, along_z, a, b, c)
-                value = shift_rows(value, a, beside[2][b, c], beside[0][b, c])
+                value = shift_rows(value, a, outer[2][b, c], outer[0][b, c])
                 value = roll(value, b - 1, 1)
                 if b == 2 - 2 * side:
                     into[a, c] = value
                 slot = 3 * a + b
-                message = above if side else below
                 if c == 2:
-                    value = jnp.where(lanes < 16, roll(message[7], -8 * slot, 1), roll(value, 16, 1))
+                    value = jnp.where(lanes < 16, roll(beside[side, 0], -8 * slot, 1), roll(value, 16, 1))
                 elif c == 0:
-                    value = jnp.where(lanes >= 112, roll(message[8], 112 - 8 * slot, 1), roll(value, -16, 1))
+                    value = jnp.where(lanes >= 112, roll(beside[side, 1], 112 - 8 * slot, 1), roll(value, -16, 1))
                 new[a, b, c] = value
     return into, new
 
@@ -320,7 +347,7 @@
     return columns
 
 
-def stream(table, state, labels, columns, left, right, left_marks, right_marks, bottom, top, out, ghost):
+def stream(table, state, labels, columns, left, right, left_marks, right_marks, bottom, top, out, ghost, whole=None):
     lanes = iota(1)
     for side, (source, marks) in enumerate(((left, left_marks), (right, right_marks))):
         a = 2 - 2 * side
@@ -328,6 +355,11 @@
             fields = [source[2 * n + j] for n in range(len(X_FIELDS))]
             for (b, c), value in entering(table, fields, marks(j), a).items():
                 ghost[side, 3 * b + c, j] = value
+
+    for a in range(3):
+        for b in range(3):
+            out[9 * a + 3 * b + 2, 0] = bottom[3 * a + b]
+            out[9 * a + 3 * b, LEVELS - 1] = top[3 * a + b]
 
     for z in range(LEVELS):
         tiles = []
@@ -362,10 +394,10 @@
                         second = jnp.where(lanes == 127, inflow, second)
                     out[9 * a + 3 * b + c, level, :, 0:128] = first
                     out[9 * a + 3 * b + c, level, :, 128:256] = second
-    for a in range(3):
-        for b in range(3):
-            out[9 * a + 3 * b + 2, 0] = bottom[3 * a + b]
-            out[9 * a + 3 * b, LEVELS - 1] = top[3 * a + b]
+        if whole and z:
+            whole(z - 1)
+    if whole:
+        whole(LEVELS - 1)
 
 
 def disk_table(sums, counts):
@@ -378,7 +410,7 @@
 
 
 def middle_kernel(
-    state, labels, domains, column_sums, left, right, below, above, bottom, top,
+    state, labels, domains, column_sums, beside, left, right, bottom, top,
     new_state, to_right, to_left, strip, counts, sums_out, f_ref, ghost,
 ):
     lanes = iota(1)
@@ -391,7 +423,7 @@
 
     marks, speeds, kept, columns = [], [], [], [{}, {}]
     for side in range(2):
-        columns[side], new = step_domain(table, side, domains, left, right, below, above)
+        columns[side], new = step_domain(table, side, domains, left, right, beside)
         ux, fields = relax(low_moments(lambda a, b, c: new[a, b, c]))
         column = lanes & 15
         near = jnp.logical_and(column >= 8, column < 13) if side else jnp.logical_and(column >= 3, column < 8)
@@ -420,23 +452,34 @@
 
 
 def last_kernel(
-    state, labels, strip, sums, counts, left, right, old_left, old_right, bottom, top, out, ghost
+    state, labels, strip, sums, counts, left, right, old_left, old_right, bottom, top, out_hbm, out, ghost, gone
 ):
     last = 2 * len(X_FIELDS) + 1
     totals = sums[...] + left[last] + right[last]
     table = disk_table(totals, counts[...])
     columns = last_columns(table, strip, left, right)
-    stream(table, state, labels, columns, left, right, marks_of(old_left), marks_of(old_right), bottom, top, out, ghost)
-
-
-def call(kernel, inputs, outputs, scratch=()):
-    whole = pl.BlockSpec(memory_space=pltpu.VMEM)
+    copies = [pltpu.make_async_copy(out.at[:, z], out_hbm.at[:, z], gone.at[z]) for z in range(LEVELS)]
+    stream(
+        table, state, labels, columns, left, right, marks_of(old_left), marks_of(old_right), bottom, top, out, ghost,
+        whole=lambda z: copies[z].start(),
+    )
+    for copy in copies:
+        copy.wait()
+
+
+def call(kernel, inputs, outputs, scratch=(), in_hbm=0, out_hbm=0, copies=0):
+    inputs = [pltpu.with_memory_space_constraint(x, pltpu.HBM) if n < in_hbm else x for n, x in enumerate(inputs)]
+
+    def specs(count, outside):
+        return [pl.BlockSpec(memory_space=pltpu.HBM if n < outside else pltpu.VMEM) for n in range(count)]
+
     return pl.pallas_call(
         kernel,
         out_shape=[jax.ShapeDtypeStruct(shape, dtype) for shape, dtype in outputs],
-        in_specs=[whole] * len(inputs),
-        out_specs=[whole] * len(outputs),
-        scratch_shapes=[pltpu.VMEM(shape, jnp.float32) for shape in scratch],
+        in_specs=specs(len(inputs), in_hbm),
+        out_specs=specs(len(outputs), out_hbm),
+        scratch_shapes=[pltpu.VMEM(shape, dtype) for shape, dtype in scratch]
+        + ([pltpu.SemaphoreType.DMA((copies,))] if copies else []),
         compiler_params=pltpu.CompilerParams(vmem_limit_bytes=VMEM_LIMIT),
     )(*inputs)
 
@@ -449,40 +492,58 @@
     )
 
 
+def swapped(even, odd, axis):
+    count = lax.axis_size(axis)
+
+    def pairs(start):
+        there = [(i, (i + 1) % count) for i in range(start, count, 2)]
+        return there + [(j, i) for i, j in there]
+
+    return lax.ppermute(even, axis, pairs(0)), lax.ppermute(odd, axis, pairs(1))
+
+
 def body(populations, bottom_in, top_in, turbine_mask, rotor_index):
     f32 = jnp.float32
     state_shape = ((10, 2, 64, 128), f32)
     one = ((8, 128), f32)
-    ghost = (2, 9, 2, 8, 128)
+    ghost = ((2, 9, 2, 8, 128), f32)
+    inflow = (bottom_in.shape, f32)
+    cells = (turbine_mask.shape, jnp.int32)
+    whole = (populations.shape, f32)
     n = 2 * len(X_FIELDS)
 
     def blocks(*count):
         return (count + (8, 128), f32)
 
-    state, labels, edges, to_up, to_down = call(
+    state, labels, edges, to_even, to_odd = call(
         first_kernel,
         (populations, turbine_mask, rotor_index, bottom_in, top_in),
         (state_shape, ((2, 64, 128), jnp.int32), blocks(12), blocks(9), blocks(9)),
-    )
-    below, above = both_ways(to_up, to_down, "gy")
-    domains, to_right, to_left, column_sums = call(
+        (whole, cells, cells, inflow, inflow),
+        in_hbm=5,
+        copies=LEVELS + 4,
+    )
+    even, odd = swapped(to_even, to_odd, "gy")
+    domains, to_right, to_left, column_sums, beside = call(
         relay_kernel,
-        (state, labels, edges, below, above),
-        (blocks(2, 11), blocks(n + 5), blocks(n + 5), one),
+        (state, labels, edges, even, odd),
+        (blocks(2, 11), blocks(n + 5), blocks(n + 5), one, blocks(2, 2)),
     )
     old_left, old_right = both_ways(to_right, to_left, "gx")
     state, to_right, to_left, strip, counts, sums = call(
         middle_kernel,
-        (state, labels, domains, column_sums, old_left, old_right, below, above, bottom_in, top_in),
+        (state, labels, domains, column_sums, beside, old_left, old_right, bottom_in, top_in),
         (state_shape, blocks(n + 2), blocks(n + 2), blocks(8), one, one),
-        (populations.shape, ghost),
+        (whole, ghost),
     )
     left, right = both_ways(to_right, to_left, "gx")
     (out,) = call(
         last_kernel,
         (state, labels, strip, sums, counts, left, right, old_left, old_right, bottom_in, top_in),
-        ((populations.shape, f32),),
-        (ghost,),
+        (whole,),
+        (whole, ghost),
+        out_hbm=1,
+        copies=LEVELS,
     )
     return out
 

time: 34.6 us -> 30.7 us (0.89)
  the two profiles are of different devices: /device:TPU:123 before, /device:TPU:102 now
where the time goes in v2:
time: 30.7 us; the launch traced here: 30.6 us
  waiting for transfers between devices  14 us (46%)
  starting transfers between devices  9.56 us (31%)
  Pallas kernels  7 us (23%)
    pallas_call x4, Pallas kernels, call(): pl.pallas_call(kernel, out_shape=[jax.ShapeDtypeStruct(shape, dtype) for...  7 us
    ppermute x2, waiting for transfers between devices, both_ways(): lax.ppermute(downward, axis, [((i + 1) % count, i) for i in range(count)])  6.66 us
    ppermute x2, waiting for transfers between devices, both_ways(): lax.ppermute(upward, axis, [(i, (i + 1) % count) for i in range(count)])  4.26 us
    ppermute x1, starting transfers between devices, swapped(): lax.ppermute(odd, axis, pairs(1))  3.96 us
    ppermute x2, starting transfers between devices, both_ways(): lax.ppermute(upward, axis, [(i, (i + 1) % count) for i in range(count)])  3.48 us
    ppermute x1, waiting for transfers between devices, swapped(): lax.ppermute(odd, axis, pairs(1))  3.12 us
    ppermute x2, starting transfers between devices, both_ways(): lax.ppermute(downward, axis, [((i + 1) % count, i) for i in range(count)])  2.03 us
  transfers between devices with their start and end apart: 6, of which 5 were waited for; matrix products, arithmetic and copies ran while one was open for 0% of the time, Pallas kernels for 0%

profile of v2, /device:TPU:102, one launch (start us, length us, event | category | flops | bytes accessed | tf_op | source)
XLA Modules:
  0.0 30.6 jit_solution(9225063347538373568)
XLA Ops:
  0.0 0.0 copy-start.1
  0.0 0.0 copy-start
  0.0 3.1 %shard_map.55 = (f32[10,2,64,128]{3,2,1,0:T(8,128)S(1)}, s32[2,64,128]{2,1,0:T(8,128)S(1)}, f32[12,8,128]{2,1,0:T(8,128)S(1)}, f32[9,8,128]{2,1,0:T(8,128)S(1)}, f32[9,8,128]{2,1,0:T(8,128)S(1)}) custom-call(f32[27,8,8,256]{3,2,1,0:T(8,128)} %f_hbm.1, s32[8,8,256]{2,1,0:T(8,128)} %mask_hbm.1, s32[8,8,256]{2,1,0:T(8,128)} %rotor_hbm.1, f32[9,8,256]{2,1,0:T(8,128)} %bottom.3, ...), custom_call_target="tpu_custom_call" | custom-call | tf_op jit(solution)/shard_map/pallas_call | solution.py:476
  3.1 0.1 collective-permute-start
  3.2 4.0 %collective-permute-start.1 = (f32[9,8,128]{2,1,0:T(8,128)S(1)}, f32[9,8,128]{2,1,0:T(8,128)S(1)}, u32[]{:S(2)}, u32[]{:S(2)}) collective-permute-start(f32[9,8,128]{2,1,0:T(8,128)S(1)} %get-tuple-element.25), channel_id=1, source_target_pairs={{1,2},{3,4},{5,6},{7,8},{9,10},{11,12},{13,14},{15,0},{2,1},{4,3},... | collective-permute-start | bytes 110600 | tf_op jit(solution)/shard_map/ppermute | solution.py:502
  7.2 0.0 collective-permute-done.even
  7.2 3.1 %collective-permute-done.1.odd = f32[9,8,128]{2,1,0:T(8,128)S(1)} collective-permute-done((f32[9,8,128]{2,1,0:T(8,128)S(1)}, f32[9,8,128]{2,1,0:T(8,128)S(1)}, u32[]{:S(2)}, u32[]{:S(2)}) %collective-permute-start.1) | collective-permute-done | bytes 36896 | tf_op jit(solution)/shard_map/ppermute | solution.py:502
  10.3 0.1 shard_map.56
  10.4 3.5 %collective-permute-start.2 = (f32[19,8,128]{2,1,0:T(8,128)S(1)}, f32[19,8,128]{2,1,0:T(8,128)S(1)}, u32[]{:S(2)}, u32[]{:S(2)}) collective-permute-start(f32[19,8,128]{2,1,0:T(8,128)S(1)} %get-tuple-element.29), channel_id=1, source_target_pairs={{0,16},{16,32},{32,48},{48,64},{64,80},{80,96},{96,112},{112,128},... | collective-permute-start | bytes 233480 | tf_op jit(solution)/shard_map/ppermute | solution.py:490
  13.9 0.0 collective-permute-start.3
  13.9 2.0 %collective-permute-done.2.left.old_left = f32[19,8,128]{2,1,0:T(8,128)S(1)} collective-permute-done((f32[19,8,128]{2,1,0:T(8,128)S(1)}, f32[19,8,128]{2,1,0:T(8,128)S(1)}, u32[]{:S(2)}, u32[]{:S(2)}) %collective-permute-start.2) | collective-permute-done | bytes 77856 | tf_op jit(solution)/shard_map/ppermute | solution.py:490
  15.9 4.5 %collective-permute-done.3.right.old_right = f32[19,8,128]{2,1,0:T(8,128)S(1)} collective-permute-done((f32[19,8,128]{2,1,0:T(8,128)S(1)}, f32[19,8,128]{2,1,0:T(8,128)S(1)}, u32[]{:S(2)}, u32[]{:S(2)}) %collective-permute-start.3) | collective-permute-done | bytes 77856 | tf_op jit(solution)/shard_map/ppermute | solution.py:491
  20.4 0.0 copy-done.1
  20.4 0.0 copy-done
  20.4 2.0 %shard_map.57 = (f32[10,2,64,128]{3,2,1,0:T(8,128)S(1)}, f32[16,8,128]{2,1,0:T(8,128)S(1)}, f32[16,8,128]{2,1,0:T(8,128)S(1)}, f32[8,8,128]{2,1,0:T(8,128)S(1)},...) custom-call(f32[10,2,64,128]{3,2,1,0:T(8,128)S(1)} %get-tuple-element.21.state, s32[2,64,128]{2,1,0:T(8,128)S(1)} %get-tuple-element.22.labels, ...), custom_call_target="tpu_custom_call" | custom-call | tf_op jit(solution)/shard_map/pallas_call | solution.py:476
  22.4 0.0 collective-permute-start.4
  22.4 2.0 %collective-permute-start.5 = (f32[16,8,128]{2,1,0:T(8,128)S(1)}, f32[16,8,128]{2,1,0:T(8,128)S(1)}, u32[]{:S(2)}, u32[]{:S(2)}) collective-permute-start(f32[16,8,128]{2,1,0:T(8,128)S(1)} %get-tuple-element.36), channel_id=1, source_target_pairs={{16,0},{32,16},{48,32},{64,48},{80,64},{96,80},{112,96},{128,112},... | collective-permute-start | bytes 196616 | tf_op jit(solution)/shard_map/ppermute | solution.py:491
  24.4 2.2 %collective-permute-done.4.left = f32[16,8,128]{2,1,0:T(8,128)S(1)} collective-permute-done((f32[16,8,128]{2,1,0:T(8,128)S(1)}, f32[16,8,128]{2,1,0:T(8,128)S(1)}, u32[]{:S(2)}, u32[]{:S(2)}) %collective-permute-start.4) | collective-permute-done | bytes 65568 | tf_op jit(solution)/shard_map/ppermute | solution.py:490
  26.6 2.2 %collective-permute-done.5.right = f32[16,8,128]{2,1,0:T(8,128)S(1)} collective-permute-done((f32[16,8,128]{2,1,0:T(8,128)S(1)}, f32[16,8,128]{2,1,0:T(8,128)S(1)}, u32[]{:S(2)}, u32[]{:S(2)}) %collective-permute-start.5) | collective-permute-done | bytes 65568 | tf_op jit(solution)/shard_map/ppermute | solution.py:491
  28.8 1.8 %shard_map.58 = f32[27,8,8,256]{3,2,1,0:T(8,128)} custom-call(f32[10,2,64,128]{3,2,1,0:T(8,128)S(1)} %get-tuple-element.31.state, s32[2,64,128]{2,1,0:T(8,128)S(1)} %get-tuple-element.22.labels, f32[8,8,128]{2,1,0:T(8,128)S(1)} %get-tuple-element.32.strip, f32[8,128]{1,0:T(8,128)S(1)} %get-tuple-element.33.sums, f32[8,128]{1,0:T(8,128)S(1)} %get-tuple-element.34.counts, ...), custom_call_target="tpu_custom_call" | custom-call | tf_op jit(solution)/shard_map/pallas_call | solution.py:476
Async XLA Ops:
  0.0 20.4 %copy-start.1 = (f32[9,8,256]{2,1,0:T(8,128)S(1)}, f32[9,8,256]{2,1,0:T(8,128)}, u32[]{:S(2)}) copy-start(f32[9,8,256]{2,1,0:T(8,128)} %top.3) | copy-start | bytes 221188
  0.0 20.4 %copy-start = (f32[9,8,256]{2,1,0:T(8,128)S(1)}, f32[9,8,256]{2,1,0:T(8,128)}, u32[]{:S(2)}) copy-start(f32[9,8,256]{2,1,0:T(8,128)} %bottom.3) | copy-start | bytes 221188
  3.1 4.1 %collective-permute-start = (f32[9,8,128]{2,1,0:T(8,128)S(1)}, f32[9,8,128]{2,1,0:T(8,128)S(1)}, u32[]{:S(2)}, u32[]{:S(2)}) collective-permute-start(f32[9,8,128]{2,1,0:T(8,128)S(1)} %get-tuple-element.24), channel_id=1, source_target_pairs={{0,1},{2,3},{4,5},{6,7},{8,9},{10,11},{12,13},{14,15},{1,0},{3,2},... | collective-permute-start | bytes 110600 | tf_op jit(solution)/shard_map/ppermute | solution.py:502
  3.2 7.1 %collective-permute-start.1 = (f32[9,8,128]{2,1,0:T(8,128)S(1)}, f32[9,8,128]{2,1,0:T(8,128)S(1)}, u32[]{:S(2)}, u32[]{:S(2)}) collective-permute-start(f32[9,8,128]{2,1,0:T(8,128)S(1)} %get-tuple-element.25), channel_id=1, source_target_pairs={{1,2},{3,4},{5,6},{7,8},{9,10},{11,12},{13,14},{15,0},{2,1},{4,3},... | collective-permute-start | bytes 110600 | tf_op jit(solution)/shard_map/ppermute | solution.py:502
  10.4 5.5 %collective-permute-start.2 = (f32[19,8,128]{2,1,0:T(8,128)S(1)}, f32[19,8,128]{2,1,0:T(8,128)S(1)}, u32[]{:S(2)}, u32[]{:S(2)}) collective-permute-start(f32[19,8,128]{2,1,0:T(8,128)S(1)} %get-tuple-element.29), channel_id=1, source_target_pairs={{0,16},{16,32},{32,48},{48,64},{64,80},{80,96},{96,112},{112,128},... | collective-permute-start | bytes 233480 | tf_op jit(solution)/shard_map/ppermute | solution.py:490
  13.9 6.5 %collective-permute-start.3 = (f32[19,8,128]{2,1,0:T(8,128)S(1)}, f32[19,8,128]{2,1,0:T(8,128)S(1)}, u32[]{:S(2)}, u32[]{:S(2)}) collective-permute-start(f32[19,8,128]{2,1,0:T(8,128)S(1)} %get-tuple-element.30), channel_id=1, source_target_pairs={{16,0},{32,16},{48,32},{64,48},{80,64},{96,80},{112,96},{128,112},... | collective-permute-start | bytes 233480 | tf_op jit(solution)/shard_map/ppermute | solution.py:491
  22.4 4.3 %collective-permute-start.4 = (f32[16,8,128]{2,1,0:T(8,128)S(1)}, f32[16,8,128]{2,1,0:T(8,128)S(1)}, u32[]{:S(2)}, u32[]{:S(2)}) collective-permute-start(f32[16,8,128]{2,1,0:T(8,128)S(1)} %get-tuple-element.35), channel_id=1, source_target_pairs={{0,16},{16,32},{32,48},{48,64},{64,80},{80,96},{96,112},{112,128},... | collective-permute-start | bytes 196616 | tf_op jit(solution)/shard_map/ppermute | solution.py:490
  22.4 6.4 %collective-permute-start.5 = (f32[16,8,128]{2,1,0:T(8,128)S(1)}, f32[16,8,128]{2,1,0:T(8,128)S(1)}, u32[]{:S(2)}, u32[]{:S(2)}) collective-permute-start(f32[16,8,128]{2,1,0:T(8,128)S(1)} %get-tuple-element.36), channel_id=1, source_target_pairs={{16,0},{32,16},{48,32},{64,48},{80,64},{96,80},{112,96},{128,112},... | collective-permute-start | bytes 196616 | tf_op jit(solution)/shard_map/ppermute | solution.py:491

commit v3 on v2

--- a/solution.py
+++ b/solution.py
@@ -19,6 +19,9 @@
 VMEM_LIMIT = 48 * 1024 * 1024
 
 RHO, VX, VY, VZ, DXX, DYY, DZZ, DXY, DXZ, DYZ = range(10)
+SPEED = 10
+LABEL = 10
+SPAN = 5
 X_FIELDS = (RHO, VX, VY, VZ, DXX, DXY, DXZ)
 Y_FIELDS = (RHO, VX, VY, VZ, DYY, DXY, DYZ)
 
@@ -84,52 +87,107 @@
     return (0.5 * (square - speed), 1.0 - square, 0.5 * (square + speed))
 
 
-def spread(values):
+def over_rows(block, join=jnp.add):
+    for shift in (4, 2, 1):
+        block = join(block, roll(block, shift, 0))
+    return block
+
+
+def spread(leaf, join=jnp.add):
     lanes = iota(1)
-    stride = 1
-    while len(values) > 1:
-        first = (lanes & stride) == 0
-        values = [
-            jnp.where(first, a, b) + roll(jnp.where(first, b, a), stride, 1)
-            for a, b in zip(values[0::2], values[1::2])
-        ]
-        stride *= 2
-    total = values[0]
-    while stride < 128:
-        total = total + roll(total, stride, 1)
-        stride *= 2
-    for shift in (4, 2, 1):
-        total = total + roll(total, shift, 0)
-    return total
-
-
-def rotor_sums(labels, speeds, with_counts):
-    sums, counts = [], []
-    for rotor in range(ROTORS):
+
+    def node(stride, index):
+        if stride == 1:
+            return leaf(index)
+        half = stride // 2
+        a, b = node(half, index), node(half, index + half)
+        first = (lanes & half) == 0
+        return join(jnp.where(first, a, b), roll(jnp.where(first, b, a), half, 1))
+
+    return over_rows(node(128, 0), join)
+
+
+def rotor_sums(labels, speeds):
+    def leaf(index):
+        rotor, counting = index % ROTORS, index >= ROTORS
         total = jnp.zeros((8, 128), jnp.float32)
-        count = jnp.zeros((8, 128), jnp.float32)
         for label, speed in zip(labels, speeds):
-            hit = label == rotor
-            total = total + jnp.where(hit, speed, 0.0)
-            if with_counts:
-                count = count + jnp.where(hit, 1.0, 0.0)
-        sums.append(total)
-        counts.append(count)
-    if with_counts:
-        return spread(sums + counts)
-    return jnp.where(iota(1) < ROTORS, spread(sums), 0.0)
-
-
-def collide(f, label, state, marks=(), speeds=(), first=False):
-    marks, speeds = list(marks), list(speeds)
+            total = total + jnp.where(label == rotor, 1.0 if counting else speed, 0.0)
+        return total
+
+    return spread(leaf)
+
+
+def take(block, index):
+    return jnp.take_along_axis(block, index, axis=1, mode="promise_in_bounds")
+
+
+def sums_kernel(state, labels, own_sums):
+    places = [(j, z) for j in range(2) for z in range(LEVELS)]
+    own_sums[...] = rotor_sums(
+        [labels[j, 8 * z : 8 * z + 8, :] for j, z in places],
+        [state[SPEED, j, 8 * z : 8 * z + 8, :] for j, z in places],
+    )
+
+
+def beside_tile(domains, n):
+    return jnp.where((iota(1) & 8) == 0, domains[0, n], domains[1, n])
+
+
+def places_kernel(labels, domains, starts, found, found_beside):
+    lanes = iota(1)
+    far = 1024.0
+    column = lanes & 15
+    near = jnp.logical_and(column >= 3, column < 13)
+    outside = jnp.where(near, index_of(beside_tile(domains, LABEL)), EMPTY)
+    inside = {(j, z): labels[j, 8 * z : 8 * z + 8, :] for j in range(2) for z in range(LEVELS)}
+
+    def leaf(index):
+        rotor = index % ROTORS
+        if index >= ROTORS:
+            return jnp.where(outside == rotor, column.astype(jnp.float32), far)
+        first = jnp.full((8, 128), far, jnp.float32)
+        for j in range(2):
+            hit = inside[j, 0] == rotor
+            for z in range(1, LEVELS):
+                hit = jnp.logical_or(hit, inside[j, z] == rotor)
+            first = jnp.minimum(first, jnp.where(hit, (lanes + 128 * j).astype(jnp.float32), far))
+        return first
+
+    both = spread(leaf, jnp.minimum)
+    begin = (jnp.where(both < far, both, 0.0)).astype(jnp.int32)
+    begin_beside = roll(begin.astype(jnp.float32), 64, 1).astype(jnp.int32)
+    starts[0] = begin
+    starts[1] = begin_beside
+    own = jnp.where(lanes < ROTORS, lanes, -1)
+    for k in range(SPAN):
+        index = (begin + k) & 127
+        for z in range(LEVELS):
+            for j in range(2):
+                found[k, j, z] = jnp.where(take(inside[j, z], index) == own, 1.0, 0.0)
+            index_beside = (begin_beside + (k + 16 * z)) & 127
+            found_beside[k, z] = jnp.where(take(outside, index_beside) == own, 1.0, 0.0)
+
+
+def found_sums(speed, speed_beside, starts, found, found_beside):
+    total = jnp.zeros((8, 128), jnp.float32)
+    for k in range(SPAN):
+        index = (starts[0] + k) & 127
+        for z in range(LEVELS):
+            for j in range(2):
+                total = total + jnp.where(found[k, j, z] > 0.0, take(speed(z, j), index), 0.0)
+            index_beside = (starts[1] + (k + 16 * z)) & 127
+            total = total + jnp.where(found_beside[k, z] > 0.0, take(speed_beside, index_beside), 0.0)
+    return over_rows(total)
+
+
+def collide(f, state, keep_speed):
     for z in range(LEVELS):
         for j in range(2):
             ux, fields = relax(low_moments(functools.partial(f, z, j)))
             for index, value in enumerate(fields):
                 state[index, j, 8 * z : 8 * z + 8, :] = value
-            marks.append(label(z, j))
-            speeds.append(ux)
-    return rotor_sums(marks, speeds, first)
+            keep_speed(z, j, ux)
 
 
 def first_kernel(
@@ -155,26 +213,30 @@
             waiting.pop(0).wait()
         return f_ref[9 * a + 3 * b + c, z, :, 128 * j : 128 * j + 128]
 
-    def label(z, j):
+    def keep_speed(z, j, ux):
         here = (z, slice(None), slice(128 * j, 128 * j + 128))
-        mark = jnp.where(mask_ref[here] != 0, rotor_ref[here], EMPTY)
-        labels[j, 8 * z : 8 * z + 8, :] = mark
-        return mark
-
-    sums = collide(f, label, state, first=True)
+        state[SPEED, j, 8 * z : 8 * z + 8, :] = ux
+        labels[j, 8 * z : 8 * z + 8, :] = jnp.where(mask_ref[here] != 0, rotor_ref[here], EMPTY)
+
+    collide(f, state, keep_speed)
 
     def edge(read):
         block = jnp.zeros((8, 128), jnp.float32)
+        inner = block
         for z in range(LEVELS):
-            both = jnp.where(lanes < 64, read(z, 0), read(z, 1))
-            block = jnp.where(lanes // 16 == z, roll(both, 16 * z + 8, 1), block)
-        return block
-
-    blocks = [edge(lambda z, j, n=n: state[n, j, 8 * z : 8 * z + 8, :]) for n in range(10)]
-    blocks.append(edge(lambda z, j: labels[j, 8 * z : 8 * z + 8, :].astype(jnp.float32)))
+            moved = roll(jnp.where(lanes < 64, read(z, 0), read(z, 1)), 16 * z + 8, 1)
+            block = jnp.where(lanes // 16 == z, moved, block)
+            wanted = jnp.logical_or(((lanes - 16 * z + 2) & 127) < 2, ((lanes - 16 * z - 16) & 127) < 2)
+            inner = jnp.where(wanted, moved, inner)
+        return block, inner
+
+    pairs = [edge(lambda z, j, n=n: state[n, j, 8 * z : 8 * z + 8, :]) for n in range(10)]
+    pairs.append(edge(lambda z, j: labels[j, 8 * z : 8 * z + 8, :].astype(jnp.float32)))
+    pairs.append(edge(lambda z, j: state[SPEED, j, 8 * z : 8 * z + 8, :]))
+    blocks = [block for block, _ in pairs]
+    inner_label, inner_speed = pairs[LABEL][1], pairs[LABEL + 1][1]
     for n, block in enumerate(blocks):
         edges[n] = block
-    edges[11] = sums
     upward_first = lax.rem(lax.axis_index("gy"), 2) == 0
     low = (lanes & 8) == 0
 
@@ -183,10 +245,14 @@
         to_odd[n] = jnp.where(upward_first, downward, upward)
 
     for n in range(6):
-        one = blocks[2 * n]
-        other = blocks[2 * n + 1] if n < 5 else one
+        one, other = blocks[2 * n], blocks[2 * n + 1]
         send(n, jnp.where(low, one, roll(other, 8, 1)), jnp.where(low, roll(other, -8, 1), one))
-    send(6, sums, sums)
+    column = lanes & 15
+    send(
+        6,
+        jnp.where(column >= 14, inner_speed, jnp.where(column >= 12, roll(inner_label, -2, 1), float(EMPTY))),
+        jnp.where(column < 2, inner_speed, jnp.where(column < 4, roll(inner_label, 2, 1), float(EMPTY))),
+    )
     others[2].wait()
     others[3].wait()
     for place, source in ((7, bottom), (8, top)):
@@ -217,7 +283,7 @@
     return slot
 
 
-def relay_kernel(state, labels, edges, even, odd, domains, to_right, to_left, column_sums, beside):
+def relay_kernel(state, labels, edges, own_sums, even, odd, domains, to_right, to_left, column_sums, beside):
     upward_first = lax.rem(lax.axis_index("gy"), 2) == 0
     below = [jnp.where(upward_first, odd[n], even[n]) for n in range(9)]
     above = [jnp.where(upward_first, even[n], odd[n]) for n in range(9)]
@@ -225,25 +291,31 @@
         for n in range(2):
             beside[side, n] = message[7 + n]
     low = (iota(1) & 8) == 0
-    sums = edges[11] + below[6] + above[6]
-    column_sums[...] = sums
-    for n in range(11):
+    for n in range(12):
         under, over = below[n // 2], above[n // 2]
         if n % 2:
             under, over = roll(under, -8, 1), roll(over, 8, 1)
         domains[0, n] = jnp.where(low, under, edges[n])
         domains[1, n] = jnp.where(low, edges[n], over)
+    column = iota(1) & 15
+    inner = jnp.where(
+        column >= 14, roll(below[6], 2, 1), jnp.where(column < 2, roll(above[6], -2, 1), float(EMPTY))
+    )
+    sums = own_sums[...] + rotor_sums(
+        [index_of(beside_tile(domains, LABEL)), index_of(inner)],
+        [beside_tile(domains, LABEL + 1), jnp.where(column >= 8, below[6], above[6])],
+    )
+    column_sums[...] = sums
     for target, row in ((to_right, 7), (to_left, 0)):
         slot = edge_rows(state, target, row)
         for j in range(2):
             target[slot + j] = labels[j, pl.ds(row, 8, stride=8), :].astype(jnp.float32)
         for side in range(2):
-            target[slot + 2 + side] = rows_of([domains[side, n] for n in X_FIELDS + (10,)], row)
+            target[slot + 2 + side] = rows_of([domains[side, n] for n in X_FIELDS + (LABEL,)], row)
         target[slot + 4] = sums
 
 
-def look_up(table, label):
-    return jnp.take_along_axis(table, label, axis=1, mode="promise_in_bounds")
+look_up = take
 
 
 def index_of(mark):
@@ -289,7 +361,7 @@
 def step_domain(table, side, domains, left, right, beside):
     lanes = iota(1)
     d = [domains[side, n] for n in range(10)]
-    thrust = look_up(table, index_of(domains[side, 10]))
+    thrust = look_up(table, index_of(domains[side, LABEL]))
     parts = [d[RHO] * h for h in shapes(d[VX] - thrust)]
     along_y, along_z = shapes(d[VY]), shapes(d[VZ])
     n = 2 * len(X_FIELDS) + 2 + side
@@ -410,8 +482,8 @@
 
 
 def middle_kernel(
-    state, labels, domains, column_sums, beside, left, right, bottom, top,
-    new_state, to_right, to_left, strip, counts, sums_out, f_ref, ghost,
+    state, labels, domains, column_sums, beside, starts, found, found_beside, left, right, bottom, top,
+    new_state, to_right, to_left, strip, counts, sums_out, f_ref, ghost, speeds,
 ):
     lanes = iota(1)
     even = (lanes & 1) == 0
@@ -421,16 +493,12 @@
     counts[...] = seen
     table = disk_table(totals, seen)
 
-    marks, speeds, kept, columns = [], [], [], [{}, {}]
+    outside, kept, columns = [], [], [{}, {}]
     for side in range(2):
         columns[side], new = step_domain(table, side, domains, left, right, beside)
         ux, fields = relax(low_moments(lambda a, b, c: new[a, b, c]))
-        column = lanes & 15
-        near = jnp.logical_and(column >= 8, column < 13) if side else jnp.logical_and(column >= 3, column < 8)
-        mark = domains[side, 10]
-        marks.append(jnp.where(near, index_of(mark), EMPTY))
-        speeds.append(ux)
-        kept.append([fields[n] for n in Y_FIELDS] + [mark])
+        outside.append(ux)
+        kept.append([fields[n] for n in Y_FIELDS] + [domains[side, LABEL]])
     strips = [jnp.where(even, roll(one, 1, 1), roll(other, -1, 1)) for one, other in zip(*kept)]
     for n, block in enumerate(strips):
         strip[n] = block
@@ -440,10 +508,15 @@
     def f(z, j, a, b, c):
         return f_ref[9 * a + 3 * b + c, z, :, 128 * j : 128 * j + 128]
 
-    def label(z, j):
-        return labels[j, 8 * z : 8 * z + 8, :]
-
-    sums = collide(f, label, new_state, marks, speeds)
+    def keep_speed(z, j, ux):
+        speeds[j, z] = ux
+
+    collide(f, new_state, keep_speed)
+    sums = found_sums(
+        lambda z, j: speeds[j, z],
+        jnp.where((lanes & 8) == 0, outside[0], outside[1]),
+        starts, found, found_beside,
+    )
     sums_out[...] = sums
     for target, row in ((to_right, 7), (to_left, 0)):
         slot = edge_rows(new_state, target, row)
@@ -518,23 +591,32 @@
     state, labels, edges, to_even, to_odd = call(
         first_kernel,
         (populations, turbine_mask, rotor_index, bottom_in, top_in),
-        (state_shape, ((2, 64, 128), jnp.int32), blocks(12), blocks(9), blocks(9)),
+        (((11, 2, 64, 128), f32), ((2, 64, 128), jnp.int32), blocks(12), blocks(9), blocks(9)),
         (whole, cells, cells, inflow, inflow),
         in_hbm=5,
         copies=LEVELS + 4,
     )
     even, odd = swapped(to_even, to_odd, "gy")
+    (own_sums,) = call(sums_kernel, (state, labels), (one,))
     domains, to_right, to_left, column_sums, beside = call(
         relay_kernel,
-        (state, labels, edges, even, odd),
-        (blocks(2, 11), blocks(n + 5), blocks(n + 5), one, blocks(2, 2)),
+        (state, labels, edges, own_sums, even, odd),
+        (blocks(2, 12), blocks(n + 5), blocks(n + 5), one, blocks(2, 2)),
     )
     old_left, old_right = both_ways(to_right, to_left, "gx")
+    starts, found, found_beside = call(
+        places_kernel,
+        (labels, domains),
+        (((2, 8, 128), jnp.int32), blocks(SPAN, 2, LEVELS), blocks(SPAN, LEVELS)),
+    )
     state, to_right, to_left, strip, counts, sums = call(
         middle_kernel,
-        (state, labels, domains, column_sums, beside, old_left, old_right, bottom_in, top_in),
+        (
+            state, labels, domains, column_sums, beside, starts, found, found_beside,
+            old_left, old_right, bottom_in, top_in,
+        ),
         (state_shape, blocks(n + 2), blocks(n + 2), blocks(8), one, one),
-        (whole, ghost),
+        (whole, ghost, blocks(2, LEVELS)),
     )
     left, right = both_ways(to_right, to_left, "gx")
     (out,) = call(

time: 30.7 us -> 29.9 us (0.974)
  the two profiles are of different devices: /device:TPU:102 before, /device:TPU:98 now
where the time goes in v3:
time: 29.9 us; the launch traced here: 29.8 us
  waiting for transfers between devices  10.8 us (36%)
  starting transfers between devices  10.3 us (34%)
  Pallas kernels  8.62 us (29%)
    pallas_call x6, Pallas kernels, call(): pl.pallas_call(kernel, out_shape=[jax.ShapeDtypeStruct(shape, dtype) for...  8.62 us
    ppermute x2, waiting for transfers between devices, both_ways(): lax.ppermute(downward, axis, [((i + 1) % count, i) for i in range(count)])  6.76 us
    ppermute x1, starting transfers between devices, swapped(): lax.ppermute(odd, axis, pairs(1))  4.68 us
    ppermute x2, starting transfers between devices, both_ways(): lax.ppermute(upward, axis, [(i, (i + 1) % count) for i in range(count)])  3.53 us
    ppermute x2, waiting for transfers between devices, both_ways(): lax.ppermute(upward, axis, [(i, (i + 1) % count) for i in range(count)])  2.94 us
    ppermute x2, starting transfers between devices, both_ways(): lax.ppermute(downward, axis, [((i + 1) % count, i) for i in range(count)])  2.02 us
    ppermute x1, waiting for transfers between devices, swapped(): lax.ppermute(odd, axis, pairs(1))  1.11 us
  transfers between devices with their start and end apart: 6, of which 5 were waited for; matrix products, arithmetic and copies ran while one was open for 0% of the time, Pallas kernels for 9%

profile of v3, /device:TPU:98, one launch (start us, length us, event | category | flops | bytes accessed | tf_op | source)
XLA Modules:
  0.0 29.8 jit_solution(414133933868666315)
XLA Ops:
  0.0 0.0 copy-start.1
  0.0 0.0 copy-start
  0.0 2.0 %shard_map.55 = (f32[11,2,64,128]{3,2,1,0:T(8,128)S(1)}, s32[2,64,128]{2,1,0:T(8,128)S(1)}, f32[12,8,128]{2,1,0:T(8,128)S(1)}, f32[9,8,128]{2,1,0:T(8,128)S(1)}, f32[9,8,128]{2,1,0:T(8,128)S(1)}) custom-call(f32[27,8,8,256]{3,2,1,0:T(8,128)} %f_hbm.1, s32[8,8,256]{2,1,0:T(8,128)} %mask_hbm.1, s32[8,8,256]{2,1,0:T(8,128)} %rotor_hbm.1, f32[9,8,256]{2,1,0:T(8,128)} %bottom.3, ...), custom_call_target="tpu_custom_call" | custom-call | tf_op jit(solution)/shard_map/pallas_call | solution.py:549
  2.0 0.1 collective-permute-start
  2.1 4.7 %collective-permute-start.1 = (f32[9,8,128]{2,1,0:T(8,128)S(1)}, f32[9,8,128]{2,1,0:T(8,128)S(1)}, u32[]{:S(2)}, u32[]{:S(2)}) collective-permute-start(f32[9,8,128]{2,1,0:T(8,128)S(1)} %get-tuple-element.28), channel_id=1, source_target_pairs={{1,2},{3,4},{5,6},{7,8},{9,10},{11,12},{13,14},{15,0},{2,1},{4,3},... | collective-permute-start | bytes 110600 | tf_op jit(solution)/shard_map/ppermute | solution.py:575
  6.8 1.3 %shard_map.56.own_sums = f32[8,128]{1,0:T(8,128)S(1)} custom-call(f32[11,2,64,128]{3,2,1,0:T(8,128)S(1)} %get-tuple-element.24.state, s32[2,64,128]{2,1,0:T(8,128)S(1)} %get-tuple-element.25.labels), custom_call_target="tpu_custom_call" | custom-call | tf_op jit(solution)/shard_map/pallas_call | solution.py:549
  8.1 0.0 collective-permute-done.even
  8.1 1.1 %collective-permute-done.1.odd = f32[9,8,128]{2,1,0:T(8,128)S(1)} collective-permute-done((f32[9,8,128]{2,1,0:T(8,128)S(1)}, f32[9,8,128]{2,1,0:T(8,128)S(1)}, u32[]{:S(2)}, u32[]{:S(2)}) %collective-permute-start.1) | collective-permute-done | bytes 36896 | tf_op jit(solution)/shard_map/ppermute | solution.py:575
  9.2 0.6 %shard_map.57 = (f32[2,12,8,128]{3,2,1,0:T(8,128)S(1)}, f32[19,8,128]{2,1,0:T(8,128)S(1)}, f32[19,8,128]{2,1,0:T(8,128)S(1)}, f32[8,128]{1,0:T(8,128)S(1)}, f32[2,2,8,128]{3,2,1,0:T(8,128)S(1)}) custom-call(f32[11,2,64,128]{3,2,1,0:T(8,128)S(1)} %get-tuple-element.24.state, s32[2,64,128]{2,1,0:T(8,128)S(1)} %get-tuple-element.25.labels, ...), custom_call_target="tpu_custom_call" | custom-call | tf_op jit(solution)/shard_map/pallas_call | solution.py:549
  9.9 3.4 %collective-permute-start.2 = (f32[19,8,128]{2,1,0:T(8,128)S(1)}, f32[19,8,128]{2,1,0:T(8,128)S(1)}, u32[]{:S(2)}, u32[]{:S(2)}) collective-permute-start(f32[19,8,128]{2,1,0:T(8,128)S(1)} %get-tuple-element.35), channel_id=1, source_target_pairs={{0,16},{16,32},{32,48},{48,64},{64,80},{80,96},{96,112},{112,128},... | collective-permute-start | bytes 233480 | tf_op jit(solution)/shard_map/ppermute | solution.py:563
  13.3 0.0 collective-permute-start.3
  13.3 1.3 %shard_map.58 = (s32[2,8,128]{2,1,0:T(8,128)S(1)}, f32[5,2,8,8,128]{4,3,2,1,0:T(8,128)S(1)}, f32[5,8,8,128]{3,2,1,0:T(8,128)S(1)}) custom-call(s32[2,64,128]{2,1,0:T(8,128)S(1)} %get-tuple-element.25.labels, f32[2,12,8,128]{3,2,1,0:T(8,128)S(1)} %get-tuple-element.29.domains), custom_call_target="tpu_custom_call" | custom-call | tf_op jit(solution)/shard_map/pallas_call | solution.py:549
  14.6 0.7 %collective-permute-done.2.left.old_left = f32[19,8,128]{2,1,0:T(8,128)S(1)} collective-permute-done((f32[19,8,128]{2,1,0:T(8,128)S(1)}, f32[19,8,128]{2,1,0:T(8,128)S(1)}, u32[]{:S(2)}, u32[]{:S(2)}) %collective-permute-start.2) | collective-permute-done | bytes 77856 | tf_op jit(solution)/shard_map/ppermute | solution.py:563
  15.4 4.6 %collective-permute-done.3.right.old_right = f32[19,8,128]{2,1,0:T(8,128)S(1)} collective-permute-done((f32[19,8,128]{2,1,0:T(8,128)S(1)}, f32[19,8,128]{2,1,0:T(8,128)S(1)}, u32[]{:S(2)}, u32[]{:S(2)}) %collective-permute-start.3) | collective-permute-done | bytes 77856 | tf_op jit(solution)/shard_map/ppermute | solution.py:564
  19.9 0.0 copy-done.1
  19.9 0.0 copy-done
  19.9 1.5 %shard_map.59 = (f32[10,2,64,128]{3,2,1,0:T(8,128)S(1)}, f32[16,8,128]{2,1,0:T(8,128)S(1)}, f32[16,8,128]{2,1,0:T(8,128)S(1)}, f32[8,8,128]{2,1,0:T(8,128)S(1)},...) custom-call(f32[11,2,64,128]{3,2,1,0:T(8,128)S(1)} %get-tuple-element.24.state, s32[2,64,128]{2,1,0:T(8,128)S(1)} %get-tuple-element.25.labels, ...), custom_call_target="tpu_custom_call" | custom-call | tf_op jit(solution)/shard_map/pallas_call | solution.py:549
  21.4 0.1 collective-permute-start.4
  21.5 2.0 %collective-permute-start.5 = (f32[16,8,128]{2,1,0:T(8,128)S(1)}, f32[16,8,128]{2,1,0:T(8,128)S(1)}, u32[]{:S(2)}, u32[]{:S(2)}) collective-permute-start(f32[16,8,128]{2,1,0:T(8,128)S(1)} %get-tuple-element.42), channel_id=1, source_target_pairs={{16,0},{32,16},{48,32},{64,48},{80,64},{96,80},{112,96},{128,112},... | collective-permute-start | bytes 196616 | tf_op jit(solution)/shard_map/ppermute | solution.py:564
  23.5 2.2 %collective-permute-done.4.left = f32[16,8,128]{2,1,0:T(8,128)S(1)} collective-permute-done((f32[16,8,128]{2,1,0:T(8,128)S(1)}, f32[16,8,128]{2,1,0:T(8,128)S(1)}, u32[]{:S(2)}, u32[]{:S(2)}) %collective-permute-start.4) | collective-permute-done | bytes 65568 | tf_op jit(solution)/shard_map/ppermute | solution.py:563
  25.8 2.2 %collective-permute-done.5.right = f32[16,8,128]{2,1,0:T(8,128)S(1)} collective-permute-done((f32[16,8,128]{2,1,0:T(8,128)S(1)}, f32[16,8,128]{2,1,0:T(8,128)S(1)}, u32[]{:S(2)}, u32[]{:S(2)}) %collective-permute-start.5) | collective-permute-done | bytes 65568 | tf_op jit(solution)/shard_map/ppermute | solution.py:564
  28.0 1.8 %shard_map.60 = f32[27,8,8,256]{3,2,1,0:T(8,128)} custom-call(f32[10,2,64,128]{3,2,1,0:T(8,128)S(1)} %get-tuple-element.37.state, s32[2,64,128]{2,1,0:T(8,128)S(1)} %get-tuple-element.25.labels, f32[8,8,128]{2,1,0:T(8,128)S(1)} %get-tuple-element.38.strip, f32[8,128]{1,0:T(8,128)S(1)} %get-tuple-element.39.sums, f32[8,128]{1,0:T(8,128)S(1)} %get-tuple-element.40.counts, ...), custom_call_target="tpu_custom_call" | custom-call | tf_op jit(solution)/shard_map/pallas_call | solution.py:549
Async XLA Ops:
  0.0 19.9 %copy-start.1 = (f32[9,8,256]{2,1,0:T(8,128)S(1)}, f32[9,8,256]{2,1,0:T(8,128)}, u32[]{:S(2)}) copy-start(f32[9,8,256]{2,1,0:T(8,128)} %top.3) | copy-start | bytes 221188
  0.0 19.9 %copy-start = (f32[9,8,256]{2,1,0:T(8,128)S(1)}, f32[9,8,256]{2,1,0:T(8,128)}, u32[]{:S(2)}) copy-start(f32[9,8,256]{2,1,0:T(8,128)} %bottom.3) | copy-start | bytes 221188
  2.0 6.1 %collective-permute-start = (f32[9,8,128]{2,1,0:T(8,128)S(1)}, f32[9,8,128]{2,1,0:T(8,128)S(1)}, u32[]{:S(2)}, u32[]{:S(2)}) collective-permute-start(f32[9,8,128]{2,1,0:T(8,128)S(1)} %get-tuple-element.27), channel_id=1, source_target_pairs={{0,1},{2,3},{4,5},{6,7},{8,9},{10,11},{12,13},{14,15},{1,0},{3,2},... | collective-permute-start | bytes 110600 | tf_op jit(solution)/shard_map/ppermute | solution.py:575
  2.1 7.1 %collective-permute-start.1 = (f32[9,8,128]{2,1,0:T(8,128)S(1)}, f32[9,8,128]{2,1,0:T(8,128)S(1)}, u32[]{:S(2)}, u32[]{:S(2)}) collective-permute-start(f32[9,8,128]{2,1,0:T(8,128)S(1)} %get-tuple-element.28), channel_id=1, source_target_pairs={{1,2},{3,4},{5,6},{7,8},{9,10},{11,12},{13,14},{15,0},{2,1},{4,3},... | collective-permute-start | bytes 110600 | tf_op jit(solution)/shard_map/ppermute | solution.py:575
  9.9 5.5 %collective-permute-start.2 = (f32[19,8,128]{2,1,0:T(8,128)S(1)}, f32[19,8,128]{2,1,0:T(8,128)S(1)}, u32[]{:S(2)}, u32[]{:S(2)}) collective-permute-start(f32[19,8,128]{2,1,0:T(8,128)S(1)} %get-tuple-element.35), channel_id=1, source_target_pairs={{0,16},{16,32},{32,48},{48,64},{64,80},{80,96},{96,112},{112,128},... | collective-permute-start | bytes 233480 | tf_op jit(solution)/shard_map/ppermute | solution.py:563
  13.3 6.6 %collective-permute-start.3 = (f32[19,8,128]{2,1,0:T(8,128)S(1)}, f32[19,8,128]{2,1,0:T(8,128)S(1)}, u32[]{:S(2)}, u32[]{:S(2)}) collective-permute-start(f32[19,8,128]{2,1,0:T(8,128)S(1)} %get-tuple-element.36), channel_id=1, source_target_pairs={{16,0},{32,16},{48,32},{64,48},{80,64},{96,80},{112,96},{128,112},... | collective-permute-start | bytes 233480 | tf_op jit(solution)/shard_map/ppermute | solution.py:564
  21.4 4.3 %collective-permute-start.4 = (f32[16,8,128]{2,1,0:T(8,128)S(1)}, f32[16,8,128]{2,1,0:T(8,128)S(1)}, u32[]{:S(2)}, u32[]{:S(2)}) collective-permute-start(f32[16,8,128]{2,1,0:T(8,128)S(1)} %get-tuple-element.41), channel_id=1, source_target_pairs={{0,16},{16,32},{32,48},{48,64},{64,80},{80,96},{96,112},{112,128},... | collective-permute-start | bytes 196616 | tf_op jit(solution)/shard_map/ppermute | solution.py:563
  21.5 6.5 %collective-permute-start.5 = (f32[16,8,128]{2,1,0:T(8,128)S(1)}, f32[16,8,128]{2,1,0:T(8,128)S(1)}, u32[]{:S(2)}, u32[]{:S(2)}) collective-permute-start(f32[16,8,128]{2,1,0:T(8,128)S(1)} %get-tuple-element.42), channel_id=1, source_target_pairs={{16,0},{32,16},{48,32},{64,48},{80,64},{96,80},{112,96},{128,112},... | collective-permute-start | bytes 196616 | tf_op jit(solution)/shard_map/ppermute | solution.py:564

commit v4 on v3

--- a/solution.py
+++ b/solution.py
@@ -16,7 +16,7 @@
 THRUST_GAIN = 4.0
 EMPTY = 127
 LEVELS = 8
-VMEM_LIMIT = 48 * 1024 * 1024
+VMEM_LIMIT = 24 * 1024 * 1024
 
 RHO, VX, VY, VZ, DXX, DYY, DZZ, DXY, DXZ, DYZ = range(10)
 SPEED = 10
@@ -96,15 +96,18 @@
 def spread(leaf, join=jnp.add):
     lanes = iota(1)
 
-    def node(stride, index):
-        if stride == 1:
-            return leaf(index)
-        half = stride // 2
-        a, b = node(half, index), node(half, index + half)
-        first = (lanes & half) == 0
-        return join(jnp.where(first, a, b), roll(jnp.where(first, b, a), half, 1))
-
-    return over_rows(node(128, 0), join)
+    def node(stride, ways, rest, index):
+        parts = [(node(*rest, index + d * stride) if rest else leaf(index + d * stride)) for d in range(ways)]
+        digit = (lanes // stride) % ways
+        moved = []
+        for k in range(ways):
+            picked = parts[k]
+            for d in range(1, ways):
+                picked = jnp.where(digit == d, parts[(d + k) % ways], picked)
+            moved.append(roll(picked, k * stride, 1))
+        return functools.reduce(join, moved)
+
+    return over_rows(node(16, 8, (2, 8, (1, 2, ())), 0), join)
 
 
 def rotor_sums(labels, speeds):
@@ -369,103 +372,144 @@
     for a, message in ((2, left), (0, right)):
         fields = row_blocks(message[n], 8)
         outer[a] = entering(table, fields[:7], index_of(fields[7]), a)
-    into, new = {}, {}
+    new = {}
     for a in range(3):
         for b in range(3):
             for c in range(3):
                 value = slot_value(d, parts, along_y, along_z, a, b, c)
                 value = shift_rows(value, a, outer[2][b, c], outer[0][b, c])
                 value = roll(value, b - 1, 1)
-                if b == 2 - 2 * side:
-                    into[a, c] = value
                 slot = 3 * a + b
                 if c == 2:
                     value = jnp.where(lanes < 16, roll(beside[side, 0], -8 * slot, 1), roll(value, 16, 1))
                 elif c == 0:
                     value = jnp.where(lanes >= 112, roll(beside[side, 1], 112 - 8 * slot, 1), roll(value, -16, 1))
                 new[a, b, c] = value
-    return into, new
-
-
-def last_columns(table, strip, left, right):
+    return outer, new
+
+
+def strip_corners(table, message, a):
     even = (iota(1) & 1) == 0
+    rho, vx, vy, vz, _, dxy, _, mark = row_blocks(message[2 * len(X_FIELDS)], 8)
+    along_y, along_z = shapes(vy), shapes(vz)
+    part = rho * shapes(vx - look_up(table, index_of(mark)))[a] * jnp.where(even, along_y[2], along_y[0])
+    slots = [part * along_z[c] for c in range(3)]
+    slots[1] = slots[1] + ((a - 1) * jnp.where(even, 0.25, -0.25)) * dxy
+    return slots
+
+
+def merged_strip(left_end, right_end):
+    return jnp.where((iota(1) & 1) == 0, roll(left_end, 1, 1), roll(right_end, -1, 1))
+
+
+def shift_columns(first, second, b, inflow):
+    lanes = iota(1)
+    if b == 2:
+        first, second = roll(first, 1, 1), roll(second, 1, 1)
+        return jnp.where(lanes == 0, inflow, first), jnp.where(lanes == 0, first, second)
+    if b == 0:
+        first, second = roll(first, -1, 1), roll(second, -1, 1)
+        return jnp.where(lanes == 127, second, first), jnp.where(lanes == 127, inflow, second)
+    return first, second
+
+
+def prepare(state, labels, strip, moved, moved_labels):
+    even = (iota(1) & 1) == 0
+    rho, vx, vy, vz, dyy, dxy, dyz, mark = strip
     sign = jnp.where(even, 0.25, -0.25)
-
-    def slots_of(fields, wanted):
-        rho, vx, vy, vz, dyy, dxy, dyz, mark = fields
-        along_x, along_y, along_z = shapes(vx - look_up(table, index_of(mark))), shapes(vy), shapes(vz)
-        part = rho * jnp.where(even, along_y[2], along_y[0])
-        slots = {}
-        for a in wanted:
-            piece = part * along_x[a]
-            for c in range(3):
-                value = piece * along_z[c]
-                if a == 1 and c == 1:
-                    value = value + 0.5 * dyy
-                elif c == 1:
-                    value = value + ((a - 1) * sign) * dxy
-                elif a == 1:
-                    value = value + ((c - 1) * sign) * dyz
-                slots[a, c] = value
-        return slots
-
-    n = 2 * len(X_FIELDS)
-    columns = slots_of([strip[k] for k in range(8)], (0, 1, 2))
-    before = slots_of(row_blocks(left[n], 8), (2,))
-    after = slots_of(row_blocks(right[n], 8), (0,))
-    for c in range(3):
-        columns[2, c] = shift_rows(columns[2, c], 2, before[2, c], None)
-        columns[0, c] = shift_rows(columns[0, c], 0, None, after[0, c])
-    return columns
-
-
-def stream(table, state, labels, columns, left, right, left_marks, right_marks, bottom, top, out, ghost, whole=None):
-    lanes = iota(1)
+    along_y, along_z = shapes(vy), shapes(vz)
+    part = rho * jnp.where(even, along_y[2], along_y[0])
+    outside = [vx] + [part * h for h in along_z] + [0.5 * dyy, sign * dyz, sign * dxy, mark]
+    for z in range(LEVELS):
+        inflow = [roll(block, -16 * z - 8, 1) for block in outside]
+        tiles = []
+        for j in range(2):
+            d = [state[n, j, 8 * z : 8 * z + 8, :] for n in range(10)]
+            mark = labels[j, 8 * z : 8 * z + 8, :].astype(jnp.float32)
+            along_y, along_z = shapes(d[VY]), shapes(d[VZ])
+            rows = [d[RHO] * h for h in along_y]
+            tiles.append((d, mark, rows, along_z))
+        for b in range(3):
+            kept = []
+            for d, mark, rows, along_z in tiles:
+                if b == 1:
+                    terms = [-(d[DXX] + d[DYY] + d[DZZ]), 0.5 * d[DZZ], 0.5 * d[DXX], mark, 0.25 * d[DXZ]]
+                else:
+                    terms = [0.5 * d[DYY], (0.25 * (b - 1)) * d[DYZ], (0.25 * (b - 1)) * d[DXY], mark]
+                kept.append([d[VX]] + [rows[b] * h for h in along_z] + terms)
+            if b != 1:
+                pairs = [shift_columns(*pair) for pair in zip(*kept, [b] * 8, inflow)]
+                kept = list(zip(*pairs))
+            for j, fields in enumerate(kept):
+                for a in range(3):
+                    place = 3 * a + b
+                    chosen = list(fields[:4])
+                    if a == 1:
+                        chosen += [fields[4], fields[5], fields[7]]
+                    elif b == 1:
+                        chosen += [fields[6], (a - 1) * fields[8], fields[7]]
+                    else:
+                        chosen += [(a - 1) * fields[6], None, fields[7]]
+                    for n, value in enumerate(chosen):
+                        if value is None:
+                            continue
+                        value = roll(value, a - 1, 0)
+                        if n == 6:
+                            moved_labels[place, j, z] = value.astype(jnp.int32)
+                        else:
+                            moved[place, n, j, z] = value
+
+
+def first_prepare_kernel(state, labels, domains, moved, moved_labels):
+    strip = [merged_strip(domains[0, n], domains[1, n]) for n in Y_FIELDS + (LABEL,)]
+    prepare(state, labels, strip, moved, moved_labels)
+
+
+def last_prepare_kernel(state, labels, strip, moved, moved_labels):
+    prepare(state, labels, [strip[n] for n in range(8)], moved, moved_labels)
+
+
+def stream(table, moved, moved_labels, left, right, left_marks, right_marks, corners, bottom, top, out, ghost, whole=None):
+    rows = iota(0)
     for side, (source, marks) in enumerate(((left, left_marks), (right, right_marks))):
         a = 2 - 2 * side
-        for j in range(2):
-            fields = [source[2 * n + j] for n in range(len(X_FIELDS))]
-            for (b, c), value in entering(table, fields, marks(j), a).items():
-                ghost[side, 3 * b + c, j] = value
-
+        halves = [
+            entering(table, [source[2 * n + j] for n in range(len(X_FIELDS))], marks(j), a) for j in range(2)
+        ]
+        for b in range(3):
+            for c in range(3):
+                inflow = None if b == 1 else take(corners[side][b, c], 16 * rows + (8 if b == 2 else 7))
+                pair = shift_columns(halves[0][b, c], halves[1][b, c], b, inflow)
+                for j in range(2):
+                    ghost[side, 3 * b + c, j] = pair[j]
     for a in range(3):
         for b in range(3):
             out[9 * a + 3 * b + 2, 0] = bottom[3 * a + b]
             out[9 * a + 3 * b, LEVELS - 1] = top[3 * a + b]
 
     for z in range(LEVELS):
-        tiles = []
         for j in range(2):
-            fields = [state[index, j, 8 * z : 8 * z + 8, :] for index in range(10)]
-            thrust = look_up(table, labels[j, 8 * z : 8 * z + 8, :])
-            parts = [fields[RHO] * h for h in shapes(fields[VX] - thrust)]
-            tiles.append((fields, parts, shapes(fields[VY]), shapes(fields[VZ])))
-        for c in range(3):
-            level = z + c - 1
-            if level < 0 or level >= LEVELS:
-                continue
             for a in range(3):
-                inflow = roll(columns[a, c], -16 * z - 8, 1)
                 for b in range(3):
-                    first, second = (
-                        shift_rows(
-                            slot_value(*tile, a, b, c),
-                            a,
-                            ghost[0, 3 * b + c, j, z : z + 1, :],
-                            ghost[1, 3 * b + c, j, z : z + 1, :],
-                        )
-                        for j, tile in enumerate(tiles)
-                    )
-                    if b == 2:
-                        first, second = roll(first, 1, 1), roll(second, 1, 1)
-                        second = jnp.where(lanes == 0, first, second)
-                        first = jnp.where(lanes == 0, inflow, first)
-                    elif b == 0:
-                        first, second = roll(first, -1, 1), roll(second, -1, 1)
-                        first = jnp.where(lanes == 127, second, first)
-                        second = jnp.where(lanes == 127, inflow, second)
-                    out[9 * a + 3 * b + c, level, :, 0:128] = first
-                    out[9 * a + 3 * b + c, level, :, 128:256] = second
+                    place = 3 * a + b
+                    speed = moved[place, 0, j, z] - look_up(table, moved_labels[place, j, z])
+                    h = shapes(speed)[a]
+                    for c in range(3):
+                        level = z + c - 1
+                        if level < 0 or level >= LEVELS:
+                            continue
+                        value = moved[place, 1 + c, j, z] * h
+                        if c == 1:
+                            value = value + moved[place, 4, j, z]
+                        elif a == 1 and b == 1:
+                            value = value + moved[place, 5, j, z]
+                        elif a == 1 or b == 1:
+                            value = value + (c - 1) * moved[place, 5, j, z]
+                        if a == 2:
+                            value = jnp.where(rows == 0, ghost[0, 3 * b + c, j, z : z + 1, :], value)
+                        elif a == 0:
+                            value = jnp.where(rows == 7, ghost[1, 3 * b + c, j, z : z + 1, :], value)
+                        out[9 * a + 3 * b + c, level, :, 128 * j : 128 * j + 128] = value
         if whole and z:
             whole(z - 1)
     if whole:
@@ -482,28 +526,32 @@
 
 
 def middle_kernel(
-    state, labels, domains, column_sums, beside, starts, found, found_beside, left, right, bottom, top,
+    moved, moved_labels, domains, column_sums, beside, starts, found, found_beside, left, right, bottom, top,
     new_state, to_right, to_left, strip, counts, sums_out, f_ref, ghost, speeds,
 ):
     lanes = iota(1)
-    even = (lanes & 1) == 0
     last = 2 * len(X_FIELDS) + 4
     totals = column_sums[...] + left[last] + right[last]
     seen = roll(totals, 64, 1)
     counts[...] = seen
     table = disk_table(totals, seen)
 
-    outside, kept, columns = [], [], [{}, {}]
+    outside, kept, corners = [], [], [{}, {}]
     for side in range(2):
-        columns[side], new = step_domain(table, side, domains, left, right, beside)
+        outer, new = step_domain(table, side, domains, left, right, beside)
         ux, fields = relax(low_moments(lambda a, b, c: new[a, b, c]))
         outside.append(ux)
         kept.append([fields[n] for n in Y_FIELDS] + [domains[side, LABEL]])
-    strips = [jnp.where(even, roll(one, 1, 1), roll(other, -1, 1)) for one, other in zip(*kept)]
+        b = 2 - 2 * side
+        for c in range(3):
+            for row, a in ((0, 2), (1, 0)):
+                corners[row][b, c] = roll(outer[a][b, c], b - 1, 1)
+    strips = [merged_strip(one, other) for one, other in zip(*kept)]
     for n, block in enumerate(strips):
         strip[n] = block
-    merged = {key: jnp.where(even, columns[0][key], columns[1][key]) for key in columns[0]}
-    stream(table, state, labels, merged, left, right, marks_of(left), marks_of(right), bottom, top, f_ref, ghost)
+    stream(
+        table, moved, moved_labels, left, right, marks_of(left), marks_of(right), corners, bottom, top, f_ref, ghost
+    )
 
     def f(z, j, a, b, c):
         return f_ref[9 * a + 3 * b + c, z, :, 128 * j : 128 * j + 128]
@@ -525,15 +573,18 @@
 
 
 def last_kernel(
-    state, labels, strip, sums, counts, left, right, old_left, old_right, bottom, top, out_hbm, out, ghost, gone
+    moved, moved_labels, sums, counts, left, right, old_left, old_right, bottom, top, out_hbm, out, ghost, gone
 ):
     last = 2 * len(X_FIELDS) + 1
     totals = sums[...] + left[last] + right[last]
     table = disk_table(totals, counts[...])
-    columns = last_columns(table, strip, left, right)
+    corners = [
+        {(b, c): value for c, value in enumerate(strip_corners(table, message, a)) for b in (0, 2)}
+        for message, a in ((left, 2), (right, 0))
+    ]
     copies = [pltpu.make_async_copy(out.at[:, z], out_hbm.at[:, z], gone.at[z]) for z in range(LEVELS)]
     stream(
-        table, state, labels, columns, left, right, marks_of(old_left), marks_of(old_right), bottom, top, out, ghost,
+        table, moved, moved_labels, left, right, marks_of(old_left), marks_of(old_right), corners, bottom, top, out, ghost,
         whole=lambda z: copies[z].start(),
     )
     for copy in copies:
@@ -609,19 +660,22 @@
         (labels, domains),
         (((2, 8, 128), jnp.int32), blocks(SPAN, 2, LEVELS), blocks(SPAN, LEVELS)),
     )
+    shifted = (blocks(9, 6, 2, LEVELS), ((9, 2, LEVELS, 8, 128), jnp.int32))
+    moved, moved_labels = call(first_prepare_kernel, (state, labels, domains), shifted)
     state, to_right, to_left, strip, counts, sums = call(
         middle_kernel,
         (
-            state, labels, domains, column_sums, beside, starts, found, found_beside,
+            moved, moved_labels, domains, column_sums, beside, starts, found, found_beside,
             old_left, old_right, bottom_in, top_in,
         ),
         (state_shape, blocks(n + 2), blocks(n + 2), blocks(8), one, one),
         (whole, ghost, blocks(2, LEVELS)),
     )
     left, right = both_ways(to_right, to_left, "gx")
+    moved, moved_labels = call(last_prepare_kernel, (state, labels, strip), shifted)
     (out,) = call(
         last_kernel,
-        (state, labels, strip, sums, counts, left, right, old_left, old_right, bottom_in, top_in),
+        (moved, moved_labels, sums, counts, left, right, old_left, old_right, bottom_in, top_in),
         (whole,),
         (whole, ghost),
         out_hbm=1,

time: 29.9 us -> 29.2 us (0.977)
  the two profiles are of different devices: /device:TPU:98 before, /device:TPU:102 now
where the time goes in v4:
time: 29.2 us; the launch traced here: 29.1 us
  waiting for transfers between devices  10.7 us (37%)
  starting transfers between devices  9.62 us (33%)
  Pallas kernels  8.76 us (30%)
    pallas_call x8, Pallas kernels, call(): pl.pallas_call(kernel, out_shape=[jax.ShapeDtypeStruct(shape, dtype) for...  8.76 us
    ppermute x2, waiting for transfers between devices, both_ways(): lax.ppermute(downward, axis, [((i + 1) % count, i) for i in range(count)])  6.75 us
    ppermute x1, starting transfers between devices, swapped(): lax.ppermute(odd, axis, pairs(1))  3.96 us
    ppermute x2, starting transfers between devices, both_ways(): lax.ppermute(upward, axis, [(i, (i + 1) % count) for i in range(count)])  3.56 us
    ppermute x1, waiting for transfers between devices, swapped(): lax.ppermute(odd, axis, pairs(1))  2.04 us
    ppermute x2, starting transfers between devices, both_ways(): lax.ppermute(downward, axis, [((i + 1) % count, i) for i in range(count)])  2.02 us
    ppermute x2, waiting for transfers between devices, both_ways(): lax.ppermute(upward, axis, [(i, (i + 1) % count) for i in range(count)])  1.89 us
  transfers between devices with their start and end apart: 6, of which 5 were waited for; matrix products, arithmetic and copies ran while one was open for 0% of the time, Pallas kernels for 12%

profile of v4, /device:TPU:102, one launch (start us, length us, event | category | flops | bytes accessed | tf_op | source)
XLA Modules:
  0.0 29.1 jit_solution(2805080408147746378)
XLA Ops:
  0.0 0.0 copy-start.1
  0.0 0.0 copy-start
  0.0 2.0 %shard_map.55 = (f32[11,2,64,128]{3,2,1,0:T(8,128)S(1)}, s32[2,64,128]{2,1,0:T(8,128)S(1)}, f32[12,8,128]{2,1,0:T(8,128)S(1)}, f32[9,8,128]{2,1,0:T(8,128)S(1)}, f32[9,8,128]{2,1,0:T(8,128)S(1)}) custom-call(f32[27,8,8,256]{3,2,1,0:T(8,128)} %f_hbm.1, s32[8,8,256]{2,1,0:T(8,128)} %mask_hbm.1, s32[8,8,256]{2,1,0:T(8,128)} %rotor_hbm.1, f32[9,8,256]{2,1,0:T(8,128)} %bottom.3, ...), custom_call_target="tpu_custom_call" | custom-call | tf_op jit(solution)/shard_map/pallas_call | solution.py:600
  2.0 0.1 collective-permute-start
  2.1 4.0 %collective-permute-start.1 = (f32[9,8,128]{2,1,0:T(8,128)S(1)}, f32[9,8,128]{2,1,0:T(8,128)S(1)}, u32[]{:S(2)}, u32[]{:S(2)}) collective-permute-start(f32[9,8,128]{2,1,0:T(8,128)S(1)} %get-tuple-element.32), channel_id=1, source_target_pairs={{1,2},{3,4},{5,6},{7,8},{9,10},{11,12},{13,14},{15,0},{2,1},{4,3},... | collective-permute-start | bytes 110600 | tf_op jit(solution)/shard_map/ppermute | solution.py:626
  6.1 1.1 %shard_map.56.own_sums = f32[8,128]{1,0:T(8,128)S(1)} custom-call(f32[11,2,64,128]{3,2,1,0:T(8,128)S(1)} %get-tuple-element.28.state, s32[2,64,128]{2,1,0:T(8,128)S(1)} %get-tuple-element.29.labels), custom_call_target="tpu_custom_call" | custom-call | tf_op jit(solution)/shard_map/pallas_call | solution.py:600
  7.2 0.0 collective-permute-done.even
  7.2 2.0 %collective-permute-done.1.odd = f32[9,8,128]{2,1,0:T(8,128)S(1)} collective-permute-done((f32[9,8,128]{2,1,0:T(8,128)S(1)}, f32[9,8,128]{2,1,0:T(8,128)S(1)}, u32[]{:S(2)}, u32[]{:S(2)}) %collective-permute-start.1) | collective-permute-done | bytes 36896 | tf_op jit(solution)/shard_map/ppermute | solution.py:626
  9.2 0.4 %shard_map.57 = (f32[2,12,8,128]{3,2,1,0:T(8,128)S(1)}, f32[19,8,128]{2,1,0:T(8,128)S(1)}, f32[19,8,128]{2,1,0:T(8,128)S(1)}, f32[8,128]{1,0:T(8,128)S(1)}, f32[2,2,8,128]{3,2,1,0:T(8,128)S(1)}) custom-call(f32[11,2,64,128]{3,2,1,0:T(8,128)S(1)} %get-tuple-element.28.state, s32[2,64,128]{2,1,0:T(8,128)S(1)} %get-tuple-element.29.labels, ...), custom_call_target="tpu_custom_call" | custom-call | tf_op jit(solution)/shard_map/pallas_call | solution.py:600
  9.7 3.5 %collective-permute-start.2 = (f32[19,8,128]{2,1,0:T(8,128)S(1)}, f32[19,8,128]{2,1,0:T(8,128)S(1)}, u32[]{:S(2)}, u32[]{:S(2)}) collective-permute-start(f32[19,8,128]{2,1,0:T(8,128)S(1)} %get-tuple-element.41), channel_id=1, source_target_pairs={{0,16},{16,32},{32,48},{48,64},{64,80},{80,96},{96,112},{112,128},... | collective-permute-start | bytes 233480 | tf_op jit(solution)/shard_map/ppermute | solution.py:614
  13.1 0.0 collective-permute-start.3
  13.1 1.3 %shard_map.59 = (s32[2,8,128]{2,1,0:T(8,128)S(1)}, f32[5,2,8,8,128]{4,3,2,1,0:T(8,128)S(1)}, f32[5,8,8,128]{3,2,1,0:T(8,128)S(1)}) custom-call(s32[2,64,128]{2,1,0:T(8,128)S(1)} %get-tuple-element.29.labels, f32[2,12,8,128]{3,2,1,0:T(8,128)S(1)} %get-tuple-element.33.domains), custom_call_target="tpu_custom_call" | custom-call | tf_op jit(solution)/shard_map/pallas_call | solution.py:600
  14.4 0.5 %shard_map.58 = (f32[9,6,2,8,8,128]{5,4,3,2,1,0:T(8,128)S(1)}, s32[9,2,8,8,128]{4,3,2,1,0:T(8,128)S(1)}) custom-call(f32[11,2,64,128]{3,2,1,0:T(8,128)S(1)} %get-tuple-element.28.state, s32[2,64,128]{2,1,0:T(8,128)S(1)} %get-tuple-element.29.labels, f32[2,12,8,128]{3,2,1,0:T(8,128)S(1)} %get-tuple-element.33.domains), custom_call_target="tpu_custom_call" | custom-call | tf_op jit(solution)/shard_map/pallas_call | solution.py:600
  15.0 0.2 collective-permute-done.2.left.old_left
  15.1 4.6 %collective-permute-done.3.right.old_right = f32[19,8,128]{2,1,0:T(8,128)S(1)} collective-permute-done((f32[19,8,128]{2,1,0:T(8,128)S(1)}, f32[19,8,128]{2,1,0:T(8,128)S(1)}, u32[]{:S(2)}, u32[]{:S(2)}) %collective-permute-start.3) | collective-permute-done | bytes 77856 | tf_op jit(solution)/shard_map/ppermute | solution.py:615
  19.7 0.0 copy-done.1
  19.7 0.0 copy-done
  19.7 1.3 %shard_map.60 = (f32[10,2,64,128]{3,2,1,0:T(8,128)S(1)}, f32[16,8,128]{2,1,0:T(8,128)S(1)}, f32[16,8,128]{2,1,0:T(8,128)S(1)}, f32[8,8,128]{2,1,0:T(8,128)S(1)},...) custom-call(f32[9,6,2,8,8,128]{5,4,3,2,1,0:T(8,128)S(1)} %get-tuple-element.34.moved, ...), custom_call_target="tpu_custom_call" | custom-call | tf_op jit(solution)/shard_map/pallas_call | solution.py:600
  21.0 0.1 collective-permute-start.4
  21.1 2.0 %collective-permute-start.5 = (f32[16,8,128]{2,1,0:T(8,128)S(1)}, f32[16,8,128]{2,1,0:T(8,128)S(1)}, u32[]{:S(2)}, u32[]{:S(2)}) collective-permute-start(f32[16,8,128]{2,1,0:T(8,128)S(1)} %get-tuple-element.50), channel_id=1, source_target_pairs={{16,0},{32,16},{48,32},{64,48},{80,64},{96,80},{112,96},{128,112},... | collective-permute-start | bytes 196616 | tf_op jit(solution)/shard_map/ppermute | solution.py:615
  23.1 0.5 %shard_map.61 = (f32[9,6,2,8,8,128]{5,4,3,2,1,0:T(8,128)S(1)}, s32[9,2,8,8,128]{4,3,2,1,0:T(8,128)S(1)}) custom-call(f32[10,2,64,128]{3,2,1,0:T(8,128)S(1)} %get-tuple-element.43.state, s32[2,64,128]{2,1,0:T(8,128)S(1)} %get-tuple-element.29.labels, f32[8,8,128]{2,1,0:T(8,128)S(1)} %get-tuple-element.44.strip), custom_call_target="tpu_custom_call" | custom-call | tf_op jit(solution)/shard_map/pallas_call | solution.py:600
  23.7 1.7 %collective-permute-done.4.left = f32[16,8,128]{2,1,0:T(8,128)S(1)} collective-permute-done((f32[16,8,128]{2,1,0:T(8,128)S(1)}, f32[16,8,128]{2,1,0:T(8,128)S(1)}, u32[]{:S(2)}, u32[]{:S(2)}) %collective-permute-start.4) | collective-permute-done | bytes 65568 | tf_op jit(solution)/shard_map/ppermute | solution.py:614
  25.4 2.2 %collective-permute-done.5.right = f32[16,8,128]{2,1,0:T(8,128)S(1)} collective-permute-done((f32[16,8,128]{2,1,0:T(8,128)S(1)}, f32[16,8,128]{2,1,0:T(8,128)S(1)}, u32[]{:S(2)}, u32[]{:S(2)}) %collective-permute-start.5) | collective-permute-done | bytes 65568 | tf_op jit(solution)/shard_map/ppermute | solution.py:615
  27.6 1.6 %shard_map.62 = f32[27,8,8,256]{3,2,1,0:T(8,128)} custom-call(f32[9,6,2,8,8,128]{5,4,3,2,1,0:T(8,128)S(1)} %get-tuple-element.45.moved, s32[9,2,8,8,128]{4,3,2,1,0:T(8,128)S(1)} %get-tuple-element.46.moved_labels, f32[8,128]{1,0:T(8,128)S(1)} %get-tuple-element.47.sums, f32[8,128]{1,0:T(8,128)S(1)} %get-tuple-element.48.counts, ...), custom_call_target="tpu_custom_call" | custom-call | tf_op jit(solution)/shard_map/pallas_call | solution.py:600
Async XLA Ops:
  0.0 19.7 %copy-start.1 = (f32[9,8,256]{2,1,0:T(8,128)S(1)}, f32[9,8,256]{2,1,0:T(8,128)}, u32[]{:S(2)}) copy-start(f32[9,8,256]{2,1,0:T(8,128)} %top.3) | copy-start | bytes 221188
  0.0 19.7 %copy-start = (f32[9,8,256]{2,1,0:T(8,128)S(1)}, f32[9,8,256]{2,1,0:T(8,128)}, u32[]{:S(2)}) copy-start(f32[9,8,256]{2,1,0:T(8,128)} %bottom.3) | copy-start | bytes 221188
  2.0 5.1 %collective-permute-start = (f32[9,8,128]{2,1,0:T(8,128)S(1)}, f32[9,8,128]{2,1,0:T(8,128)S(1)}, u32[]{:S(2)}, u32[]{:S(2)}) collective-permute-start(f32[9,8,128]{2,1,0:T(8,128)S(1)} %get-tuple-element.31), channel_id=1, source_target_pairs={{0,1},{2,3},{4,5},{6,7},{8,9},{10,11},{12,13},{14,15},{1,0},{3,2},... | collective-permute-start | bytes 110600 | tf_op jit(solution)/shard_map/ppermute | solution.py:626
  2.1 7.1 %collective-permute-start.1 = (f32[9,8,128]{2,1,0:T(8,128)S(1)}, f32[9,8,128]{2,1,0:T(8,128)S(1)}, u32[]{:S(2)}, u32[]{:S(2)}) collective-permute-start(f32[9,8,128]{2,1,0:T(8,128)S(1)} %get-tuple-element.32), channel_id=1, source_target_pairs={{1,2},{3,4},{5,6},{7,8},{9,10},{11,12},{13,14},{15,0},{2,1},{4,3},... | collective-permute-start | bytes 110600 | tf_op jit(solution)/shard_map/ppermute | solution.py:626
  9.7 5.5 %collective-permute-start.2 = (f32[19,8,128]{2,1,0:T(8,128)S(1)}, f32[19,8,128]{2,1,0:T(8,128)S(1)}, u32[]{:S(2)}, u32[]{:S(2)}) collective-permute-start(f32[19,8,128]{2,1,0:T(8,128)S(1)} %get-tuple-element.41), channel_id=1, source_target_pairs={{0,16},{16,32},{32,48},{48,64},{64,80},{80,96},{96,112},{112,128},... | collective-permute-start | bytes 233480 | tf_op jit(solution)/shard_map/ppermute | solution.py:614
  13.1 6.6 %collective-permute-start.3 = (f32[19,8,128]{2,1,0:T(8,128)S(1)}, f32[19,8,128]{2,1,0:T(8,128)S(1)}, u32[]{:S(2)}, u32[]{:S(2)}) collective-permute-start(f32[19,8,128]{2,1,0:T(8,128)S(1)} %get-tuple-element.42), channel_id=1, source_target_pairs={{16,0},{32,16},{48,32},{64,48},{80,64},{96,80},{112,96},{128,112},... | collective-permute-start | bytes 233480 | tf_op jit(solution)/shard_map/ppermute | solution.py:615
  21.0 4.3 %collective-permute-start.4 = (f32[16,8,128]{2,1,0:T(8,128)S(1)}, f32[16,8,128]{2,1,0:T(8,128)S(1)}, u32[]{:S(2)}, u32[]{:S(2)}) collective-permute-start(f32[16,8,128]{2,1,0:T(8,128)S(1)} %get-tuple-element.49), channel_id=1, source_target_pairs={{0,16},{16,32},{32,48},{48,64},{64,80},{80,96},{96,112},{112,128},... | collective-permute-start | bytes 196616 | tf_op jit(solution)/shard_map/ppermute | solution.py:614
  21.1 6.5 %collective-permute-start.5 = (f32[16,8,128]{2,1,0:T(8,128)S(1)}, f32[16,8,128]{2,1,0:T(8,128)S(1)}, u32[]{:S(2)}, u32[]{:S(2)}) collective-permute-start(f32[16,8,128]{2,1,0:T(8,128)S(1)} %get-tuple-element.50), channel_id=1, source_target_pairs={{16,0},{32,16},{48,32},{64,48},{80,64},{96,80},{112,96},{128,112},... | collective-permute-start | bytes 196616 | tf_op jit(solution)/shard_map/ppermute | solution.py:615

commit v5 on v4

--- a/solution.py
+++ b/solution.py
@@ -240,12 +240,8 @@
     inner_label, inner_speed = pairs[LABEL][1], pairs[LABEL + 1][1]
     for n, block in enumerate(blocks):
         edges[n] = block
-    upward_first = lax.rem(lax.axis_index("gy"), 2) == 0
     low = (lanes & 8) == 0
-
-    def send(n, upward, downward):
-        to_even[n] = jnp.where(upward_first, upward, downward)
-        to_odd[n] = jnp.where(upward_first, downward, upward)
+    send = Paired("gy", to_even, to_odd).put
 
     for n in range(6):
         one, other = blocks[2 * n], blocks[2 * n + 1]
@@ -269,6 +265,29 @@
         send(place, upward, downward)
 
 
+class Paired:
+    def __init__(self, axis, even, odd):
+        self.next_first = lax.rem(lax.axis_index(axis), 2) == 0
+        self.refs = (even, odd)
+
+    def put(self, n, to_next, to_previous):
+        even, odd = self.refs
+        even[n] = jnp.where(self.next_first, to_next, to_previous)
+        odd[n] = jnp.where(self.next_first, to_previous, to_next)
+
+    def received(self):
+        even, odd = self.refs
+        return Chosen(self.next_first, odd, even), Chosen(self.next_first, even, odd)
+
+
+class Chosen:
+    def __init__(self, flag, one, other):
+        self.flag, self.one, self.other = flag, one, other
+
+    def __getitem__(self, n):
+        return jnp.where(self.flag, self.one[n], self.other[n])
+
+
 def rows_of(blocks, row):
     rows = iota(0)
     out = jnp.broadcast_to(blocks[0][row : row + 1], (8, 128))
@@ -277,19 +296,17 @@
     return out
 
 
-def edge_rows(state, target, row):
+def edge_rows(state, sent):
     slot = 0
     for index in X_FIELDS:
         for j in range(2):
-            target[slot] = state[index, j, pl.ds(row, 8, stride=8), :]
+            sent.put(slot, *(state[index, j, pl.ds(row, 8, stride=8), :] for row in (7, 0)))
             slot += 1
     return slot
 
 
-def relay_kernel(state, labels, edges, own_sums, even, odd, domains, to_right, to_left, column_sums, beside):
-    upward_first = lax.rem(lax.axis_index("gy"), 2) == 0
-    below = [jnp.where(upward_first, odd[n], even[n]) for n in range(9)]
-    above = [jnp.where(upward_first, even[n], odd[n]) for n in range(9)]
+def relay_kernel(state, labels, edges, own_sums, even, odd, domains, to_even, to_odd, column_sums, beside):
+    below, above = ([chosen[n] for n in range(9)] for chosen in Paired("gy", even, odd).received())
     for side, message in enumerate((below, above)):
         for n in range(2):
             beside[side, n] = message[7 + n]
@@ -309,13 +326,14 @@
         [beside_tile(domains, LABEL + 1), jnp.where(column >= 8, below[6], above[6])],
     )
     column_sums[...] = sums
-    for target, row in ((to_right, 7), (to_left, 0)):
-        slot = edge_rows(state, target, row)
-        for j in range(2):
-            target[slot + j] = labels[j, pl.ds(row, 8, stride=8), :].astype(jnp.float32)
-        for side in range(2):
-            target[slot + 2 + side] = rows_of([domains[side, n] for n in X_FIELDS + (LABEL,)], row)
-        target[slot + 4] = sums
+    sent = Paired("gx", to_even, to_odd)
+    slot = edge_rows(state, sent)
+    for j in range(2):
+        sent.put(slot + j, *(labels[j, pl.ds(row, 8, stride=8), :].astype(jnp.float32) for row in (7, 0)))
+    for side in range(2):
+        blocks = [domains[side, n] for n in X_FIELDS + (LABEL,)]
+        sent.put(slot + 2 + side, rows_of(blocks, 7), rows_of(blocks, 0))
+    sent.put(slot + 4, sums, sums)
 
 
 look_up = take
@@ -526,10 +544,11 @@
 
 
 def middle_kernel(
-    moved, moved_labels, domains, column_sums, beside, starts, found, found_beside, left, right, bottom, top,
-    new_state, to_right, to_left, strip, counts, sums_out, f_ref, ghost, speeds,
+    moved, moved_labels, domains, column_sums, beside, starts, found, found_beside, even, odd, bottom, top,
+    new_state, to_even, to_odd, strip, counts, sums_out, f_ref, ghost, speeds,
 ):
     lanes = iota(1)
+    left, right = Paired("gx", even, odd).received()
     last = 2 * len(X_FIELDS) + 4
     totals = column_sums[...] + left[last] + right[last]
     seen = roll(totals, 64, 1)
@@ -566,15 +585,17 @@
         starts, found, found_beside,
     )
     sums_out[...] = sums
-    for target, row in ((to_right, 7), (to_left, 0)):
-        slot = edge_rows(new_state, target, row)
-        target[slot] = rows_of(strips, row)
-        target[slot + 1] = sums
+    sent = Paired("gx", to_even, to_odd)
+    slot = edge_rows(new_state, sent)
+    sent.put(slot, rows_of(strips, 7), rows_of(strips, 0))
+    sent.put(slot + 1, sums, sums)
 
 
 def last_kernel(
-    moved, moved_labels, sums, counts, left, right, old_left, old_right, bottom, top, out_hbm, out, ghost, gone
+    moved, moved_labels, sums, counts, even, odd, old_even, old_odd, bottom, top, out_hbm, out, ghost, gone
 ):
+    left, right = Paired("gx", even, odd).received()
+    old_left, old_right = Paired("gx", old_even, old_odd).received()
     last = 2 * len(X_FIELDS) + 1
     totals = sums[...] + left[last] + right[last]
     table = disk_table(totals, counts[...])
@@ -608,14 +629,6 @@
     )(*inputs)
 
 
-def both_ways(upward, downward, axis):
-    count = lax.axis_size(axis)
-    return (
-        lax.ppermute(upward, axis, [(i, (i + 1) % count) for i in range(count)]),
-        lax.ppermute(downward, axis, [((i + 1) % count, i) for i in range(count)]),
-    )
-
-
 def swapped(even, odd, axis):
     count = lax.axis_size(axis)
 
@@ -649,12 +662,12 @@
     )
     even, odd = swapped(to_even, to_odd, "gy")
     (own_sums,) = call(sums_kernel, (state, labels), (one,))
-    domains, to_right, to_left, column_sums, beside = call(
+    domains, to_even, to_odd, column_sums, beside = call(
         relay_kernel,
         (state, labels, edges, own_sums, even, odd),
         (blocks(2, 12), blocks(n + 5), blocks(n + 5), one, blocks(2, 2)),
     )
-    old_left, old_right = both_ways(to_right, to_left, "gx")
+    old_even, old_odd = swapped(to_even, to_odd, "gx")
     starts, found, found_beside = call(
         places_kernel,
         (labels, domains),
@@ -662,20 +675,20 @@
     )
     shifted = (blocks(9, 6, 2, LEVELS), ((9, 2, LEVELS, 8, 128), jnp.int32))
     moved, moved_labels = call(first_prepare_kernel, (state, labels, domains), shifted)
-    state, to_right, to_left, strip, counts, sums = call(
+    state, to_even, to_odd, strip, counts, sums = call(
         middle_kernel,
         (
             moved, moved_labels, domains, column_sums, beside, starts, found, found_beside,
-            old_left, old_right, bottom_in, top_in,
+            old_even, old_odd, bottom_in, top_in,
         ),
         (state_shape, blocks(n + 2), blocks(n + 2), blocks(8), one, one),
         (whole, ghost, blocks(2, LEVELS)),
     )
-    left, right = both_ways(to_right, to_left, "gx")
+    even, odd = swapped(to_even, to_odd, "gx")
     moved, moved_labels = call(last_prepare_kernel, (state, labels, strip), shifted)
     (out,) = call(
         last_kernel,
-        (moved, moved_labels, sums, counts, left, right, old_left, old_right, bottom_in, top_in),
+        (moved, moved_labels, sums, counts, even, odd, old_even, old_odd, bottom_in, top_in),
         (whole,),
         (whole, ghost),
         out_hbm=1,

time: 29.2 us -> 29.1 us (level)
  the two profiles are of different devices: /device:TPU:102 before, /device:TPU:4 now
where the time goes in v5:
time: 29.1 us; the launch traced here: 29 us
  starting transfers between devices  14.9 us (51%)
  Pallas kernels  8.78 us (30%)
  waiting for transfers between devices  5.2 us (18%)
    ppermute x3, starting transfers between devices, swapped(): lax.ppermute(odd, axis, pairs(1))  13.4 us
    pallas_call x8, Pallas kernels, call(): pl.pallas_call(kernel, out_shape=[jax.ShapeDtypeStruct(shape, dtype) for...  8.78 us
    ppermute x3, waiting for transfers between devices, swapped(): lax.ppermute(odd, axis, pairs(1))  5.2 us
    ppermute x3, starting transfers between devices, swapped(): lax.ppermute(even, axis, pairs(0))  1.47 us
  transfers between devices with their start and end apart: 6, of which 3 were waited for; matrix products, arithmetic and copies ran while one was open for 0% of the time, Pallas kernels for 12%

profile of v5, /device:TPU:4, one launch (start us, length us, event | category | flops | bytes accessed | tf_op | source)
XLA Modules:
  0.0 29.0 jit_solution(15651991920771438000)
XLA Ops:
  0.0 0.0 copy-start.1
  0.0 0.0 copy-start
  0.0 2.0 %shard_map.55 = (f32[11,2,64,128]{3,2,1,0:T(8,128)S(1)}, s32[2,64,128]{2,1,0:T(8,128)S(1)}, f32[12,8,128]{2,1,0:T(8,128)S(1)}, f32[9,8,128]{2,1,0:T(8,128)S(1)}, f32[9,8,128]{2,1,0:T(8,128)S(1)}) custom-call(f32[27,8,8,256]{3,2,1,0:T(8,128)} %f_hbm.1, s32[8,8,256]{2,1,0:T(8,128)} %mask_hbm.1, s32[8,8,256]{2,1,0:T(8,128)} %rotor_hbm.1, f32[9,8,256]{2,1,0:T(8,128)} %bottom.3, ...), custom_call_target="tpu_custom_call" | custom-call | tf_op jit(solution)/shard_map/pallas_call | solution.py:621
  2.0 0.1 collective-permute-start
  2.1 3.1 %collective-permute-start.1 = (f32[9,8,128]{2,1,0:T(8,128)S(1)}, f32[9,8,128]{2,1,0:T(8,128)S(1)}, u32[]{:S(2)}, u32[]{:S(2)}) collective-permute-start(f32[9,8,128]{2,1,0:T(8,128)S(1)} %get-tuple-element.32), channel_id=1, source_target_pairs={{1,2},{3,4},{5,6},{7,8},{9,10},{11,12},{13,14},{15,0},{2,1},{4,3},... | collective-permute-start | bytes 110600 | tf_op jit(solution)/shard_map/ppermute | solution.py:639
  5.2 1.1 %shard_map.56.own_sums = f32[8,128]{1,0:T(8,128)S(1)} custom-call(f32[11,2,64,128]{3,2,1,0:T(8,128)S(1)} %get-tuple-element.28.state, s32[2,64,128]{2,1,0:T(8,128)S(1)} %get-tuple-element.29.labels), custom_call_target="tpu_custom_call" | custom-call | tf_op jit(solution)/shard_map/pallas_call | solution.py:621
  6.3 0.0 collective-permute-done.even
  6.3 2.9 %collective-permute-done.1.odd = f32[9,8,128]{2,1,0:T(8,128)S(1)} collective-permute-done((f32[9,8,128]{2,1,0:T(8,128)S(1)}, f32[9,8,128]{2,1,0:T(8,128)S(1)}, u32[]{:S(2)}, u32[]{:S(2)}) %collective-permute-start.1) | collective-permute-done | bytes 36896 | tf_op jit(solution)/shard_map/ppermute | solution.py:639
  9.2 0.4 %shard_map.57 = (f32[2,12,8,128]{3,2,1,0:T(8,128)S(1)}, f32[19,8,128]{2,1,0:T(8,128)S(1)}, f32[19,8,128]{2,1,0:T(8,128)S(1)}, f32[8,128]{1,0:T(8,128)S(1)}, f32[2,2,8,128]{3,2,1,0:T(8,128)S(1)}) custom-call(f32[11,2,64,128]{3,2,1,0:T(8,128)S(1)} %get-tuple-element.28.state, s32[2,64,128]{2,1,0:T(8,128)S(1)} %get-tuple-element.29.labels, ...), custom_call_target="tpu_custom_call" | custom-call | tf_op jit(solution)/shard_map/pallas_call | solution.py:621
  9.7 1.3 %collective-permute-start.2 = (f32[19,8,128]{2,1,0:T(8,128)S(1)}, f32[19,8,128]{2,1,0:T(8,128)S(1)}, u32[]{:S(2)}, u32[]{:S(2)}) collective-permute-start(f32[19,8,128]{2,1,0:T(8,128)S(1)} %get-tuple-element.41), channel_id=1, source_target_pairs={{0,16},{32,48},{64,80},{96,112},{128,144},{160,176},{192,208},{224... | collective-permute-start | bytes 233480 | tf_op jit(solution)/shard_map/ppermute | solution.py:639
  10.9 6.1 %collective-permute-start.3 = (f32[19,8,128]{2,1,0:T(8,128)S(1)}, f32[19,8,128]{2,1,0:T(8,128)S(1)}, u32[]{:S(2)}, u32[]{:S(2)}) collective-permute-start(f32[19,8,128]{2,1,0:T(8,128)S(1)} %get-tuple-element.42), channel_id=1, source_target_pairs={{16,32},{48,64},{80,96},{112,128},{144,160},{176,192},{208,224},{2... | collective-permute-start | bytes 233480 | tf_op jit(solution)/shard_map/ppermute | solution.py:639
  17.1 1.3 %shard_map.59 = (s32[2,8,128]{2,1,0:T(8,128)S(1)}, f32[5,2,8,8,128]{4,3,2,1,0:T(8,128)S(1)}, f32[5,8,8,128]{3,2,1,0:T(8,128)S(1)}) custom-call(s32[2,64,128]{2,1,0:T(8,128)S(1)} %get-tuple-element.29.labels, f32[2,12,8,128]{3,2,1,0:T(8,128)S(1)} %get-tuple-element.33.domains), custom_call_target="tpu_custom_call" | custom-call | tf_op jit(solution)/shard_map/pallas_call | solution.py:621
  18.4 0.5 %shard_map.58 = (f32[9,6,2,8,8,128]{5,4,3,2,1,0:T(8,128)S(1)}, s32[9,2,8,8,128]{4,3,2,1,0:T(8,128)S(1)}) custom-call(f32[11,2,64,128]{3,2,1,0:T(8,128)S(1)} %get-tuple-element.28.state, s32[2,64,128]{2,1,0:T(8,128)S(1)} %get-tuple-element.29.labels, f32[2,12,8,128]{3,2,1,0:T(8,128)S(1)} %get-tuple-element.33.domains), custom_call_target="tpu_custom_call" | custom-call | tf_op jit(solution)/shard_map/pallas_call | solution.py:621
  18.9 0.0 collective-permute-done.2.even.old_even
  18.9 0.5 %collective-permute-done.3.odd.old_odd = f32[19,8,128]{2,1,0:T(8,128)S(1)} collective-permute-done((f32[19,8,128]{2,1,0:T(8,128)S(1)}, f32[19,8,128]{2,1,0:T(8,128)S(1)}, u32[]{:S(2)}, u32[]{:S(2)}) %collective-permute-start.3) | collective-permute-done | bytes 77856 | tf_op jit(solution)/shard_map/ppermute | solution.py:639
  19.5 0.0 copy-done.1
  19.5 0.0 copy-done
  19.5 1.3 %shard_map.60 = (f32[10,2,64,128]{3,2,1,0:T(8,128)S(1)}, f32[16,8,128]{2,1,0:T(8,128)S(1)}, f32[16,8,128]{2,1,0:T(8,128)S(1)}, f32[8,8,128]{2,1,0:T(8,128)S(1)},...) custom-call(f32[9,6,2,8,8,128]{5,4,3,2,1,0:T(8,128)S(1)} %get-tuple-element.34.moved, ...), custom_call_target="tpu_custom_call" | custom-call | tf_op jit(solution)/shard_map/pallas_call | solution.py:621
  20.8 0.1 collective-permute-start.4
  20.9 4.3 %collective-permute-start.5 = (f32[16,8,128]{2,1,0:T(8,128)S(1)}, f32[16,8,128]{2,1,0:T(8,128)S(1)}, u32[]{:S(2)}, u32[]{:S(2)}) collective-permute-start(f32[16,8,128]{2,1,0:T(8,128)S(1)} %get-tuple-element.50), channel_id=1, source_target_pairs={{16,32},{48,64},{80,96},{112,128},{144,160},{176,192},{208,224},{2... | collective-permute-start | bytes 196616 | tf_op jit(solution)/shard_map/ppermute | solution.py:639
  25.2 0.5 %shard_map.61 = (f32[9,6,2,8,8,128]{5,4,3,2,1,0:T(8,128)S(1)}, s32[9,2,8,8,128]{4,3,2,1,0:T(8,128)S(1)}) custom-call(f32[10,2,64,128]{3,2,1,0:T(8,128)S(1)} %get-tuple-element.43.state, s32[2,64,128]{2,1,0:T(8,128)S(1)} %get-tuple-element.29.labels, f32[8,8,128]{2,1,0:T(8,128)S(1)} %get-tuple-element.44.strip), custom_call_target="tpu_custom_call" | custom-call | tf_op jit(solution)/shard_map/pallas_call | solution.py:621
  25.7 0.0 collective-permute-done.4.even
  25.7 1.7 %collective-permute-done.5.odd = f32[16,8,128]{2,1,0:T(8,128)S(1)} collective-permute-done((f32[16,8,128]{2,1,0:T(8,128)S(1)}, f32[16,8,128]{2,1,0:T(8,128)S(1)}, u32[]{:S(2)}, u32[]{:S(2)}) %collective-permute-start.5) | collective-permute-done | bytes 65568 | tf_op jit(solution)/shard_map/ppermute | solution.py:639
  27.4 1.5 %shard_map.62 = f32[27,8,8,256]{3,2,1,0:T(8,128)} custom-call(f32[9,6,2,8,8,128]{5,4,3,2,1,0:T(8,128)S(1)} %get-tuple-element.45.moved, s32[9,2,8,8,128]{4,3,2,1,0:T(8,128)S(1)} %get-tuple-element.46.moved_labels, f32[8,128]{1,0:T(8,128)S(1)} %get-tuple-element.47.sums, f32[8,128]{1,0:T(8,128)S(1)} %get-tuple-element.48.counts, ...), custom_call_target="tpu_custom_call" | custom-call | tf_op jit(solution)/shard_map/pallas_call | solution.py:621
Async XLA Ops:
  0.0 19.5 %copy-start.1 = (f32[9,8,256]{2,1,0:T(8,128)S(1)}, f32[9,8,256]{2,1,0:T(8,128)}, u32[]{:S(2)}) copy-start(f32[9,8,256]{2,1,0:T(8,128)} %top.3) | copy-start | bytes 221188
  0.0 19.5 %copy-start = (f32[9,8,256]{2,1,0:T(8,128)S(1)}, f32[9,8,256]{2,1,0:T(8,128)}, u32[]{:S(2)}) copy-start(f32[9,8,256]{2,1,0:T(8,128)} %bottom.3) | copy-start | bytes 221188
  2.0 4.2 %collective-permute-start = (f32[9,8,128]{2,1,0:T(8,128)S(1)}, f32[9,8,128]{2,1,0:T(8,128)S(1)}, u32[]{:S(2)}, u32[]{:S(2)}) collective-permute-start(f32[9,8,128]{2,1,0:T(8,128)S(1)} %get-tuple-element.31), channel_id=1, source_target_pairs={{0,1},{2,3},{4,5},{6,7},{8,9},{10,11},{12,13},{14,15},{1,0},{3,2},... | collective-permute-start | bytes 110600 | tf_op jit(solution)/shard_map/ppermute | solution.py:639
  2.1 7.1 %collective-permute-start.1 = (f32[9,8,128]{2,1,0:T(8,128)S(1)}, f32[9,8,128]{2,1,0:T(8,128)S(1)}, u32[]{:S(2)}, u32[]{:S(2)}) collective-permute-start(f32[9,8,128]{2,1,0:T(8,128)S(1)} %get-tuple-element.32), channel_id=1, source_target_pairs={{1,2},{3,4},{5,6},{7,8},{9,10},{11,12},{13,14},{15,0},{2,1},{4,3},... | collective-permute-start | bytes 110600 | tf_op jit(solution)/shard_map/ppermute | solution.py:639
  9.7 9.3 %collective-permute-start.2 = (f32[19,8,128]{2,1,0:T(8,128)S(1)}, f32[19,8,128]{2,1,0:T(8,128)S(1)}, u32[]{:S(2)}, u32[]{:S(2)}) collective-permute-start(f32[19,8,128]{2,1,0:T(8,128)S(1)} %get-tuple-element.41), channel_id=1, source_target_pairs={{0,16},{32,48},{64,80},{96,112},{128,144},{160,176},{192,208},{224... | collective-permute-start | bytes 233480 | tf_op jit(solution)/shard_map/ppermute | solution.py:639
  10.9 8.5 %collective-permute-start.3 = (f32[19,8,128]{2,1,0:T(8,128)S(1)}, f32[19,8,128]{2,1,0:T(8,128)S(1)}, u32[]{:S(2)}, u32[]{:S(2)}) collective-permute-start(f32[19,8,128]{2,1,0:T(8,128)S(1)} %get-tuple-element.42), channel_id=1, source_target_pairs={{16,32},{48,64},{80,96},{112,128},{144,160},{176,192},{208,224},{2... | collective-permute-start | bytes 233480 | tf_op jit(solution)/shard_map/ppermute | solution.py:639
  20.8 4.9 %collective-permute-start.4 = (f32[16,8,128]{2,1,0:T(8,128)S(1)}, f32[16,8,128]{2,1,0:T(8,128)S(1)}, u32[]{:S(2)}, u32[]{:S(2)}) collective-permute-start(f32[16,8,128]{2,1,0:T(8,128)S(1)} %get-tuple-element.49), channel_id=1, source_target_pairs={{0,16},{32,48},{64,80},{96,112},{128,144},{160,176},{192,208},{224... | collective-permute-start | bytes 196616 | tf_op jit(solution)/shard_map/ppermute | solution.py:639
  20.9 6.5 %collective-permute-start.5 = (f32[16,8,128]{2,1,0:T(8,128)S(1)}, f32[16,8,128]{2,1,0:T(8,128)S(1)}, u32[]{:S(2)}, u32[]{:S(2)}) collective-permute-start(f32[16,8,128]{2,1,0:T(8,128)S(1)} %get-tuple-element.50), channel_id=1, source_target_pairs={{16,32},{48,64},{80,96},{112,128},{144,160},{176,192},{208,224},{2... | collective-permute-start | bytes 196616 | tf_op jit(solution)/shard_map/ppermute | solution.py:639

commit v6 on v5

--- a/solution.py
+++ b/solution.py
@@ -330,10 +330,11 @@
     slot = edge_rows(state, sent)
     for j in range(2):
         sent.put(slot + j, *(labels[j, pl.ds(row, 8, stride=8), :].astype(jnp.float32) for row in (7, 0)))
-    for side in range(2):
-        blocks = [domains[side, n] for n in X_FIELDS + (LABEL,)]
-        sent.put(slot + 2 + side, rows_of(blocks, 7), rows_of(blocks, 0))
-    sent.put(slot + 4, sums, sums)
+    ends = [
+        jnp.where(column < 9, domains[0, n], roll(domains[1, n], 2, 1)) for n in X_FIELDS + (LABEL,)
+    ]
+    sent.put(slot + 2, rows_of(ends, 7), rows_of(ends, 0))
+    sent.put(slot + 3, sums, sums)
 
 
 look_up = take
@@ -385,10 +386,10 @@
     thrust = look_up(table, index_of(domains[side, LABEL]))
     parts = [d[RHO] * h for h in shapes(d[VX] - thrust)]
     along_y, along_z = shapes(d[VY]), shapes(d[VZ])
-    n = 2 * len(X_FIELDS) + 2 + side
+    n = 2 * len(X_FIELDS) + 2
     outer = {}
     for a, message in ((2, left), (0, right)):
-        fields = row_blocks(message[n], 8)
+        fields = row_blocks(roll(message[n], -2 * side, 1), 8)
         outer[a] = entering(table, fields[:7], index_of(fields[7]), a)
     new = {}
     for a in range(3):
@@ -487,7 +488,7 @@
     prepare(state, labels, [strip[n] for n in range(8)], moved, moved_labels)
 
 
-def stream(table, moved, moved_labels, left, right, left_marks, right_marks, corners, bottom, top, out, ghost, whole=None):
+def streamed(table, moved, moved_labels, left, right, left_marks, right_marks, corners, bottom, top, ghost):
     rows = iota(0)
     for side, (source, marks) in enumerate(((left, left_marks), (right, right_marks))):
         a = 2 - 2 * side
@@ -500,38 +501,29 @@
                 pair = shift_columns(halves[0][b, c], halves[1][b, c], b, inflow)
                 for j in range(2):
                     ghost[side, 3 * b + c, j] = pair[j]
-    for a in range(3):
-        for b in range(3):
-            out[9 * a + 3 * b + 2, 0] = bottom[3 * a + b]
-            out[9 * a + 3 * b, LEVELS - 1] = top[3 * a + b]
-
-    for z in range(LEVELS):
-        for j in range(2):
-            for a in range(3):
-                for b in range(3):
-                    place = 3 * a + b
-                    speed = moved[place, 0, j, z] - look_up(table, moved_labels[place, j, z])
-                    h = shapes(speed)[a]
-                    for c in range(3):
-                        level = z + c - 1
-                        if level < 0 or level >= LEVELS:
-                            continue
-                        value = moved[place, 1 + c, j, z] * h
-                        if c == 1:
-                            value = value + moved[place, 4, j, z]
-                        elif a == 1 and b == 1:
-                            value = value + moved[place, 5, j, z]
-                        elif a == 1 or b == 1:
-                            value = value + (c - 1) * moved[place, 5, j, z]
-                        if a == 2:
-                            value = jnp.where(rows == 0, ghost[0, 3 * b + c, j, z : z + 1, :], value)
-                        elif a == 0:
-                            value = jnp.where(rows == 7, ghost[1, 3 * b + c, j, z : z + 1, :], value)
-                        out[9 * a + 3 * b + c, level, :, 128 * j : 128 * j + 128] = value
-        if whole and z:
-            whole(z - 1)
-    if whole:
-        whole(LEVELS - 1)
+
+    @functools.cache
+    def along_x(place, j, z):
+        return shapes(moved[place, 0, j, z] - look_up(table, moved_labels[place, j, z]))[place // 3]
+
+    def slot(level, j, a, b, c):
+        z, place = level + 1 - c, 3 * a + b
+        if z < 0 or z >= LEVELS:
+            return (bottom if z < 0 else top)[place, :, 128 * j : 128 * j + 128]
+        value = moved[place, 1 + c, j, z] * along_x(place, j, z)
+        if c == 1:
+            value = value + moved[place, 4, j, z]
+        elif a == 1 and b == 1:
+            value = value + moved[place, 5, j, z]
+        elif a == 1 or b == 1:
+            value = value + (c - 1) * moved[place, 5, j, z]
+        if a == 2:
+            return jnp.where(rows == 0, ghost[0, 3 * b + c, j, z : z + 1, :], value)
+        if a == 0:
+            return jnp.where(rows == 7, ghost[1, 3 * b + c, j, z : z + 1, :], value)
+        return value
+
+    return slot
 
 
 def disk_table(sums, counts):
@@ -545,11 +537,11 @@
 
 def middle_kernel(
     moved, moved_labels, domains, column_sums, beside, starts, found, found_beside, even, odd, bottom, top,
-    new_state, to_even, to_odd, strip, counts, sums_out, f_ref, ghost, speeds,
+    new_state, to_even, to_odd, strip, counts, sums_out, ghost, speeds,
 ):
     lanes = iota(1)
     left, right = Paired("gx", even, odd).received()
-    last = 2 * len(X_FIELDS) + 4
+    last = 2 * len(X_FIELDS) + 3
     totals = column_sums[...] + left[last] + right[last]
     seen = roll(totals, 64, 1)
     counts[...] = seen
@@ -568,12 +560,9 @@
     strips = [merged_strip(one, other) for one, other in zip(*kept)]
     for n, block in enumerate(strips):
         strip[n] = block
-    stream(
-        table, moved, moved_labels, left, right, marks_of(left), marks_of(right), corners, bottom, top, f_ref, ghost
-    )
-
-    def f(z, j, a, b, c):
-        return f_ref[9 * a + 3 * b + c, z, :, 128 * j : 128 * j + 128]
+    f = streamed(
+        table, moved, moved_labels, left, right, marks_of(left), marks_of(right), corners, bottom, top, ghost
+    )
 
     def keep_speed(z, j, ux):
         speeds[j, z] = ux
@@ -604,10 +593,14 @@
         for message, a in ((left, 2), (right, 0))
     ]
     copies = [pltpu.make_async_copy(out.at[:, z], out_hbm.at[:, z], gone.at[z]) for z in range(LEVELS)]
-    stream(
-        table, moved, moved_labels, left, right, marks_of(old_left), marks_of(old_right), corners, bottom, top, out, ghost,
-        whole=lambda z: copies[z].start(),
-    )
+    f = streamed(
+        table, moved, moved_labels, left, right, marks_of(old_left), marks_of(old_right), corners, bottom, top, ghost
+    )
+    for z in range(LEVELS):
+        for j in range(2):
+            for slot in range(27):
+                out[slot, z, :, 128 * j : 128 * j + 128] = f(z, j, slot // 9, slot // 3 % 3, slot % 3)
+        copies[z].start()
     for copy in copies:
         copy.wait()
 
@@ -665,7 +658,7 @@
     domains, to_even, to_odd, column_sums, beside = call(
         relay_kernel,
         (state, labels, edges, own_sums, even, odd),
-        (blocks(2, 12), blocks(n + 5), blocks(n + 5), one, blocks(2, 2)),
+        (blocks(2, 12), blocks(n + 4), blocks(n + 4), one, blocks(2, 2)),
     )
     old_even, old_odd = swapped(to_even, to_odd, "gx")
     starts, found, found_beside = call(
@@ -682,7 +675,7 @@
             old_even, old_odd, bottom_in, top_in,
         ),
         (state_shape, blocks(n + 2), blocks(n + 2), blocks(8), one, one),
-        (whole, ghost, blocks(2, LEVELS)),
+        (ghost, blocks(2, LEVELS)),
     )
     even, odd = swapped(to_even, to_odd, "gx")
     moved, moved_labels = call(last_prepare_kernel, (state, labels, strip), shifted)

time: 29.1 us -> 29 us (level)
  no operation moved by 1% of the time
where the time goes in v6:
time: 29 us; the launch traced here: 28.9 us
  starting transfers between devices  14.9 us (51%)
  Pallas kernels  8.78 us (30%)
  waiting for transfers between devices  5.1 us (18%)
    ppermute x3, starting transfers between devices, swapped(): lax.ppermute(odd, axis, pairs(1))  13.4 us
    pallas_call x8, Pallas kernels, call(): pl.pallas_call(kernel, out_shape=[jax.ShapeDtypeStruct(shape, dtype) for...  8.78 us
    ppermute x3, waiting for transfers between devices, swapped(): lax.ppermute(odd, axis, pairs(1))  5.09 us
    ppermute x3, starting transfers between devices, swapped(): lax.ppermute(even, axis, pairs(0))  1.47 us
  transfers between devices with their start and end apart: 6, of which 3 were waited for; matrix products, arithmetic and copies ran while one was open for 0% of the time, Pallas kernels for 12%

profile of v6, /device:TPU:4, one launch (start us, length us, event | category | flops | bytes accessed | tf_op | source)
XLA Modules:
  0.0 28.9 jit_solution(1831523752013304244)
XLA Ops:
  0.0 0.0 copy-start.1
  0.0 0.0 copy-start
  0.0 2.0 %shard_map.55 = (f32[11,2,64,128]{3,2,1,0:T(8,128)S(1)}, s32[2,64,128]{2,1,0:T(8,128)S(1)}, f32[12,8,128]{2,1,0:T(8,128)S(1)}, f32[9,8,128]{2,1,0:T(8,128)S(1)}, f32[9,8,128]{2,1,0:T(8,128)S(1)}) custom-call(f32[27,8,8,256]{3,2,1,0:T(8,128)} %f_hbm.1, s32[8,8,256]{2,1,0:T(8,128)} %mask_hbm.1, s32[8,8,256]{2,1,0:T(8,128)} %rotor_hbm.1, f32[9,8,256]{2,1,0:T(8,128)} %bottom.3, ...), custom_call_target="tpu_custom_call" | custom-call | tf_op jit(solution)/shard_map/pallas_call | solution.py:614
  2.0 0.1 collective-permute-start
  2.1 3.1 %collective-permute-start.1 = (f32[9,8,128]{2,1,0:T(8,128)S(1)}, f32[9,8,128]{2,1,0:T(8,128)S(1)}, u32[]{:S(2)}, u32[]{:S(2)}) collective-permute-start(f32[9,8,128]{2,1,0:T(8,128)S(1)} %get-tuple-element.32), channel_id=1, source_target_pairs={{1,2},{3,4},{5,6},{7,8},{9,10},{11,12},{13,14},{15,0},{2,1},{4,3},... | collective-permute-start | bytes 110600 | tf_op jit(solution)/shard_map/ppermute | solution.py:632
  5.2 1.1 %shard_map.56.own_sums = f32[8,128]{1,0:T(8,128)S(1)} custom-call(f32[11,2,64,128]{3,2,1,0:T(8,128)S(1)} %get-tuple-element.28.state, s32[2,64,128]{2,1,0:T(8,128)S(1)} %get-tuple-element.29.labels), custom_call_target="tpu_custom_call" | custom-call | tf_op jit(solution)/shard_map/pallas_call | solution.py:614
  6.3 0.0 collective-permute-done.even
  6.3 3.0 %collective-permute-done.1.odd = f32[9,8,128]{2,1,0:T(8,128)S(1)} collective-permute-done((f32[9,8,128]{2,1,0:T(8,128)S(1)}, f32[9,8,128]{2,1,0:T(8,128)S(1)}, u32[]{:S(2)}, u32[]{:S(2)}) %collective-permute-start.1) | collective-permute-done | bytes 36896 | tf_op jit(solution)/shard_map/ppermute | solution.py:632
  9.2 0.4 %shard_map.57 = (f32[2,12,8,128]{3,2,1,0:T(8,128)S(1)}, f32[18,8,128]{2,1,0:T(8,128)S(1)}, f32[18,8,128]{2,1,0:T(8,128)S(1)}, f32[8,128]{1,0:T(8,128)S(1)}, f32[2,2,8,128]{3,2,1,0:T(8,128)S(1)}) custom-call(f32[11,2,64,128]{3,2,1,0:T(8,128)S(1)} %get-tuple-element.28.state, s32[2,64,128]{2,1,0:T(8,128)S(1)} %get-tuple-element.29.labels, ...), custom_call_target="tpu_custom_call" | custom-call | tf_op jit(solution)/shard_map/pallas_call | solution.py:614
  9.7 1.3 %collective-permute-start.2 = (f32[18,8,128]{2,1,0:T(8,128)S(1)}, f32[18,8,128]{2,1,0:T(8,128)S(1)}, u32[]{:S(2)}, u32[]{:S(2)}) collective-permute-start(f32[18,8,128]{2,1,0:T(8,128)S(1)} %get-tuple-element.41), channel_id=1, source_target_pairs={{0,16},{32,48},{64,80},{96,112},{128,144},{160,176},{192,208},{224... | collective-permute-start | bytes 221192 | tf_op jit(solution)/shard_map/ppermute | solution.py:632
  10.9 6.1 %collective-permute-start.3 = (f32[18,8,128]{2,1,0:T(8,128)S(1)}, f32[18,8,128]{2,1,0:T(8,128)S(1)}, u32[]{:S(2)}, u32[]{:S(2)}) collective-permute-start(f32[18,8,128]{2,1,0:T(8,128)S(1)} %get-tuple-element.42), channel_id=1, source_target_pairs={{16,32},{48,64},{80,96},{112,128},{144,160},{176,192},{208,224},{2... | collective-permute-start | bytes 221192 | tf_op jit(solution)/shard_map/ppermute | solution.py:632
  17.1 1.3 %shard_map.59 = (s32[2,8,128]{2,1,0:T(8,128)S(1)}, f32[5,2,8,8,128]{4,3,2,1,0:T(8,128)S(1)}, f32[5,8,8,128]{3,2,1,0:T(8,128)S(1)}) custom-call(s32[2,64,128]{2,1,0:T(8,128)S(1)} %get-tuple-element.29.labels, f32[2,12,8,128]{3,2,1,0:T(8,128)S(1)} %get-tuple-element.33.domains), custom_call_target="tpu_custom_call" | custom-call | tf_op jit(solution)/shard_map/pallas_call | solution.py:614
  18.4 0.6 %shard_map.58 = (f32[9,6,2,8,8,128]{5,4,3,2,1,0:T(8,128)S(1)}, s32[9,2,8,8,128]{4,3,2,1,0:T(8,128)S(1)}) custom-call(f32[11,2,64,128]{3,2,1,0:T(8,128)S(1)} %get-tuple-element.28.state, s32[2,64,128]{2,1,0:T(8,128)S(1)} %get-tuple-element.29.labels, f32[2,12,8,128]{3,2,1,0:T(8,128)S(1)} %get-tuple-element.33.domains), custom_call_target="tpu_custom_call" | custom-call | tf_op jit(solution)/shard_map/pallas_call | solution.py:614
  18.9 0.0 collective-permute-done.2.even.old_even
  19.0 0.5 %collective-permute-done.3.odd.old_odd = f32[18,8,128]{2,1,0:T(8,128)S(1)} collective-permute-done((f32[18,8,128]{2,1,0:T(8,128)S(1)}, f32[18,8,128]{2,1,0:T(8,128)S(1)}, u32[]{:S(2)}, u32[]{:S(2)}) %collective-permute-start.3) | collective-permute-done | bytes 73760 | tf_op jit(solution)/shard_map/ppermute | solution.py:632
  19.4 0.0 copy-done.1
  19.4 0.0 copy-done
  19.4 1.3 %shard_map.60 = (f32[10,2,64,128]{3,2,1,0:T(8,128)S(1)}, f32[16,8,128]{2,1,0:T(8,128)S(1)}, f32[16,8,128]{2,1,0:T(8,128)S(1)}, f32[8,8,128]{2,1,0:T(8,128)S(1)},...) custom-call(f32[9,6,2,8,8,128]{5,4,3,2,1,0:T(8,128)S(1)} %get-tuple-element.34.moved, ...), custom_call_target="tpu_custom_call" | custom-call | tf_op jit(solution)/shard_map/pallas_call | solution.py:614
  20.7 0.1 collective-permute-start.4
  20.8 4.3 %collective-permute-start.5 = (f32[16,8,128]{2,1,0:T(8,128)S(1)}, f32[16,8,128]{2,1,0:T(8,128)S(1)}, u32[]{:S(2)}, u32[]{:S(2)}) collective-permute-start(f32[16,8,128]{2,1,0:T(8,128)S(1)} %get-tuple-element.50), channel_id=1, source_target_pairs={{16,32},{48,64},{80,96},{112,128},{144,160},{176,192},{208,224},{2... | collective-permute-start | bytes 196616 | tf_op jit(solution)/shard_map/ppermute | solution.py:632
  25.1 0.5 %shard_map.61 = (f32[9,6,2,8,8,128]{5,4,3,2,1,0:T(8,128)S(1)}, s32[9,2,8,8,128]{4,3,2,1,0:T(8,128)S(1)}) custom-call(f32[10,2,64,128]{3,2,1,0:T(8,128)S(1)} %get-tuple-element.43.state, s32[2,64,128]{2,1,0:T(8,128)S(1)} %get-tuple-element.29.labels, f32[8,8,128]{2,1,0:T(8,128)S(1)} %get-tuple-element.44.strip), custom_call_target="tpu_custom_call" | custom-call | tf_op jit(solution)/shard_map/pallas_call | solution.py:614
  25.6 0.0 collective-permute-done.4.even
  25.7 1.7 %collective-permute-done.5.odd = f32[16,8,128]{2,1,0:T(8,128)S(1)} collective-permute-done((f32[16,8,128]{2,1,0:T(8,128)S(1)}, f32[16,8,128]{2,1,0:T(8,128)S(1)}, u32[]{:S(2)}, u32[]{:S(2)}) %collective-permute-start.5) | collective-permute-done | bytes 65568 | tf_op jit(solution)/shard_map/ppermute | solution.py:632
  27.3 1.5 %shard_map.62 = f32[27,8,8,256]{3,2,1,0:T(8,128)} custom-call(f32[9,6,2,8,8,128]{5,4,3,2,1,0:T(8,128)S(1)} %get-tuple-element.45.moved, s32[9,2,8,8,128]{4,3,2,1,0:T(8,128)S(1)} %get-tuple-element.46.moved_labels, f32[8,128]{1,0:T(8,128)S(1)} %get-tuple-element.47.sums, f32[8,128]{1,0:T(8,128)S(1)} %get-tuple-element.48.counts, ...), custom_call_target="tpu_custom_call" | custom-call | tf_op jit(solution)/shard_map/pallas_call | solution.py:614
Async XLA Ops:
  0.0 19.4 %copy-start.1 = (f32[9,8,256]{2,1,0:T(8,128)S(1)}, f32[9,8,256]{2,1,0:T(8,128)}, u32[]{:S(2)}) copy-start(f32[9,8,256]{2,1,0:T(8,128)} %top.3) | copy-start | bytes 221188
  0.0 19.4 %copy-start = (f32[9,8,256]{2,1,0:T(8,128)S(1)}, f32[9,8,256]{2,1,0:T(8,128)}, u32[]{:S(2)}) copy-start(f32[9,8,256]{2,1,0:T(8,128)} %bottom.3) | copy-start | bytes 221188
  2.0 4.2 %collective-permute-start = (f32[9,8,128]{2,1,0:T(8,128)S(1)}, f32[9,8,128]{2,1,0:T(8,128)S(1)}, u32[]{:S(2)}, u32[]{:S(2)}) collective-permute-start(f32[9,8,128]{2,1,0:T(8,128)S(1)} %get-tuple-element.31), channel_id=1, source_target_pairs={{0,1},{2,3},{4,5},{6,7},{8,9},{10,11},{12,13},{14,15},{1,0},{3,2},... | collective-permute-start | bytes 110600 | tf_op jit(solution)/shard_map/ppermute | solution.py:632
  2.1 7.1 %collective-permute-start.1 = (f32[9,8,128]{2,1,0:T(8,128)S(1)}, f32[9,8,128]{2,1,0:T(8,128)S(1)}, u32[]{:S(2)}, u32[]{:S(2)}) collective-permute-start(f32[9,8,128]{2,1,0:T(8,128)S(1)} %get-tuple-element.32), channel_id=1, source_target_pairs={{1,2},{3,4},{5,6},{7,8},{9,10},{11,12},{13,14},{15,0},{2,1},{4,3},... | collective-permute-start | bytes 110600 | tf_op jit(solution)/shard_map/ppermute | solution.py:632
  9.7 9.3 %collective-permute-start.2 = (f32[18,8,128]{2,1,0:T(8,128)S(1)}, f32[18,8,128]{2,1,0:T(8,128)S(1)}, u32[]{:S(2)}, u32[]{:S(2)}) collective-permute-start(f32[18,8,128]{2,1,0:T(8,128)S(1)} %get-tuple-element.41), channel_id=1, source_target_pairs={{0,16},{32,48},{64,80},{96,112},{128,144},{160,176},{192,208},{224... | collective-permute-start | bytes 221192 | tf_op jit(solution)/shard_map/ppermute | solution.py:632
  10.9 8.5 %collective-permute-start.3 = (f32[18,8,128]{2,1,0:T(8,128)S(1)}, f32[18,8,128]{2,1,0:T(8,128)S(1)}, u32[]{:S(2)}, u32[]{:S(2)}) collective-permute-start(f32[18,8,128]{2,1,0:T(8,128)S(1)} %get-tuple-element.42), channel_id=1, source_target_pairs={{16,32},{48,64},{80,96},{112,128},{144,160},{176,192},{208,224},{2... | collective-permute-start | bytes 221192 | tf_op jit(solution)/shard_map/ppermute | solution.py:632
  20.7 4.9 %collective-permute-start.4 = (f32[16,8,128]{2,1,0:T(8,128)S(1)}, f32[16,8,128]{2,1,0:T(8,128)S(1)}, u32[]{:S(2)}, u32[]{:S(2)}) collective-permute-start(f32[16,8,128]{2,1,0:T(8,128)S(1)} %get-tuple-element.49), channel_id=1, source_target_pairs={{0,16},{32,48},{64,80},{96,112},{128,144},{160,176},{192,208},{224... | collective-permute-start | bytes 196616 | tf_op jit(solution)/shard_map/ppermute | solution.py:632
  20.8 6.5 %collective-permute-start.5 = (f32[16,8,128]{2,1,0:T(8,128)S(1)}, f32[16,8,128]{2,1,0:T(8,128)S(1)}, u32[]{:S(2)}, u32[]{:S(2)}) collective-permute-start(f32[16,8,128]{2,1,0:T(8,128)S(1)} %get-tuple-element.50), channel_id=1, source_target_pairs={{16,32},{48,64},{80,96},{112,128},{144,160},{176,192},{208,224},{2... | collective-permute-start | bytes 196616 | tf_op jit(solution)/shard_map/ppermute | solution.py:632

commit v7 on v6

--- a/solution.py
+++ b/solution.py
@@ -205,10 +205,20 @@
             ((mask_hbm, mask_ref), (rotor_hbm, rotor_ref), (bottom_hbm, bottom), (top_hbm, top))
         )
     ]
-    for copy in [levels[0]] + others[:2] + levels[1:] + others[2:]:
+    for copy in others + levels:
         copy.start()
-    others[0].wait()
-    others[1].wait()
+    for copy in others:
+        copy.wait()
+    send = Paired("gy", to_even, to_odd).put
+    for place, source in ((7, bottom), (8, top)):
+        upward = jnp.zeros((8, 128), jnp.float32)
+        downward = upward
+        for n in range(9):
+            both = jnp.where(lanes < 64, source[n, :, 0:128], source[n, :, 128:256])
+            moved = roll(both, 8 * n + 8, 1)
+            upward = jnp.where(lanes // 8 == n, moved, upward)
+            downward = jnp.where(lanes // 8 == n + 1, moved, downward)
+        send(place, upward, downward)
     waiting = list(levels)
 
     def f(z, j, a, b, c):
@@ -241,7 +251,6 @@
     for n, block in enumerate(blocks):
         edges[n] = block
     low = (lanes & 8) == 0
-    send = Paired("gy", to_even, to_odd).put
 
     for n in range(6):
         one, other = blocks[2 * n], blocks[2 * n + 1]
@@ -252,17 +261,6 @@
         jnp.where(column >= 14, inner_speed, jnp.where(column >= 12, roll(inner_label, -2, 1), float(EMPTY))),
         jnp.where(column < 2, inner_speed, jnp.where(column < 4, roll(inner_label, 2, 1), float(EMPTY))),
     )
-    others[2].wait()
-    others[3].wait()
-    for place, source in ((7, bottom), (8, top)):
-        upward = jnp.zeros((8, 128), jnp.float32)
-        downward = upward
-        for n in range(9):
-            both = jnp.where(lanes < 64, source[n, :, 0:128], source[n, :, 128:256])
-            moved = roll(both, 8 * n + 8, 1)
-            upward = jnp.where(lanes // 8 == n, moved, upward)
-            downward = jnp.where(lanes // 8 == n + 1, moved, downward)
-        send(place, upward, downward)
 
 
 class Paired:

time: 29 us -> 29 us (level)
  no operation moved by 1% of the time
where the time goes in v7:
time: 29 us; the launch traced here: 28.9 us
  starting transfers between devices  14.9 us (51%)
  Pallas kernels  8.77 us (30%)
  waiting for transfers between devices  5.1 us (18%)
    ppermute x3, starting transfers between devices, swapped(): lax.ppermute(odd, axis, pairs(1))  13.4 us
    pallas_call x8, Pallas kernels, call(): pl.pallas_call(kernel, out_shape=[jax.ShapeDtypeStruct(shape, dtype) for...  8.77 us
    ppermute x3, waiting for transfers between devices, swapped(): lax.ppermute(odd, axis, pairs(1))  5.09 us
    ppermute x3, starting transfers between devices, swapped(): lax.ppermute(even, axis, pairs(0))  1.47 us
  transfers between devices with their start and end apart: 6, of which 3 were waited for; matrix products, arithmetic and copies ran while one was open for 0% of the time, Pallas kernels for 12%

profile of v7, /device:TPU:4, one launch (start us, length us, event | category | flops | bytes accessed | tf_op | source)
XLA Modules:
  0.0 28.9 jit_solution(637742374333563319)
XLA Ops:
  0.0 0.0 copy-start.1
  0.0 0.0 copy-start
  0.0 2.0 %shard_map.55 = (f32[11,2,64,128]{3,2,1,0:T(8,128)S(1)}, s32[2,64,128]{2,1,0:T(8,128)S(1)}, f32[12,8,128]{2,1,0:T(8,128)S(1)}, f32[9,8,128]{2,1,0:T(8,128)S(1)}, f32[9,8,128]{2,1,0:T(8,128)S(1)}) custom-call(f32[27,8,8,256]{3,2,1,0:T(8,128)} %f_hbm.1, s32[8,8,256]{2,1,0:T(8,128)} %mask_hbm.1, s32[8,8,256]{2,1,0:T(8,128)} %rotor_hbm.1, f32[9,8,256]{2,1,0:T(8,128)} %bottom.3, ...), custom_call_target="tpu_custom_call" | custom-call | tf_op jit(solution)/shard_map/pallas_call | solution.py:612
  2.0 0.1 collective-permute-start
  2.1 3.1 %collective-permute-start.1 = (f32[9,8,128]{2,1,0:T(8,128)S(1)}, f32[9,8,128]{2,1,0:T(8,128)S(1)}, u32[]{:S(2)}, u32[]{:S(2)}) collective-permute-start(f32[9,8,128]{2,1,0:T(8,128)S(1)} %get-tuple-element.32), channel_id=1, source_target_pairs={{1,2},{3,4},{5,6},{7,8},{9,10},{11,12},{13,14},{15,0},{2,1},{4,3},... | collective-permute-start | bytes 110600 | tf_op jit(solution)/shard_map/ppermute | solution.py:630
  5.2 1.1 %shard_map.56.own_sums = f32[8,128]{1,0:T(8,128)S(1)} custom-call(f32[11,2,64,128]{3,2,1,0:T(8,128)S(1)} %get-tuple-element.28.state, s32[2,64,128]{2,1,0:T(8,128)S(1)} %get-tuple-element.29.labels), custom_call_target="tpu_custom_call" | custom-call | tf_op jit(solution)/shard_map/pallas_call | solution.py:612
  6.3 0.0 collective-permute-done.even
  6.3 3.0 %collective-permute-done.1.odd = f32[9,8,128]{2,1,0:T(8,128)S(1)} collective-permute-done((f32[9,8,128]{2,1,0:T(8,128)S(1)}, f32[9,8,128]{2,1,0:T(8,128)S(1)}, u32[]{:S(2)}, u32[]{:S(2)}) %collective-permute-start.1) | collective-permute-done | bytes 36896 | tf_op jit(solution)/shard_map/ppermute | solution.py:630
  9.2 0.4 %shard_map.57 = (f32[2,12,8,128]{3,2,1,0:T(8,128)S(1)}, f32[18,8,128]{2,1,0:T(8,128)S(1)}, f32[18,8,128]{2,1,0:T(8,128)S(1)}, f32[8,128]{1,0:T(8,128)S(1)}, f32[2,2,8,128]{3,2,1,0:T(8,128)S(1)}) custom-call(f32[11,2,64,128]{3,2,1,0:T(8,128)S(1)} %get-tuple-element.28.state, s32[2,64,128]{2,1,0:T(8,128)S(1)} %get-tuple-element.29.labels, ...), custom_call_target="tpu_custom_call" | custom-call | tf_op jit(solution)/shard_map/pallas_call | solution.py:612
  9.6 1.3 %collective-permute-start.2 = (f32[18,8,128]{2,1,0:T(8,128)S(1)}, f32[18,8,128]{2,1,0:T(8,128)S(1)}, u32[]{:S(2)}, u32[]{:S(2)}) collective-permute-start(f32[18,8,128]{2,1,0:T(8,128)S(1)} %get-tuple-element.41), channel_id=1, source_target_pairs={{0,16},{32,48},{64,80},{96,112},{128,144},{160,176},{192,208},{224... | collective-permute-start | bytes 221192 | tf_op jit(solution)/shard_map/ppermute | solution.py:630
  10.9 6.1 %collective-permute-start.3 = (f32[18,8,128]{2,1,0:T(8,128)S(1)}, f32[18,8,128]{2,1,0:T(8,128)S(1)}, u32[]{:S(2)}, u32[]{:S(2)}) collective-permute-start(f32[18,8,128]{2,1,0:T(8,128)S(1)} %get-tuple-element.42), channel_id=1, source_target_pairs={{16,32},{48,64},{80,96},{112,128},{144,160},{176,192},{208,224},{2... | collective-permute-start | bytes 221192 | tf_op jit(solution)/shard_map/ppermute | solution.py:630
  17.0 1.3 %shard_map.59 = (s32[2,8,128]{2,1,0:T(8,128)S(1)}, f32[5,2,8,8,128]{4,3,2,1,0:T(8,128)S(1)}, f32[5,8,8,128]{3,2,1,0:T(8,128)S(1)}) custom-call(s32[2,64,128]{2,1,0:T(8,128)S(1)} %get-tuple-element.29.labels, f32[2,12,8,128]{3,2,1,0:T(8,128)S(1)} %get-tuple-element.33.domains), custom_call_target="tpu_custom_call" | custom-call | tf_op jit(solution)/shard_map/pallas_call | solution.py:612
  18.4 0.6 %shard_map.58 = (f32[9,6,2,8,8,128]{5,4,3,2,1,0:T(8,128)S(1)}, s32[9,2,8,8,128]{4,3,2,1,0:T(8,128)S(1)}) custom-call(f32[11,2,64,128]{3,2,1,0:T(8,128)S(1)} %get-tuple-element.28.state, s32[2,64,128]{2,1,0:T(8,128)S(1)} %get-tuple-element.29.labels, f32[2,12,8,128]{3,2,1,0:T(8,128)S(1)} %get-tuple-element.33.domains), custom_call_target="tpu_custom_call" | custom-call | tf_op jit(solution)/shard_map/pallas_call | solution.py:612
  18.9 0.0 collective-permute-done.2.even.old_even
  18.9 0.5 %collective-permute-done.3.odd.old_odd = f32[18,8,128]{2,1,0:T(8,128)S(1)} collective-permute-done((f32[18,8,128]{2,1,0:T(8,128)S(1)}, f32[18,8,128]{2,1,0:T(8,128)S(1)}, u32[]{:S(2)}, u32[]{:S(2)}) %collective-permute-start.3) | collective-permute-done | bytes 73760 | tf_op jit(solution)/shard_map/ppermute | solution.py:630
  19.4 0.0 copy-done.1
  19.4 0.0 copy-done
  19.4 1.3 %shard_map.60 = (f32[10,2,64,128]{3,2,1,0:T(8,128)S(1)}, f32[16,8,128]{2,1,0:T(8,128)S(1)}, f32[16,8,128]{2,1,0:T(8,128)S(1)}, f32[8,8,128]{2,1,0:T(8,128)S(1)},...) custom-call(f32[9,6,2,8,8,128]{5,4,3,2,1,0:T(8,128)S(1)} %get-tuple-element.34.moved, ...), custom_call_target="tpu_custom_call" | custom-call | tf_op jit(solution)/shard_map/pallas_call | solution.py:612
  20.7 0.1 collective-permute-start.4
  20.8 4.3 %collective-permute-start.5 = (f32[16,8,128]{2,1,0:T(8,128)S(1)}, f32[16,8,128]{2,1,0:T(8,128)S(1)}, u32[]{:S(2)}, u32[]{:S(2)}) collective-permute-start(f32[16,8,128]{2,1,0:T(8,128)S(1)} %get-tuple-element.50), channel_id=1, source_target_pairs={{16,32},{48,64},{80,96},{112,128},{144,160},{176,192},{208,224},{2... | collective-permute-start | bytes 196616 | tf_op jit(solution)/shard_map/ppermute | solution.py:630
  25.1 0.5 %shard_map.61 = (f32[9,6,2,8,8,128]{5,4,3,2,1,0:T(8,128)S(1)}, s32[9,2,8,8,128]{4,3,2,1,0:T(8,128)S(1)}) custom-call(f32[10,2,64,128]{3,2,1,0:T(8,128)S(1)} %get-tuple-element.43.state, s32[2,64,128]{2,1,0:T(8,128)S(1)} %get-tuple-element.29.labels, f32[8,8,128]{2,1,0:T(8,128)S(1)} %get-tuple-element.44.strip), custom_call_target="tpu_custom_call" | custom-call | tf_op jit(solution)/shard_map/pallas_call | solution.py:612
  25.6 0.0 collective-permute-done.4.even
  25.6 1.7 %collective-permute-done.5.odd = f32[16,8,128]{2,1,0:T(8,128)S(1)} collective-permute-done((f32[16,8,128]{2,1,0:T(8,128)S(1)}, f32[16,8,128]{2,1,0:T(8,128)S(1)}, u32[]{:S(2)}, u32[]{:S(2)}) %collective-permute-start.5) | collective-permute-done | bytes 65568 | tf_op jit(solution)/shard_map/ppermute | solution.py:630
  27.3 1.5 %shard_map.62 = f32[27,8,8,256]{3,2,1,0:T(8,128)} custom-call(f32[9,6,2,8,8,128]{5,4,3,2,1,0:T(8,128)S(1)} %get-tuple-element.45.moved, s32[9,2,8,8,128]{4,3,2,1,0:T(8,128)S(1)} %get-tuple-element.46.moved_labels, f32[8,128]{1,0:T(8,128)S(1)} %get-tuple-element.47.sums, f32[8,128]{1,0:T(8,128)S(1)} %get-tuple-element.48.counts, ...), custom_call_target="tpu_custom_call" | custom-call | tf_op jit(solution)/shard_map/pallas_call | solution.py:612
Async XLA Ops:
  0.0 19.4 %copy-start.1 = (f32[9,8,256]{2,1,0:T(8,128)S(1)}, f32[9,8,256]{2,1,0:T(8,128)}, u32[]{:S(2)}) copy-start(f32[9,8,256]{2,1,0:T(8,128)} %top.3) | copy-start | bytes 221188
  0.0 19.4 %copy-start = (f32[9,8,256]{2,1,0:T(8,128)S(1)}, f32[9,8,256]{2,1,0:T(8,128)}, u32[]{:S(2)}) copy-start(f32[9,8,256]{2,1,0:T(8,128)} %bottom.3) | copy-start | bytes 221188
  2.0 4.2 %collective-permute-start = (f32[9,8,128]{2,1,0:T(8,128)S(1)}, f32[9,8,128]{2,1,0:T(8,128)S(1)}, u32[]{:S(2)}, u32[]{:S(2)}) collective-permute-start(f32[9,8,128]{2,1,0:T(8,128)S(1)} %get-tuple-element.31), channel_id=1, source_target_pairs={{0,1},{2,3},{4,5},{6,7},{8,9},{10,11},{12,13},{14,15},{1,0},{3,2},... | collective-permute-start | bytes 110600 | tf_op jit(solution)/shard_map/ppermute | solution.py:630
  2.1 7.1 %collective-permute-start.1 = (f32[9,8,128]{2,1,0:T(8,128)S(1)}, f32[9,8,128]{2,1,0:T(8,128)S(1)}, u32[]{:S(2)}, u32[]{:S(2)}) collective-permute-start(f32[9,8,128]{2,1,0:T(8,128)S(1)} %get-tuple-element.32), channel_id=1, source_target_pairs={{1,2},{3,4},{5,6},{7,8},{9,10},{11,12},{13,14},{15,0},{2,1},{4,3},... | collective-permute-start | bytes 110600 | tf_op jit(solution)/shard_map/ppermute | solution.py:630
  9.6 9.3 %collective-permute-start.2 = (f32[18,8,128]{2,1,0:T(8,128)S(1)}, f32[18,8,128]{2,1,0:T(8,128)S(1)}, u32[]{:S(2)}, u32[]{:S(2)}) collective-permute-start(f32[18,8,128]{2,1,0:T(8,128)S(1)} %get-tuple-element.41), channel_id=1, source_target_pairs={{0,16},{32,48},{64,80},{96,112},{128,144},{160,176},{192,208},{224... | collective-permute-start | bytes 221192 | tf_op jit(solution)/shard_map/ppermute | solution.py:630
  10.9 8.5 %collective-permute-start.3 = (f32[18,8,128]{2,1,0:T(8,128)S(1)}, f32[18,8,128]{2,1,0:T(8,128)S(1)}, u32[]{:S(2)}, u32[]{:S(2)}) collective-permute-start(f32[18,8,128]{2,1,0:T(8,128)S(1)} %get-tuple-element.42), channel_id=1, source_target_pairs={{16,32},{48,64},{80,96},{112,128},{144,160},{176,192},{208,224},{2... | collective-permute-start | bytes 221192 | tf_op jit(solution)/shard_map/ppermute | solution.py:630
  20.7 4.9 %collective-permute-start.4 = (f32[16,8,128]{2,1,0:T(8,128)S(1)}, f32[16,8,128]{2,1,0:T(8,128)S(1)}, u32[]{:S(2)}, u32[]{:S(2)}) collective-permute-start(f32[16,8,128]{2,1,0:T(8,128)S(1)} %get-tuple-element.49), channel_id=1, source_target_pairs={{0,16},{32,48},{64,80},{96,112},{128,144},{160,176},{192,208},{224... | collective-permute-start | bytes 196616 | tf_op jit(solution)/shard_map/ppermute | solution.py:630
  20.8 6.5 %collective-permute-start.5 = (f32[16,8,128]{2,1,0:T(8,128)S(1)}, f32[16,8,128]{2,1,0:T(8,128)S(1)}, u32[]{:S(2)}, u32[]{:S(2)}) collective-permute-start(f32[16,8,128]{2,1,0:T(8,128)S(1)} %get-tuple-element.50), channel_id=1, source_target_pairs={{16,32},{48,64},{80,96},{112,128},{144,160},{176,192},{208,224},{2... | collective-permute-start | bytes 196616 | tf_op jit(solution)/shard_map/ppermute | solution.py:630

commit v8 on v7

--- a/solution.py
+++ b/solution.py
@@ -93,7 +93,7 @@
     return block
 
 
-def spread(leaf, join=jnp.add):
+def spread(leaf, join=jnp.add, tree=(16, 8, (2, 8, (1, 2, ())))):
     lanes = iota(1)
 
     def node(stride, ways, rest, index):
@@ -107,7 +107,7 @@
             moved.append(roll(picked, k * stride, 1))
         return functools.reduce(join, moved)
 
-    return over_rows(node(16, 8, (2, 8, (1, 2, ())), 0), join)
+    return over_rows(node(*tree, 0), join)
 
 
 def rotor_sums(labels, speeds):
@@ -157,7 +157,7 @@
             first = jnp.minimum(first, jnp.where(hit, (lanes + 128 * j).astype(jnp.float32), far))
         return first
 
-    both = spread(leaf, jnp.minimum)
+    both = spread(leaf, jnp.minimum, (8, 16, (1, 8, ())))
     begin = (jnp.where(both < far, both, 0.0)).astype(jnp.int32)
     begin_beside = roll(begin.astype(jnp.float32), 64, 1).astype(jnp.int32)
     starts[0] = begin

time: 29 us -> 29 us (level)
  no operation moved by 1% of the time
where the time goes in v8:
time: 29 us; the launch traced here: 28.9 us
  starting transfers between devices  14.9 us (51%)
  Pallas kernels  8.72 us (30%)
  waiting for transfers between devices  5.15 us (18%)
    ppermute x3, starting transfers between devices, swapped(): lax.ppermute(odd, axis, pairs(1))  13.4 us
    pallas_call x8, Pallas kernels, call(): pl.pallas_call(kernel, out_shape=[jax.ShapeDtypeStruct(shape, dtype) for...  8.72 us
    ppermute x3, waiting for transfers between devices, swapped(): lax.ppermute(odd, axis, pairs(1))  5.15 us
    ppermute x3, starting transfers between devices, swapped(): lax.ppermute(even, axis, pairs(0))  1.47 us
  transfers between devices with their start and end apart: 6, of which 3 were waited for; matrix products, arithmetic and copies ran while one was open for 0% of the time, Pallas kernels for 12%

profile of v8, /device:TPU:4, one launch (start us, length us, event | category | flops | bytes accessed | tf_op | source)
XLA Modules:
  0.0 28.9 jit_solution(6945064641583722763)
XLA Ops:
  0.0 0.0 copy-start.1
  0.0 0.0 copy-start
  0.0 2.0 %shard_map.55 = (f32[11,2,64,128]{3,2,1,0:T(8,128)S(1)}, s32[2,64,128]{2,1,0:T(8,128)S(1)}, f32[12,8,128]{2,1,0:T(8,128)S(1)}, f32[9,8,128]{2,1,0:T(8,128)S(1)}, f32[9,8,128]{2,1,0:T(8,128)S(1)}) custom-call(f32[27,8,8,256]{3,2,1,0:T(8,128)} %f_hbm.1, s32[8,8,256]{2,1,0:T(8,128)} %mask_hbm.1, s32[8,8,256]{2,1,0:T(8,128)} %rotor_hbm.1, f32[9,8,256]{2,1,0:T(8,128)} %bottom.3, ...), custom_call_target="tpu_custom_call" | custom-call | tf_op jit(solution)/shard_map/pallas_call | solution.py:612
  2.0 0.1 collective-permute-start
  2.1 3.1 %collective-permute-start.1 = (f32[9,8,128]{2,1,0:T(8,128)S(1)}, f32[9,8,128]{2,1,0:T(8,128)S(1)}, u32[]{:S(2)}, u32[]{:S(2)}) collective-permute-start(f32[9,8,128]{2,1,0:T(8,128)S(1)} %get-tuple-element.32), channel_id=1, source_target_pairs={{1,2},{3,4},{5,6},{7,8},{9,10},{11,12},{13,14},{15,0},{2,1},{4,3},... | collective-permute-start | bytes 110600 | tf_op jit(solution)/shard_map/ppermute | solution.py:630
  5.2 1.1 %shard_map.56.own_sums = f32[8,128]{1,0:T(8,128)S(1)} custom-call(f32[11,2,64,128]{3,2,1,0:T(8,128)S(1)} %get-tuple-element.28.state, s32[2,64,128]{2,1,0:T(8,128)S(1)} %get-tuple-element.29.labels), custom_call_target="tpu_custom_call" | custom-call | tf_op jit(solution)/shard_map/pallas_call | solution.py:612
  6.3 0.0 collective-permute-done.even
  6.3 3.0 %collective-permute-done.1.odd = f32[9,8,128]{2,1,0:T(8,128)S(1)} collective-permute-done((f32[9,8,128]{2,1,0:T(8,128)S(1)}, f32[9,8,128]{2,1,0:T(8,128)S(1)}, u32[]{:S(2)}, u32[]{:S(2)}) %collective-permute-start.1) | collective-permute-done | bytes 36896 | tf_op jit(solution)/shard_map/ppermute | solution.py:630
  9.2 0.4 %shard_map.57 = (f32[2,12,8,128]{3,2,1,0:T(8,128)S(1)}, f32[18,8,128]{2,1,0:T(8,128)S(1)}, f32[18,8,128]{2,1,0:T(8,128)S(1)}, f32[8,128]{1,0:T(8,128)S(1)}, f32[2,2,8,128]{3,2,1,0:T(8,128)S(1)}) custom-call(f32[11,2,64,128]{3,2,1,0:T(8,128)S(1)} %get-tuple-element.28.state, s32[2,64,128]{2,1,0:T(8,128)S(1)} %get-tuple-element.29.labels, ...), custom_call_target="tpu_custom_call" | custom-call | tf_op jit(solution)/shard_map/pallas_call | solution.py:612
  9.6 1.3 %collective-permute-start.2 = (f32[18,8,128]{2,1,0:T(8,128)S(1)}, f32[18,8,128]{2,1,0:T(8,128)S(1)}, u32[]{:S(2)}, u32[]{:S(2)}) collective-permute-start(f32[18,8,128]{2,1,0:T(8,128)S(1)} %get-tuple-element.41), channel_id=1, source_target_pairs={{0,16},{32,48},{64,80},{96,112},{128,144},{160,176},{192,208},{224... | collective-permute-start | bytes 221192 | tf_op jit(solution)/shard_map/ppermute | solution.py:630
  10.9 6.1 %collective-permute-start.3 = (f32[18,8,128]{2,1,0:T(8,128)S(1)}, f32[18,8,128]{2,1,0:T(8,128)S(1)}, u32[]{:S(2)}, u32[]{:S(2)}) collective-permute-start(f32[18,8,128]{2,1,0:T(8,128)S(1)} %get-tuple-element.42), channel_id=1, source_target_pairs={{16,32},{48,64},{80,96},{112,128},{144,160},{176,192},{208,224},{2... | collective-permute-start | bytes 221192 | tf_op jit(solution)/shard_map/ppermute | solution.py:630
  17.0 1.3 %shard_map.59 = (s32[2,8,128]{2,1,0:T(8,128)S(1)}, f32[5,2,8,8,128]{4,3,2,1,0:T(8,128)S(1)}, f32[5,8,8,128]{3,2,1,0:T(8,128)S(1)}) custom-call(s32[2,64,128]{2,1,0:T(8,128)S(1)} %get-tuple-element.29.labels, f32[2,12,8,128]{3,2,1,0:T(8,128)S(1)} %get-tuple-element.33.domains), custom_call_target="tpu_custom_call" | custom-call | tf_op jit(solution)/shard_map/pallas_call | solution.py:612
  18.3 0.6 %shard_map.58 = (f32[9,6,2,8,8,128]{5,4,3,2,1,0:T(8,128)S(1)}, s32[9,2,8,8,128]{4,3,2,1,0:T(8,128)S(1)}) custom-call(f32[11,2,64,128]{3,2,1,0:T(8,128)S(1)} %get-tuple-element.28.state, s32[2,64,128]{2,1,0:T(8,128)S(1)} %get-tuple-element.29.labels, f32[2,12,8,128]{3,2,1,0:T(8,128)S(1)} %get-tuple-element.33.domains), custom_call_target="tpu_custom_call" | custom-call | tf_op jit(solution)/shard_map/pallas_call | solution.py:612
  18.9 0.0 collective-permute-done.2.even.old_even
  18.9 0.5 %collective-permute-done.3.odd.old_odd = f32[18,8,128]{2,1,0:T(8,128)S(1)} collective-permute-done((f32[18,8,128]{2,1,0:T(8,128)S(1)}, f32[18,8,128]{2,1,0:T(8,128)S(1)}, u32[]{:S(2)}, u32[]{:S(2)}) %collective-permute-start.3) | collective-permute-done | bytes 73760 | tf_op jit(solution)/shard_map/ppermute | solution.py:630
  19.4 0.0 copy-done.1
  19.4 0.0 copy-done
  19.4 1.3 %shard_map.60 = (f32[10,2,64,128]{3,2,1,0:T(8,128)S(1)}, f32[16,8,128]{2,1,0:T(8,128)S(1)}, f32[16,8,128]{2,1,0:T(8,128)S(1)}, f32[8,8,128]{2,1,0:T(8,128)S(1)},...) custom-call(f32[9,6,2,8,8,128]{5,4,3,2,1,0:T(8,128)S(1)} %get-tuple-element.34.moved, ...), custom_call_target="tpu_custom_call" | custom-call | tf_op jit(solution)/shard_map/pallas_call | solution.py:612
  20.7 0.1 collective-permute-start.4
  20.8 4.3 %collective-permute-start.5 = (f32[16,8,128]{2,1,0:T(8,128)S(1)}, f32[16,8,128]{2,1,0:T(8,128)S(1)}, u32[]{:S(2)}, u32[]{:S(2)}) collective-permute-start(f32[16,8,128]{2,1,0:T(8,128)S(1)} %get-tuple-element.50), channel_id=1, source_target_pairs={{16,32},{48,64},{80,96},{112,128},{144,160},{176,192},{208,224},{2... | collective-permute-start | bytes 196616 | tf_op jit(solution)/shard_map/ppermute | solution.py:630
  25.1 0.5 %shard_map.61 = (f32[9,6,2,8,8,128]{5,4,3,2,1,0:T(8,128)S(1)}, s32[9,2,8,8,128]{4,3,2,1,0:T(8,128)S(1)}) custom-call(f32[10,2,64,128]{3,2,1,0:T(8,128)S(1)} %get-tuple-element.43.state, s32[2,64,128]{2,1,0:T(8,128)S(1)} %get-tuple-element.29.labels, f32[8,8,128]{2,1,0:T(8,128)S(1)} %get-tuple-element.44.strip), custom_call_target="tpu_custom_call" | custom-call | tf_op jit(solution)/shard_map/pallas_call | solution.py:612
  25.6 0.0 collective-permute-done.4.even
  25.6 1.7 %collective-permute-done.5.odd = f32[16,8,128]{2,1,0:T(8,128)S(1)} collective-permute-done((f32[16,8,128]{2,1,0:T(8,128)S(1)}, f32[16,8,128]{2,1,0:T(8,128)S(1)}, u32[]{:S(2)}, u32[]{:S(2)}) %collective-permute-start.5) | collective-permute-done | bytes 65568 | tf_op jit(solution)/shard_map/ppermute | solution.py:630
  27.3 1.5 %shard_map.62 = f32[27,8,8,256]{3,2,1,0:T(8,128)} custom-call(f32[9,6,2,8,8,128]{5,4,3,2,1,0:T(8,128)S(1)} %get-tuple-element.45.moved, s32[9,2,8,8,128]{4,3,2,1,0:T(8,128)S(1)} %get-tuple-element.46.moved_labels, f32[8,128]{1,0:T(8,128)S(1)} %get-tuple-element.47.sums, f32[8,128]{1,0:T(8,128)S(1)} %get-tuple-element.48.counts, ...), custom_call_target="tpu_custom_call" | custom-call | tf_op jit(solution)/shard_map/pallas_call | solution.py:612
Async XLA Ops:
  0.0 19.4 %copy-start.1 = (f32[9,8,256]{2,1,0:T(8,128)S(1)}, f32[9,8,256]{2,1,0:T(8,128)}, u32[]{:S(2)}) copy-start(f32[9,8,256]{2,1,0:T(8,128)} %top.3) | copy-start | bytes 221188
  0.0 19.4 %copy-start = (f32[9,8,256]{2,1,0:T(8,128)S(1)}, f32[9,8,256]{2,1,0:T(8,128)}, u32[]{:S(2)}) copy-start(f32[9,8,256]{2,1,0:T(8,128)} %bottom.3) | copy-start | bytes 221188
  2.0 4.2 %collective-permute-start = (f32[9,8,128]{2,1,0:T(8,128)S(1)}, f32[9,8,128]{2,1,0:T(8,128)S(1)}, u32[]{:S(2)}, u32[]{:S(2)}) collective-permute-start(f32[9,8,128]{2,1,0:T(8,128)S(1)} %get-tuple-element.31), channel_id=1, source_target_pairs={{0,1},{2,3},{4,5},{6,7},{8,9},{10,11},{12,13},{14,15},{1,0},{3,2},... | collective-permute-start | bytes 110600 | tf_op jit(solution)/shard_map/ppermute | solution.py:630
  2.1 7.1 %collective-permute-start.1 = (f32[9,8,128]{2,1,0:T(8,128)S(1)}, f32[9,8,128]{2,1,0:T(8,128)S(1)}, u32[]{:S(2)}, u32[]{:S(2)}) collective-permute-start(f32[9,8,128]{2,1,0:T(8,128)S(1)} %get-tuple-element.32), channel_id=1, source_target_pairs={{1,2},{3,4},{5,6},{7,8},{9,10},{11,12},{13,14},{15,0},{2,1},{4,3},... | collective-permute-start | bytes 110600 | tf_op jit(solution)/shard_map/ppermute | solution.py:630
  9.6 9.2 %collective-permute-start.2 = (f32[18,8,128]{2,1,0:T(8,128)S(1)}, f32[18,8,128]{2,1,0:T(8,128)S(1)}, u32[]{:S(2)}, u32[]{:S(2)}) collective-permute-start(f32[18,8,128]{2,1,0:T(8,128)S(1)} %get-tuple-element.41), channel_id=1, source_target_pairs={{0,16},{32,48},{64,80},{96,112},{128,144},{160,176},{192,208},{224... | collective-permute-start | bytes 221192 | tf_op jit(solution)/shard_map/ppermute | solution.py:630
  10.9 8.5 %collective-permute-start.3 = (f32[18,8,128]{2,1,0:T(8,128)S(1)}, f32[18,8,128]{2,1,0:T(8,128)S(1)}, u32[]{:S(2)}, u32[]{:S(2)}) collective-permute-start(f32[18,8,128]{2,1,0:T(8,128)S(1)} %get-tuple-element.42), channel_id=1, source_target_pairs={{16,32},{48,64},{80,96},{112,128},{144,160},{176,192},{208,224},{2... | collective-permute-start | bytes 221192 | tf_op jit(solution)/shard_map/ppermute | solution.py:630
  20.7 4.9 %collective-permute-start.4 = (f32[16,8,128]{2,1,0:T(8,128)S(1)}, f32[16,8,128]{2,1,0:T(8,128)S(1)}, u32[]{:S(2)}, u32[]{:S(2)}) collective-permute-start(f32[16,8,128]{2,1,0:T(8,128)S(1)} %get-tuple-element.49), channel_id=1, source_target_pairs={{0,16},{32,48},{64,80},{96,112},{128,144},{160,176},{192,208},{224... | collective-permute-start | bytes 196616 | tf_op jit(solution)/shard_map/ppermute | solution.py:630
  20.8 6.5 %collective-permute-start.5 = (f32[16,8,128]{2,1,0:T(8,128)S(1)}, f32[16,8,128]{2,1,0:T(8,128)S(1)}, u32[]{:S(2)}, u32[]{:S(2)}) collective-permute-start(f32[16,8,128]{2,1,0:T(8,128)S(1)} %get-tuple-element.50), channel_id=1, source_target_pairs={{16,32},{48,64},{80,96},{112,128},{144,160},{176,192},{208,224},{2... | collective-permute-start | bytes 196616 | tf_op jit(solution)/shard_map/ppermute | solution.py:630
